TPU v7x, 32 devices: a whole 2x2x4 slice. The times are simulated.
32 devices in a mesh: seq: 16 (over z, y, x), head: 2 (over core).
Axes of the slice: x: 2, y: 2, z: 4, core: 2. Of those that a mesh axis runs over, the one named last changes fastest.
Arguments:
- queries: bfloat16 [8192, 32, 128], P('seq', 'head'), may hold values from -400 to 400
- key_vectors: bfloat16 [8192, 4, 128], P('seq', 'head'), may hold values from -400 to 400
- value_vectors: bfloat16 [8192, 4, 128], P('seq', 'head'), may hold values from -6 to 6
- query_map: bfloat16 [32, 128, 64], P('head'), may hold values from -0.5 to 0.5
- key_map: bfloat16 [32, 128, 64], P('head'), may hold values from -0.5 to 0.5
- window_param: float32 [32], P('head'), may hold values from 2 to 7
Outputs:
- attended: bfloat16 [32, 8192, 128], P(None, ('seq', 'head'))
All inputs are finite; a program needn't handle non-finite values.
Results may differ from a plain program's by a relative error of at most 0.0013.
The roundings to bfloat16 on the way count: a program that leaves them out, or rounds other values in their place, can miss the bound.
Values may be sent and summed in bfloat16 or wider, within the bound.
No kernel may reach another device: no remote copies, remote signals or barrier semaphores. Data moves between devices by JAX's collectives and lax.ppermute only.
A program may use at most 320 MiB of HBM per device.

v0:
```python
import functools

import jax
import jax.numpy as jnp
import numpy as np
from jax import lax
from jax.experimental import pallas as pl
from jax.experimental.pallas import tpu as pltpu
from jax.sharding import PartitionSpec as P

WINDOW = 64
PART = 4
BF = jnp.bfloat16
F32 = jnp.float32
LIMIT = 64 * 1024 * 1024
STEP = 2
SPLIT = (4, 12)


def mm(a, b, ca=1, cb=0):
    return lax.dot_general(a, b, (((ca,), (cb,)), ((), ())), preferred_element_type=F32)


def features_t(logits):
    top = jnp.max(logits, axis=0, keepdims=True)
    low = jnp.min(logits, axis=0, keepdims=True)
    up = jnp.exp(logits - top)
    down = jnp.exp(low - logits)
    up = up / jnp.sum(up, axis=0, keepdims=True)
    down = down / jnp.sum(down, axis=0, keepdims=True)
    return jnp.concatenate([up, down], axis=0).astype(BF)


def split_norm(state):
    width = state.shape[-1]
    norm = state[width : width + 1]
    high = norm.astype(BF).astype(F32)
    low = norm - high
    row = lax.broadcasted_iota(jnp.int32, (8, width), 0)
    tail = jnp.where(row == 0, high, jnp.where(row == 1, low, 0.0))
    return jnp.concatenate([state[:width], tail], axis=0).astype(BF)


def join_norm(piece):
    wide = piece.astype(F32)
    width = wide.shape[-1]
    norm = wide[width : width + 1] + wide[width + 1 : width + 2]
    row = lax.broadcasted_iota(jnp.int32, (8, width), 0)
    return jnp.concatenate([wide[:width], jnp.where(row == 0, norm, 0.0)], axis=0)


def values_with_one(values):
    row = lax.broadcasted_iota(jnp.int32, (8, values.shape[0]), 0)
    return jnp.concatenate([values.astype(F32).T, jnp.where(row == 0, 1.0, 0.0)], axis=0).astype(BF)


def state_kernel(per_part, group_size, idx_ref, k_ref, v_ref, w_ref, feat_ref, kg_ref, vg_ref, p0, p1, p2, p3, vt):
    m = pl.program_id(0)
    rows, groups, width = k_ref.shape

    @pl.when(m == 0)
    def _():
        wide_k = k_ref[...].astype(F32)
        wide_v = v_ref[...].astype(F32)
        for g in range(groups):
            kg_ref[g] = wide_k[:, g].astype(BF)
            values = wide_v[:, g].astype(BF)
            vg_ref[g] = values
            vt[g] = values_with_one(values)

    g = lax.bitwise_xor(idx_ref[0], m) * per_part // group_size
    logits = mm(w_ref[...].reshape(-1, width), kg_ref[g], 1, 1)
    states = []
    for e in range(per_part):
        f = logits.shape[0] // per_part
        feat = features_t(logits[e * f : (e + 1) * f]).T
        feat_ref[e] = feat
        states.append(split_norm(mm(vt[g], feat)))
    for k, out in enumerate((p0, p1, p2, p3)):

        @pl.when(m == k)
        def _(out=out):
            for e in range(per_part):
                out[e] = states[e]


def total_kernel(a, b, c, d, _, out):
    for e in range(out.shape[0]):
        out[e] = split_norm(join_norm(a[e]) + join_norm(b[e]) + join_norm(c[e]) + join_norm(d[e]))


def prefix_kernel(zs, idx_ref, *refs):
    own, outs = refs[:PART], refs[PART + zs + 1 :]
    me = idx_ref[0]
    for e in range(outs[0].shape[0]):
        base = jnp.zeros(own[0].shape[1:], F32)
        for k in range(zs):
            base = base + join_norm(refs[PART + k][e])
        terms = [join_norm(r[e]) for r in own]
        for m in range(PART):
            total = base
            for k in range(PART):
                earlier = lax.bitwise_xor(me, k) < lax.bitwise_xor(me, m)
                total = total + jnp.where(earlier, terms[k], 0.0)
            outs[m][e] = split_norm(total)


def near_kernel(
    group_size, first, idx_ref, share_ref, q_ref, k_ref, v_ref, hk_ref, hv_ref, feat_ref, wq_ref, wk_ref, *refs
):
    num_ref, den_ref, qf_ref, tail_ref, q_wide, kx, vt, hv, fx = refs[-9:]
    step = pl.program_id(0)
    count = feat_ref.shape[0]
    head = first + step * count
    rows, width = k_ref.shape[1:]
    scale = np.float32(np.log2(np.e) / np.sqrt(width))

    @pl.when((step == 0) | (head % group_size == 0))
    def _():
        q_wide[...] = q_ref[...].astype(F32).reshape(rows * group_size, width)
        kx[:WINDOW] = hk_ref[0]
        kx[WINDOW:] = k_ref[0]
        vt[...] = jnp.concatenate([hv_ref[0], v_ref[0]], axis=0).astype(F32).T.astype(BF)
        hv[...] = values_with_one(jnp.concatenate([hv_ref[0], hv_ref[0]], axis=0))

    present = idx_ref[1] > 0
    block = 128
    span = block + WINDOW
    key = lax.broadcasted_iota(jnp.int32, (span, block), 0)
    row = lax.broadcasted_iota(jnp.int32, (span, block), 1)
    band = (key > row) & (key <= row + WINDOW)
    key_sq = lax.broadcasted_iota(jnp.int32, (block, block), 0)
    row_sq = lax.broadcasted_iota(jnp.int32, (block, block), 1)
    causal = key_sq <= row_sq
    for e in range(count):
        halo_feat = features_t(mm(wk_ref[e], kx[:128], 1, 1)).T[:WINDOW]
        halo_feat = jnp.where(present, halo_feat.astype(F32), 0.0).astype(BF)
        fx[e, :WINDOW] = halo_feat
        fx[e, WINDOW:] = feat_ref[e]
        tail_ref[e] = mm(hv[:, :WINDOW], halo_feat)

        mix = jax.nn.sigmoid(jnp.full((1, block), share_ref[head + e], F32))
        rest = 1.0 - mix
        q = q_wide[pl.ds(head % group_size + e, rows, stride=group_size), :].astype(BF)
        qf = features_t(mm(wq_ref[e], q, 1, 1))
        qf_ref[e] = qf
        for r in range(rows // block):
            at = r * block
            mask = (band & ((key >= WINDOW) | present)) if r == 0 else band
            s = mm(kx[at : at + span], q[at : at + block], 1, 1)
            s = jnp.where(mask, s, -1e30)
            p = jnp.exp2((s - jnp.max(s, axis=0, keepdims=True)) * scale)
            wsum = jnp.sum(p, axis=0, keepdims=True)
            wnum = mm(vt[:, at : at + span], p.astype(BF))
            a = mm(fx[e, : at + block], qf[:, at : at + block])
            last = jnp.where(causal, a[at:], 0.0)
            a = last if r == 0 else jnp.concatenate([a[:at], last], axis=0)
            lsum = jnp.sum(a, axis=0, keepdims=True)
            lnum = mm(vt[:, : at + block], a.astype(BF))
            num_ref[e, :, at : at + block] = mix * wnum + rest * lnum
            den_ref[e, :, at : at + block] = mix * wsum + rest * lsum


def final_kernel(idx_ref, share_ref, num_ref, den_ref, qf_ref, tail_ref, state_ref, out_ref):
    count, width, rows = num_ref.shape
    for e in range(count):
        share = share_ref[pl.program_id(0) * count + e]
        rest = 1.0 - jax.nn.sigmoid(jnp.full((1, rows), share, F32))
        state = join_norm(state_ref[0, e]) - tail_ref[e]
        high = state.astype(BF)
        low = (state - high.astype(F32)).astype(BF)
        both = mm(high, qf_ref[e]) + mm(low, qf_ref[e])
        numer = num_ref[e] + rest * both[:width]
        denom = den_ref[e] + rest * both[width : width + 1]
        out_ref[e] = (numer * (1.0 / denom)).astype(BF).T


def per_device(queries, key_vectors, value_vectors, query_map, key_map, window_param):
    rows, heads, width = queries.shape
    groups = key_vectors.shape[1]
    group_size = heads // groups
    feat = query_map.shape[2]
    per_part = heads // PART
    tall = width + 8
    devices = lax.axis_size("seq")
    zs = devices // PART
    position = lax.axis_index("seq")
    core = lax.axis_index("head")
    me = position % PART
    idx = jnp.stack([me, position, core, 1 - core]).astype(jnp.int32)
    params = pltpu.CompilerParams(vmem_limit_bytes=LIMIT)
    smem = pl.BlockSpec(memory_space=pltpu.SMEM)
    anywhere = pl.BlockSpec(memory_space=pl.ANY)
    query_map = query_map.transpose(0, 2, 1)
    key_map = key_map.transpose(0, 2, 1)

    def xor(x, m):
        return lax.ppermute(x, "seq", [(i, i ^ m) for i in range(devices)])

    def shift(x, by):
        return lax.ppermute(x, "seq", [(i, i + by) for i in range(devices - by)])

    halo = shift(jnp.stack([key_vectors[rows - WINDOW :], value_vectors[rows - WINDOW :]]).transpose(0, 2, 1, 3), 1)

    def part_of(m, idx):
        return lax.bitwise_xor(idx[0], m)

    raw = pl.BlockSpec((rows, groups, width), lambda m, idx: (0, 0, 0))
    whole = pl.BlockSpec((groups, rows, width), lambda m, idx: (0, 0, 0))
    piece = pl.BlockSpec((per_part, tall, width), lambda m, idx: (0, 0, 0))
    piece_shape = jax.ShapeDtypeStruct((per_part, tall, width), BF)
    own_feat, keys, values, *pieces = pl.pallas_call(
        functools.partial(state_kernel, per_part, group_size),
        grid_spec=pltpu.PrefetchScalarGridSpec(
            num_scalar_prefetch=1,
            grid=(PART,),
            in_specs=[raw, raw, pl.BlockSpec((per_part, feat, width), lambda m, idx: (part_of(m, idx), 0, 0))],
            out_specs=[pl.BlockSpec((per_part, rows, width), lambda m, idx: (part_of(m, idx), 0, 0)), whole, whole]
            + [piece] * PART,
            scratch_shapes=[pltpu.VMEM((groups, tall, rows), BF)],
        ),
        out_shape=[jax.ShapeDtypeStruct((heads, rows, width), BF)]
        + [jax.ShapeDtypeStruct((groups, rows, width), BF)] * 2
        + [piece_shape] * PART,
        compiler_params=params,
        name="states",
    )(idx, key_vectors, value_vectors, key_map)

    def per_group(first, *dims):
        return pl.BlockSpec((1,) + dims, lambda h, *_: ((first + h * STEP) // group_size,) + (0,) * len(dims))

    near_shapes = [
        jax.ShapeDtypeStruct((heads, width, rows), F32),
        jax.ShapeDtypeStruct((heads, 1, rows), F32),
        jax.ShapeDtypeStruct((heads, 2 * feat, rows), BF),
        jax.ShapeDtypeStruct((heads, tall, width), F32),
    ]

    def near(first, count, before, after):
        def per_head(*dims):
            return pl.BlockSpec((STEP,) + dims, lambda h, *_: (first // STEP + h,) + (0,) * len(dims))

        return pl.pallas_call(
            functools.partial(near_kernel, group_size, first),
            grid_spec=pltpu.PrefetchScalarGridSpec(
                num_scalar_prefetch=1,
                grid=(count // STEP,),
                in_specs=[
                    smem,
                    pl.BlockSpec((rows, group_size, width), lambda h, *_: (0, (first + h * STEP) // group_size, 0)),
                    per_group(first, rows, width),
                    per_group(first, rows, width),
                    per_group(first, WINDOW, width),
                    per_group(first, WINDOW, width),
                    per_head(rows, width),
                    per_head(feat, width),
                    per_head(feat, width),
                ]
                + [anywhere] * (len(before) + len(after)),
                out_specs=[per_head(width, rows), per_head(1, rows), per_head(2 * feat, rows), per_head(tall, width)],
                scratch_shapes=[
                    pltpu.VMEM((rows * group_size, width), F32),
                    pltpu.VMEM((WINDOW + rows, width), BF),
                    pltpu.VMEM((width, WINDOW + rows), BF),
                    pltpu.VMEM((tall, 2 * WINDOW), BF),
                    pltpu.VMEM((STEP, WINDOW + rows, 2 * feat), BF),
                ],
            ),
            out_shape=near_shapes,
            input_output_aliases={10 + k: k for k in range(len(before))},
            compiler_params=params,
            cost_estimate=pl.CostEstimate(
                flops=count * 4 * 10**8, bytes_accessed=count * 10**6, transcendentals=count * 3 * 10**5
            ),
            name="near_%d" % first,
        )(idx, window_param, queries, keys, values, halo[0], halo[1], own_feat, query_map, key_map, *before, *after)

    pieces = [pieces[0]] + [xor(pieces[m], m) for m in range(1, PART)]
    held = near(0, SPLIT[0], [], [])
    vmem = pl.BlockSpec(memory_space=pltpu.VMEM)
    total = pl.pallas_call(
        total_kernel, in_specs=[vmem] * PART + [anywhere], out_specs=vmem, out_shape=piece_shape, name="totals"
    )(*pieces, held[1])
    if zs <= 4:
        earlier = [shift(total, PART * k) for k in range(1, zs)]
    else:
        columns = [[z * PART + k for z in range(zs)] for k in range(PART)]
        gathered = lax.all_gather(total, "seq", axis_index_groups=columns)
        below = jnp.arange(zs) < position // PART
        summed = jnp.sum(jnp.where(below[:, None, None, None], gathered.astype(F32), 0.0), axis=0)
        high = summed.astype(BF)
        earlier = [high, (summed - high.astype(F32)).astype(BF)]
    held = near(SPLIT[0], SPLIT[1] - SPLIT[0], held, [total])
    prefixes = pl.pallas_call(
        functools.partial(prefix_kernel, len(earlier)),
        in_specs=[smem] + [vmem] * (PART + len(earlier)) + [anywhere],
        out_specs=[vmem] * PART,
        out_shape=[piece_shape] * PART,
        name="prefixes",
    )(idx, *pieces, *earlier, held[1])
    prior = jnp.stack([prefixes[0]] + [xor(prefixes[m], m) for m in range(1, PART)])
    num, den, qf, tail = near(SPLIT[1], heads - SPLIT[1], held, [prefixes[0]])

    half = rows // 2

    def finish(name, which, out_heads, out_at):
        def half_of(dims):
            return pl.BlockSpec((per_part, dims, half), lambda h, idx: (h, 0, idx[which]))

        return pl.pallas_call(
            final_kernel,
            grid_spec=pltpu.PrefetchScalarGridSpec(
                num_scalar_prefetch=1,
                grid=(PART,),
                in_specs=[
                    smem,
                    half_of(width),
                    half_of(1),
                    half_of(2 * feat),
                    pl.BlockSpec((per_part, tall, width), lambda h, *_: (h, 0, 0)),
                    pl.BlockSpec((1, per_part, tall, width), lambda h, idx: (part_of(h, idx), 0, 0, 0)),
                ],
                out_specs=pl.BlockSpec((per_part, half, width), lambda h, idx: (h + out_at(idx), 0, 0)),
            ),
            out_shape=jax.ShapeDtypeStruct((out_heads, half, width), BF),
            compiler_params=params,
            cost_estimate=pl.CostEstimate(flops=10**9, bytes_accessed=5 * 10**6, transcendentals=0),
            name=name,
        )(idx, window_param, num, den, qf, tail, prior)

    theirs = finish("final_sent", 3, heads, lambda idx: 0)
    got = lax.ppermute(theirs, "head", [(0, 1), (1, 0)])
    out = finish("final_kept", 2, 2 * heads, lambda idx: PART * idx[2])
    return lax.dynamic_update_slice(out, got, (heads * (1 - core), 0, 0))


def solution(mesh):
    in_specs = (
        P("seq", "head", None),
        P("seq", "head", None),
        P("seq", "head", None),
        P("head", None, None),
        P("head", None, None),
        P("head"),
    )
    out_specs = P(None, ("seq", "head"), None)
    return jax.shard_map(
        per_device, mesh=mesh, in_specs=in_specs, out_specs=out_specs, check_vma=False
    )
```

profile of v0, /device:TPU:0, one launch (start us, length us, event | category | flops | bytes accessed | tf_op | source)
XLA Modules:
  0.0 83.6 jit_solution(3109545644085738133)
XLA Ops:
  0.0 0.8 slice.16
  0.8 0.8 slice.17
  1.6 0.6 maximum_bitcast_fusion
  2.2 5.5 %collective-permute-start = (bf16[2,2,64,128]{3,2,1,0:T(8,128)(2,1)}, bf16[2,2,64,128]{3,2,1,0:T(8,128)(2,1)}, u32[]{:S(2)}, u32[]{:S(2)}) collective-permute-start(bf16[2,2,64,128]{3,2,1,0:T(8,128)(2,1)} %maximum_bitcast_fusion), channel_id=1, source_target_pairs={{0,2},{2,4},{4,6},{6,8},{8,10},{10,12},{12,14},{14,16},{16,18},{18... | collective-permute-start | bytes 196616 | tf_op jit(solution)/shard_map/ppermute | solution.py:201
  7.7 0.6 pad_add_fusion.idx_ref
  8.3 8.0 %states.1 = (bf16[16,512,128]{2,1,0:T(8,128)(2,1)}, bf16[2,512,128]{2,1,0:T(8,128)(2,1)}, bf16[2,512,128]{2,1,0:T(8,128)(2,1)}, bf16[4,136,128]{2,1,0:T(8,128)(2...) custom-call(s32[4]{0:T(128)} %pad_add_fusion.idx_ref, ...), custom_call_target="tpu_custom_call" | custom-call | tf_op jit(solution)/shard_map/states/pallas_call | solution.py:212
  16.3 0.9 %collective-permute-start.1 = (bf16[4,136,128]{2,1,0:T(8,128)(2,1)}, bf16[4,136,128]{2,1,0:T(8,128)(2,1)}, u32[]{:S(2)}, u32[]{:S(2)}) collective-permute-start(bf16[4,136,128]{2,1,0:T(8,128)(2,1)} %get-tuple-element.36), channel_id=1, source_target_pairs={{0,2},{2,0},{4,6},{6,4},{8,10},{10,8},{12,14},{14,12},{16,18},{18,... | collective-permute-start | bytes 417800 | tf_op jit(solution)/shard_map/ppermute | solution.py:198
  17.2 1.5 %collective-permute-start.2 = (bf16[4,136,128]{2,1,0:T(8,128)(2,1)}, bf16[4,136,128]{2,1,0:T(8,128)(2,1)}, u32[]{:S(2)}, u32[]{:S(2)}) collective-permute-start(bf16[4,136,128]{2,1,0:T(8,128)(2,1)} %get-tuple-element.37), channel_id=1, source_target_pairs={{0,4},{2,6},{4,0},{6,2},{8,12},{10,14},{12,8},{14,10},{16,20},{18,... | collective-permute-start | bytes 417800 | tf_op jit(solution)/shard_map/ppermute | solution.py:198
  18.7 1.1 %collective-permute-start.3 = (bf16[4,136,128]{2,1,0:T(8,128)(2,1)}, bf16[4,136,128]{2,1,0:T(8,128)(2,1)}, u32[]{:S(2)}, u32[]{:S(2)}) collective-permute-start(bf16[4,136,128]{2,1,0:T(8,128)(2,1)} %get-tuple-element.38), channel_id=1, source_target_pairs={{0,6},{2,4},{4,2},{6,0},{8,14},{10,12},{12,10},{14,8},{16,22},{18,... | collective-permute-start | bytes 417800 | tf_op jit(solution)/shard_map/ppermute | solution.py:198
  19.8 0.0 collective-permute-done
  19.8 1.4 %slice_bitcast_fusion = (bf16[2,64,128]{2,1,0:T(8,128)(2,1)}, bf16[2,64,128]{2,1,0:T(8,128)(2,1)}) fusion(bf16[2,2,64,128]{3,2,1,0:T(8,128)(2,1)} %collective-permute-done), kind=kLoop, calls=%fused_computation.2 | loop fusion | bytes 131072 | tf_op jit(solution)/shard_map/squeeze | solution.py:276
  21.2 8.0 %near_0.1 = (f32[16,128,512]{2,1,0:T(8,128)}, f32[16,1,512]{2,1,0:T(1,128)}, bf16[16,128,512]{2,1,0:T(8,128)(2,1)}, f32[16,136,128]{2,1,0:T(8,128)}) custom-call(s32[4]{0:T(128)} %pad_add_fusion.idx_ref, f32[16]{0:T(128)} %share_ref.9, bf16[512,16,128]{2,1,0:T(8,128)(2,1)} %q_ref.5, bf16[2,512,128]{2,1,0:T(8,128)(2,1)} %get-tuple-element.28.k_ref, ...), custom_call_target="tpu_custom_call" | custom-call | flops 1600000000 | bytes 4000000 | tf_op jit(solution)/shard_map/near_0/pallas_call | solution.py:243
  29.3 0.0 collective-permute-done.1.b.refs_1_
  29.3 0.0 collective-permute-done.2.c.refs_2_
  29.3 0.0 collective-permute-done.3.d.refs_3_
  29.3 1.9 %totals.1.refs_4_ = bf16[4,136,128]{2,1,0:T(8,128)(2,1)} custom-call(bf16[4,136,128]{2,1,0:T(8,128)(2,1)} %get-tuple-element.35.a.refs_0_, bf16[4,136,128]{2,1,0:T(8,128)(2,1)} %collective-permute-done.1.b.refs_1_, bf16[4,136,128]{2,1,0:T(8,128)(2,1)} %collective-permute-done.2.c.refs_2_, bf16[4,136,128]{2,1,0:T(8,128)(2,1)} %collective-permute-done.3.d.refs_3_, ...), custom_call_target="tpu_custom_call" | custom-call | tf_op jit(solution)/shard_map/totals/pallas_call | solution.py:281
  31.1 5.6 %collective-permute-start.6 = (bf16[4,136,128]{2,1,0:T(8,128)(2,1)}, bf16[4,136,128]{2,1,0:T(8,128)(2,1)}, u32[]{:S(2)}, u32[]{:S(2)}) collective-permute-start(bf16[4,136,128]{2,1,0:T(8,128)(2,1)} %totals.1.refs_4_), channel_id=1, source_target_pairs={{0,24},{2,26},{4,28},{6,30},{1,25},{3,27},{5,29},{7,31}} | collective-permute-start | bytes 417800 | tf_op jit(solution)/shard_map/ppermute | solution.py:201
  36.7 1.9 %collective-permute-start.5 = (bf16[4,136,128]{2,1,0:T(8,128)(2,1)}, bf16[4,136,128]{2,1,0:T(8,128)(2,1)}, u32[]{:S(2)}, u32[]{:S(2)}) collective-permute-start(bf16[4,136,128]{2,1,0:T(8,128)(2,1)} %totals.1.refs_4_), channel_id=1, source_target_pairs={{0,16},{2,18},{4,20},{6,22},{8,24},{10,26},{12,28},{14,30},{1,17},... | collective-permute-start | bytes 417800 | tf_op jit(solution)/shard_map/ppermute | solution.py:201
  38.6 2.5 %collective-permute-start.4 = (bf16[4,136,128]{2,1,0:T(8,128)(2,1)}, bf16[4,136,128]{2,1,0:T(8,128)(2,1)}, u32[]{:S(2)}, u32[]{:S(2)}) collective-permute-start(bf16[4,136,128]{2,1,0:T(8,128)(2,1)} %totals.1.refs_4_), channel_id=1, source_target_pairs={{0,8},{2,10},{4,12},{6,14},{8,16},{10,18},{12,20},{14,22},{16,24},... | collective-permute-start | bytes 417800 | tf_op jit(solution)/shard_map/ppermute | solution.py:201
  41.1 13.3 %near_4.1 = (f32[16,128,512]{2,1,0:T(8,128)}, f32[16,1,512]{2,1,0:T(1,128)}, bf16[16,128,512]{2,1,0:T(8,128)(2,1)}, f32[16,136,128]{2,1,0:T(8,128)}) custom-call(s32[4]{0:T(128)} %pad_add_fusion.idx_ref, f32[16]{0:T(128)} %share_ref.9, bf16[512,16,128]{2,1,0:T(8,128)(2,1)} %q_ref.5, ...), custom_call_target="tpu_custom_call", output_to_operand_aliasing={{0}: (10, {}), {1}: (11, {}), {2}: (12, {}), {3}: (13, {})} | custom-call | flops 3200000000 | bytes 8000000 | tf_op jit(solution)/shard_map/near_4/pallas_call | solution.py:243
  54.4 0.0 collective-permute-done.6.refs_6_
  54.4 0.0 collective-permute-done.5.refs_5_
  54.4 0.0 collective-permute-done.4.refs_4_
  54.4 2.4 %prefixes.1 = (bf16[4,136,128]{2,1,0:T(8,128)(2,1)}, bf16[4,136,128]{2,1,0:T(8,128)(2,1)}, bf16[4,136,128]{2,1,0:T(8,128)(2,1)}, bf16[4,136,128]{2,1,0:T(8,128)(2,1)}) custom-call(s32[4]{0:T(128)} %pad_add_fusion.idx_ref, bf16[4,136,128]{2,1,0:T(8,128)(2,1)} %get-tuple-element.35.a.refs_0_, bf16[4,136,128]{2,1,0:T(8,128)(2,1)} %collective-permute-done.1.b.refs_1_, ...), custom_call_target="tpu_custom_call" | custom-call | tf_op jit(solution)/shard_map/prefixes/pallas_call | solution.py:294
  56.8 1.5 %collective-permute-start.7 = (bf16[4,136,128]{2,1,0:T(8,128)(2,1)}, bf16[4,136,128]{2,1,0:T(8,128)(2,1)}, u32[]{:S(2)}, u32[]{:S(2)}) collective-permute-start(bf16[4,136,128]{2,1,0:T(8,128)(2,1)} %get-tuple-element.48), channel_id=1, source_target_pairs={{0,2},{2,0},{4,6},{6,4},{8,10},{10,8},{12,14},{14,12},{16,18},{18,... | collective-permute-start | bytes 417800 | tf_op jit(solution)/shard_map/ppermute | solution.py:198
  58.3 0.1 collective-permute-start.8
  58.4 1.9 %collective-permute-start.9 = (bf16[4,136,128]{2,1,0:T(8,128)(2,1)}, bf16[4,136,128]{2,1,0:T(8,128)(2,1)}, u32[]{:S(2)}, u32[]{:S(2)}) collective-permute-start(bf16[4,136,128]{2,1,0:T(8,128)(2,1)} %get-tuple-element.50), channel_id=1, source_target_pairs={{0,6},{2,4},{4,2},{6,0},{8,14},{10,12},{12,10},{14,8},{16,22},{18,... | collective-permute-start | bytes 417800 | tf_op jit(solution)/shard_map/ppermute | solution.py:198
  60.3 8.0 %near_12.1 = (f32[16,128,512]{2,1,0:T(8,128)}, f32[16,1,512]{2,1,0:T(1,128)}, bf16[16,128,512]{2,1,0:T(8,128)(2,1)}, f32[16,136,128]{2,1,0:T(8,128)}) custom-call(s32[4]{0:T(128)} %pad_add_fusion.idx_ref, f32[16]{0:T(128)} %share_ref.9, bf16[512,16,128]{2,1,0:T(8,128)(2,1)} %q_ref.5, ...), custom_call_target="tpu_custom_call", output_to_operand_aliasing={{0}: (10, {}), {1}: (11, {}), {2}: (12, {}), {3}: (13, {})} | custom-call | flops 1600000000 | bytes 4000000 | tf_op jit(solution)/shard_map/near_12/pallas_call | solution.py:243
  68.4 0.0 collective-permute-done.7
  68.4 0.0 collective-permute-done.8
  68.4 0.0 collective-permute-done.9
  68.4 2.0 %pad_maximum_fusion.state_ref = bf16[4,4,136,128]{3,2,1,0:T(8,128)(2,1)} fusion(bf16[1,4,136,128]{3,2,1,0:T(8,128)(2,1)} %bitcast.14, bf16[1,4,136,128]{3,2,1,0:T(8,128)(2,1)} %bitcast.13, bf16[1,4,136,128]{3,2,1,0:T(8,128)(2,1)} %bitcast.12, bf16[1,4,136,128]{3,2,1,0:T(8,128)(2,1)} %bitcast.27), kind=kLoop, calls=%fused_computation | loop fusion | flops 835584 | bytes 1114112 | tf_op jit(solution)/shard_map/stack | solution.py:301
  70.4 5.5 %final_sent.1 = bf16[16,256,128]{2,1,0:T(8,128)(2,1)} custom-call(s32[4]{0:T(128)} %pad_add_fusion.idx_ref, f32[16]{0:T(128)} %share_ref.9, f32[16,128,512]{2,1,0:T(8,128)} %get-tuple-element.44.num_ref, f32[16,1,512]{2,1,0:T(1,128)} %get-tuple-element.45.den_ref, bf16[16,128,512]{2,1,0:T(8,128)(2,1)} %get-tuple-element.46.qf_ref, ...), custom_call_target="tpu_custom_call" | custom-call | flops 1000000000 | bytes 5000000 | tf_op jit(solution)/shard_map/final_sent/pallas_call | solution.py:310
  75.8 0.0 collective-permute-start.10
  75.9 5.5 %final_kept.1 = bf16[32,256,128]{2,1,0:T(8,128)(2,1)} custom-call(s32[4]{0:T(128)} %pad_add_fusion.idx_ref, f32[16]{0:T(128)} %share_ref.9, f32[16,128,512]{2,1,0:T(8,128)} %get-tuple-element.44.num_ref, f32[16,1,512]{2,1,0:T(1,128)} %get-tuple-element.45.den_ref, bf16[16,128,512]{2,1,0:T(8,128)(2,1)} %get-tuple-element.46.qf_ref, ...), custom_call_target="tpu_custom_call" | custom-call | flops 1000000000 | bytes 5000000 | tf_op jit(solution)/shard_map/final_kept/pallas_call | solution.py:310
  81.3 0.0 collective-permute-done.10
  81.3 2.3 %constant_dynamic-update-slice_fusion = bf16[32,256,128]{2,1,0:T(8,128)(2,1)} fusion(bf16[32,256,128]{2,1,0:T(8,128)(2,1)} %final_kept.1, bf16[16,256,128]{2,1,0:T(8,128)(2,1)} %collective-permute-done.10, s32[]{:T(128)S(6)} %select_n.11), kind=kLoop, calls=%fused_computation.7 | loop fusion | bytes 2097156 | tf_op jit(solution)/shard_map/dynamic_update_slice | solution.py:334
  (1 shorter events, 0.0 us)
Async XLA Ops:
  2.2 17.6 %collective-permute-start = (bf16[2,2,64,128]{3,2,1,0:T(8,128)(2,1)}, bf16[2,2,64,128]{3,2,1,0:T(8,128)(2,1)}, u32[]{:S(2)}, u32[]{:S(2)}) collective-permute-start(bf16[2,2,64,128]{3,2,1,0:T(8,128)(2,1)} %maximum_bitcast_fusion), channel_id=1, source_target_pairs={{0,2},{2,4},{4,6},{6,8},{8,10},{10,12},{12,14},{14,16},{16,18},{18... | collective-permute-start | bytes 196616 | tf_op jit(solution)/shard_map/ppermute | solution.py:201
  16.3 13.0 %collective-permute-start.1 = (bf16[4,136,128]{2,1,0:T(8,128)(2,1)}, bf16[4,136,128]{2,1,0:T(8,128)(2,1)}, u32[]{:S(2)}, u32[]{:S(2)}) collective-permute-start(bf16[4,136,128]{2,1,0:T(8,128)(2,1)} %get-tuple-element.36), channel_id=1, source_target_pairs={{0,2},{2,0},{4,6},{6,4},{8,10},{10,8},{12,14},{14,12},{16,18},{18,... | collective-permute-start | bytes 417800 | tf_op jit(solution)/shard_map/ppermute | solution.py:198
  17.2 12.1 %collective-permute-start.2 = (bf16[4,136,128]{2,1,0:T(8,128)(2,1)}, bf16[4,136,128]{2,1,0:T(8,128)(2,1)}, u32[]{:S(2)}, u32[]{:S(2)}) collective-permute-start(bf16[4,136,128]{2,1,0:T(8,128)(2,1)} %get-tuple-element.37), channel_id=1, source_target_pairs={{0,4},{2,6},{4,0},{6,2},{8,12},{10,14},{12,8},{14,10},{16,20},{18,... | collective-permute-start | bytes 417800 | tf_op jit(solution)/shard_map/ppermute | solution.py:198
  18.7 10.5 %collective-permute-start.3 = (bf16[4,136,128]{2,1,0:T(8,128)(2,1)}, bf16[4,136,128]{2,1,0:T(8,128)(2,1)}, u32[]{:S(2)}, u32[]{:S(2)}) collective-permute-start(bf16[4,136,128]{2,1,0:T(8,128)(2,1)} %get-tuple-element.38), channel_id=1, source_target_pairs={{0,6},{2,4},{4,2},{6,0},{8,14},{10,12},{12,10},{14,8},{16,22},{18,... | collective-permute-start | bytes 417800 | tf_op jit(solution)/shard_map/ppermute | solution.py:198
  31.1 23.3 %collective-permute-start.6 = (bf16[4,136,128]{2,1,0:T(8,128)(2,1)}, bf16[4,136,128]{2,1,0:T(8,128)(2,1)}, u32[]{:S(2)}, u32[]{:S(2)}) collective-permute-start(bf16[4,136,128]{2,1,0:T(8,128)(2,1)} %totals.1.refs_4_), channel_id=1, source_target_pairs={{0,24},{2,26},{4,28},{6,30},{1,25},{3,27},{5,29},{7,31}} | collective-permute-start | bytes 417800 | tf_op jit(solution)/shard_map/ppermute | solution.py:201
  36.7 17.7 %collective-permute-start.5 = (bf16[4,136,128]{2,1,0:T(8,128)(2,1)}, bf16[4,136,128]{2,1,0:T(8,128)(2,1)}, u32[]{:S(2)}, u32[]{:S(2)}) collective-permute-start(bf16[4,136,128]{2,1,0:T(8,128)(2,1)} %totals.1.refs_4_), channel_id=1, source_target_pairs={{0,16},{2,18},{4,20},{6,22},{8,24},{10,26},{12,28},{14,30},{1,17},... | collective-permute-start | bytes 417800 | tf_op jit(solution)/shard_map/ppermute | solution.py:201
  38.6 15.8 %collective-permute-start.4 = (bf16[4,136,128]{2,1,0:T(8,128)(2,1)}, bf16[4,136,128]{2,1,0:T(8,128)(2,1)}, u32[]{:S(2)}, u32[]{:S(2)}) collective-permute-start(bf16[4,136,128]{2,1,0:T(8,128)(2,1)} %totals.1.refs_4_), channel_id=1, source_target_pairs={{0,8},{2,10},{4,12},{6,14},{8,16},{10,18},{12,20},{14,22},{16,24},... | collective-permute-start | bytes 417800 | tf_op jit(solution)/shard_map/ppermute | solution.py:201
  56.8 11.5 %collective-permute-start.7 = (bf16[4,136,128]{2,1,0:T(8,128)(2,1)}, bf16[4,136,128]{2,1,0:T(8,128)(2,1)}, u32[]{:S(2)}, u32[]{:S(2)}) collective-permute-start(bf16[4,136,128]{2,1,0:T(8,128)(2,1)} %get-tuple-element.48), channel_id=1, source_target_pairs={{0,2},{2,0},{4,6},{6,4},{8,10},{10,8},{12,14},{14,12},{16,18},{18,... | collective-permute-start | bytes 417800 | tf_op jit(solution)/shard_map/ppermute | solution.py:198
  58.3 10.0 %collective-permute-start.8 = (bf16[4,136,128]{2,1,0:T(8,128)(2,1)}, bf16[4,136,128]{2,1,0:T(8,128)(2,1)}, u32[]{:S(2)}, u32[]{:S(2)}) collective-permute-start(bf16[4,136,128]{2,1,0:T(8,128)(2,1)} %get-tuple-element.49), channel_id=1, source_target_pairs={{0,4},{2,6},{4,0},{6,2},{8,12},{10,14},{12,8},{14,10},{16,20},{18,... | collective-permute-start | bytes 417800 | tf_op jit(solution)/shard_map/ppermute | solution.py:198
  58.4 9.9 %collective-permute-start.9 = (bf16[4,136,128]{2,1,0:T(8,128)(2,1)}, bf16[4,136,128]{2,1,0:T(8,128)(2,1)}, u32[]{:S(2)}, u32[]{:S(2)}) collective-permute-start(bf16[4,136,128]{2,1,0:T(8,128)(2,1)} %get-tuple-element.50), channel_id=1, source_target_pairs={{0,6},{2,4},{4,2},{6,0},{8,14},{10,12},{12,10},{14,8},{16,22},{18,... | collective-permute-start | bytes 417800 | tf_op jit(solution)/shard_map/ppermute | solution.py:198
  75.8 5.5 %collective-permute-start.10 = (bf16[16,256,128]{2,1,0:T(8,128)(2,1)}, bf16[16,256,128]{2,1,0:T(8,128)(2,1)}, u32[]{:S(2)}, u32[]{:S(2)}) collective-permute-start(bf16[16,256,128]{2,1,0:T(8,128)(2,1)} %final_sent.1), channel_id=1, source_target_pairs={{0,1},{1,0},{2,3},{3,2},{4,5},{5,4},{6,7},{7,6},{8,9},{9,8},{10,11... | collective-permute-start | bytes 3145736 | tf_op jit(solution)/shard_map/ppermute | solution.py:332
where the time goes:
time: 84.6 us; the launch traced here: 83.6 us
  Pallas kernels  52.5 us (62%)
  starting transfers between devices  22.4 us (26%)
  local copies, waits for them, and re-layouts  5.28 us (6%)
  other arithmetic  3.21 us (4%)
    pallas_call x3, Pallas kernels, near(): pl.pallas_call(functools.partial(near_kernel, group_size, first), grid_sp...  29.3 us
    ppermute x4, starting transfers between devices, shift(): return lax.ppermute(x, 'seq', [(i, i + by) for i in range(devices - by)])  15.4 us
    pallas_call x2, Pallas kernels, finish(): pl.pallas_call(final_kernel, grid_spec=pltpu.PrefetchScalarGridSpec(num_s...  10.9 us
    pallas_call x1, Pallas kernels, per_device(): pl.pallas_call(functools.partial(state_kernel, per_part, group_size), gri...  8.01 us
    ppermute x6, starting transfers between devices, xor(): return lax.ppermute(x, 'seq', [(i, i ^ m) for i in range(devices)])  7 us
    pallas_call x1, Pallas kernels, per_device(): pl.pallas_call(functools.partial(prefix_kernel, len(earlier)), in_specs=[...  2.4 us
    dynamic_update_slice x1, local copies, waits for them, and re-layouts, per_device(): return lax.dynamic_update_slice(out, got, (heads * (1 - core), 0, 0))  2.3 us
    another operation x1, other arithmetic, per_device(): jnp.stack([prefixes[0]] + [xor(prefixes[m], m) for m in range(1, PART)])  1.99 us
  transfers between devices with their start and end apart: 11, of which 0 were waited for; matrix products, arithmetic and copies ran while one was open for 2% of the time, Pallas kernels for 51%

commit v1 on v0

v1 whole, which is shorter than its diff:
```python
import functools

import jax
import jax.numpy as jnp
import numpy as np
from jax import lax
from jax.experimental import pallas as pl
from jax.experimental.pallas import tpu as pltpu
from jax.sharding import PartitionSpec as P

WINDOW = 64
PART = 4
BF = jnp.bfloat16
F32 = jnp.float32
LIMIT = 16 * 1024 * 1024
STEP = 2
SPLIT = (4, 12)


def mm(a, b, ca=1, cb=0):
    return lax.dot_general(a, b, (((ca,), (cb,)), ((), ())), preferred_element_type=F32)


def features_t(logits):
    top = jnp.max(logits, axis=0, keepdims=True)
    low = jnp.min(logits, axis=0, keepdims=True)
    up = jnp.exp(logits - top)
    down = jnp.exp(low - logits)
    up = up * (1.0 / jnp.sum(up, axis=0, keepdims=True))
    down = down * (1.0 / jnp.sum(down, axis=0, keepdims=True))
    return jnp.concatenate([up, down], axis=0).astype(BF)


def split_norm(state):
    width = state.shape[-1]
    norm = state[width : width + 1]
    high = norm.astype(BF).astype(F32)
    low = norm - high
    row = lax.broadcasted_iota(jnp.int32, (8, width), 0)
    tail = jnp.where(row == 0, high, jnp.where(row == 1, low, 0.0))
    return jnp.concatenate([state[:width], tail], axis=0).astype(BF)


def join_norm(piece):
    wide = piece.astype(F32)
    width = wide.shape[-1]
    norm = wide[width : width + 1] + wide[width + 1 : width + 2]
    row = lax.broadcasted_iota(jnp.int32, (8, width), 0)
    return jnp.concatenate([wide[:width], jnp.where(row == 0, norm, 0.0)], axis=0)


def values_with_one(values):
    row = lax.broadcasted_iota(jnp.int32, (8, values.shape[0]), 0)
    return jnp.concatenate([values.T, jnp.where(row == 0, 1.0, 0.0).astype(BF)], axis=0)


def state_kernel(per_part, group_size, idx_ref, k_ref, v_ref, w_ref, feat_ref, kg_ref, vg_ref, p0, p1, p2, p3, vt):
    rows, groups, width = k_ref.shape
    wide_k = k_ref[...].astype(F32)
    wide_v = v_ref[...].astype(F32)
    for g in range(groups):
        kg_ref[g] = wide_k[:, g].astype(BF)
        values = wide_v[:, g].astype(BF)
        vg_ref[g] = values
        vt[g] = values_with_one(values)
    for m, out in enumerate((p0, p1, p2, p3)):
        head = lax.bitwise_xor(idx_ref[0], m) * per_part
        g = head // group_size
        logits = mm(w_ref[pl.ds(head, per_part)].reshape(-1, width), kg_ref[g], 1, 1)
        for e in range(per_part):
            f = logits.shape[0] // per_part
            feat = features_t(logits[e * f : (e + 1) * f]).T
            feat_ref[head + e] = feat
            out[e] = split_norm(mm(vt[g], feat))


def total_kernel(a, b, c, d, _, out):
    for e in range(out.shape[0]):
        out[e] = split_norm(join_norm(a[e]) + join_norm(b[e]) + join_norm(c[e]) + join_norm(d[e]))


def prefix_kernel(zs, idx_ref, *refs):
    own, outs = refs[:PART], refs[PART + zs + 1 :]
    me = idx_ref[0]
    for e in range(outs[0].shape[0]):
        base = jnp.zeros(own[0].shape[1:], F32)
        for k in range(zs):
            base = base + join_norm(refs[PART + k][e])
        terms = [join_norm(r[e]) for r in own]
        for m in range(PART):
            total = base
            for k in range(PART):
                earlier = lax.bitwise_xor(me, k) < lax.bitwise_xor(me, m)
                total = total + jnp.where(earlier, terms[k], 0.0)
            outs[m][e] = split_norm(total)


def prepare_kernel(group_size, q_ref, k_ref, v_ref, halo_ref, q_wide, kx, vt):
    rows, _, width = q_ref.shape
    wide = halo_ref[...].astype(F32)
    for g in range(k_ref.shape[0]):
        q = q_ref[:, g * group_size : (g + 1) * group_size].astype(F32)
        q_wide[g] = q.reshape(rows * group_size, width)
        kx[g, :WINDOW] = wide[0, :, g].astype(BF)
        kx[g, WINDOW:] = k_ref[g]
        vt[g] = jnp.concatenate([wide[1, :, g].astype(BF), v_ref[g]], axis=0).T


def near_kernel(group_size, first, count, idx_ref, share_ref, q_wide, kx_ref, vt_ref, feat_ref, wq_ref, wk_ref, *refs):
    num_ref, den_ref, qf_ref, fx = refs[-4:]
    out = pl.program_id(0) * count
    head = first + out
    g = head // group_size
    rows, width = feat_ref.shape[1:]
    scale = np.float32(np.log2(np.e) / np.sqrt(width))
    kx, vt = kx_ref.at[g], vt_ref.at[g]
    present = idx_ref[1] > 0
    block = 128
    span = block + WINDOW
    key = lax.broadcasted_iota(jnp.int32, (span, 2 * block), 0)
    row = lax.broadcasted_iota(jnp.int32, (span, 2 * block), 1) % block
    band = (key > row) & (key <= row + WINDOW)
    wide = 2 * block
    causal = lax.broadcasted_iota(jnp.int32, (wide, wide), 0) <= lax.broadcasted_iota(jnp.int32, (wide, wide), 1)
    halo_logits = mm(wk_ref[pl.ds(head, count)].reshape(-1, width), kx[:128], 1, 1)
    feat = halo_logits.shape[0] // count
    for pair in range(0, count, 2):
        qs, mixes, rests, lnums, lsums = [], [], [], [], []
        for e in (pair, pair + 1):
            halo_feat = features_t(halo_logits[e * feat : (e + 1) * feat]).T[:WINDOW]
            fx[e, :WINDOW] = jnp.where(present, halo_feat.astype(F32), 0.0).astype(BF)
            fx[e, WINDOW:] = feat_ref[head + e]
            mixes.append(jax.nn.sigmoid(jnp.full((1, block), share_ref[head + e], F32)))
            rests.append(1.0 - mixes[-1])
            q = q_wide[g, pl.ds(head % group_size + e, rows, stride=group_size), :].astype(BF)
            qs.append(q)
            qf = features_t(mm(wq_ref[head + e], q, 1, 1))
            qf_ref[out + e] = qf
            for r in range(rows // wide):
                at = r * wide
                lnum = None
                lsum = None
                for kc in range(r + 1):
                    a = mm(fx[e, kc * wide : kc * wide + wide], qf[:, at : at + wide])
                    if kc == r:
                        last = jnp.where(causal, a, 0.0)
                    else:
                        last = a
                    if kc == 0:
                        halo = a[:WINDOW]
                        kept = halo.astype(BF).astype(F32)
                        body = last[WINDOW:]
                        part = jnp.sum(body, axis=0, keepdims=True)
                        if r == 0:
                            inside = causal[:WINDOW]
                            kept = jnp.where(inside, kept, 0.0)
                            part = part - jnp.sum(jnp.where(inside, 0.0, halo), axis=0, keepdims=True)
                        w = jnp.concatenate([(kept - halo).astype(BF), body.astype(BF)], axis=0)
                    else:
                        w = last.astype(BF)
                        part = jnp.sum(last, axis=0, keepdims=True)
                    t = mm(vt[:, kc * wide : kc * wide + wide], w)
                    lnum = t if lnum is None else lnum + t
                    lsum = part if lsum is None else lsum + part
                lnums.append(lnum)
                lsums.append(lsum)
        for r in range(rows // block):
            at = r * block
            mask = (band & ((key >= WINDOW) | present)) if r == 0 else band
            both = jnp.concatenate([q[at : at + block] for q in qs], axis=0)
            s = mm(kx[at : at + span], both, 1, 1)
            s = jnp.where(mask, s, -1e30)
            p = jnp.exp2((s - jnp.max(s, axis=0, keepdims=True)) * scale)
            wsum = jnp.sum(p, axis=0, keepdims=True)
            wnum = mm(vt[:, at : at + span], p.astype(BF))
            for k in range(2):
                mine = slice(k * block, (k + 1) * block)
                mixed = k * (rows // wide) + at // wide
                part = slice(at % wide, at % wide + block)
                num_ref[out + pair + k, :, at : at + block] = (
                    mixes[k] * wnum[:, mine] + rests[k] * lnums[mixed][:, part]
                )
                den_ref[out + pair + k, :, at : at + block] = (
                    mixes[k] * wsum[:, mine] + rests[k] * lsums[mixed][:, part]
                )


def finished(per_part, which, half, idx_ref, share_ref, held, pieces):
    at = pl.ds(pl.multiple_of(idx_ref[which] * half, 128), half)
    head = 0
    for num, den, qf in held:
        count, width, _ = num.shape
        for e in range(count):
            m = lax.bitwise_xor(idx_ref[0], head // per_part)
            state = pieces[0][head % per_part]
            for k in range(1, PART):
                state = jnp.where(m == k, pieces[k][head % per_part], state)
            rest = 1.0 - jax.nn.sigmoid(jnp.full((1, half), share_ref[head], F32))
            both = mm(state, qf[e, :, at])
            numer = num[e, :, at] + rest * both[:width]
            denom = den[e, :, at] + rest * (both[width : width + 1] + both[width + 1 : width + 2])
            yield head, (numer * (1.0 / denom)).astype(BF).T
            head += 1


def split_refs(refs):
    held = [refs[3 * k : 3 * k + 3] for k in range(3)]
    return held, refs[9 : 9 + PART]


def final_sent_kernel(per_part, half, idx_ref, share_ref, *refs):
    out_ref = refs[-1]
    for head, rows in finished(per_part, 3, half, idx_ref, share_ref, *split_refs(refs)):
        out_ref[head] = rows


def final_kept_kernel(per_part, half, idx_ref, share_ref, *refs):
    out_ref, kept, sems = refs[-3:]
    heads = kept.shape[0]
    copies = []
    for head, rows in finished(per_part, 2, half, idx_ref, share_ref, *split_refs(refs)):
        kept[head] = rows
        copies.append(pltpu.make_async_copy(kept.at[head], out_ref.at[heads * idx_ref[2] + head], sems.at[head]))
        copies[-1].start()
    for copy in copies:
        copy.wait()


def tails_kernel(k_ref, v_ref, out_ref, sems):
    rows = k_ref.shape[0]
    copies = [
        pltpu.make_async_copy(ref.at[pl.ds(rows - WINDOW, WINDOW)], out_ref.at[n], sems.at[n])
        for n, ref in enumerate((k_ref, v_ref))
    ]
    for copy in copies:
        copy.start()
    for copy in copies:
        copy.wait()


def place_kernel(idx_ref, got_ref, _, out_ref, sems):
    heads = got_ref.shape[0]
    copies = [
        pltpu.make_async_copy(got_ref.at[head], out_ref.at[heads * idx_ref[3] + head], sems.at[head])
        for head in range(heads)
    ]
    for copy in copies:
        copy.start()
    for copy in copies:
        copy.wait()


def per_device(queries, key_vectors, value_vectors, query_map, key_map, window_param):
    rows, heads, width = queries.shape
    groups = key_vectors.shape[1]
    group_size = heads // groups
    feat = query_map.shape[2]
    per_part = heads // PART
    tall = width + 8
    devices = lax.axis_size("seq")
    zs = devices // PART
    position = lax.axis_index("seq")
    core = lax.axis_index("head")
    me = position % PART
    idx = jnp.stack([me, position, core, 1 - core]).astype(jnp.int32)
    params = pltpu.CompilerParams(vmem_limit_bytes=LIMIT)
    smem = pl.BlockSpec(memory_space=pltpu.SMEM)
    anywhere = pl.BlockSpec(memory_space=pl.ANY)
    vmem = pl.BlockSpec(memory_space=pltpu.VMEM)
    query_map = query_map.transpose(0, 2, 1)
    key_map = key_map.transpose(0, 2, 1)

    def xor(x, m):
        return lax.ppermute(x, "seq", [(i, i ^ m) for i in range(devices)])

    def shift(x, by):
        return lax.ppermute(x, "seq", [(i, i + by) for i in range(devices - by)])

    tails = pl.pallas_call(
        tails_kernel,
        in_specs=[anywhere] * 2,
        out_specs=pl.BlockSpec(memory_space=pltpu.VMEM),
        out_shape=jax.ShapeDtypeStruct((2, WINDOW, groups, width), BF),
        scratch_shapes=[pltpu.SemaphoreType.DMA((2,))],
        compiler_params=params,
        name="tails",
    )(key_vectors, value_vectors)
    halo = shift(tails, 1)

    piece_shape = jax.ShapeDtypeStruct((per_part, tall, width), BF)
    grouped = jax.ShapeDtypeStruct((groups, rows, width), BF)
    own_feat, keys, values, *pieces = pl.pallas_call(
        functools.partial(state_kernel, per_part, group_size),
        in_specs=[smem] + [vmem] * 3,
        out_specs=[vmem] * (3 + PART),
        out_shape=[jax.ShapeDtypeStruct((heads, rows, width), BF), grouped, grouped] + [piece_shape] * PART,
        scratch_shapes=[pltpu.VMEM((groups, tall, rows), BF)],
        compiler_params=params,
        name="states",
    )(idx, key_vectors, value_vectors, key_map)
    q_wide, keys, values = pl.pallas_call(
        functools.partial(prepare_kernel, group_size),
        in_specs=[vmem] * 4,
        out_specs=[vmem] * 3,
        out_shape=[
            jax.ShapeDtypeStruct((groups, rows * group_size, width), F32),
            jax.ShapeDtypeStruct((groups, WINDOW + rows, width), BF),
            jax.ShapeDtypeStruct((groups, width, WINDOW + rows), BF),
        ],
        compiler_params=params,
        name="prepare",
    )(queries, keys, values, halo)

    def near(first, count, after):
        return pl.pallas_call(
            functools.partial(near_kernel, group_size, first, STEP),
            grid=(count // STEP,),
            in_specs=[smem, smem] + [vmem] * 6 + [anywhere] * len(after),
            out_specs=[vmem] * 3,
            scratch_shapes=[pltpu.VMEM((STEP, WINDOW + rows, 2 * feat), BF)],
            out_shape=[
                jax.ShapeDtypeStruct((count, width, rows), F32),
                jax.ShapeDtypeStruct((count, 1, rows), F32),
                jax.ShapeDtypeStruct((count, 2 * feat, rows), BF),
            ],
            compiler_params=params,
            cost_estimate=pl.CostEstimate(
                flops=count * 4 * 10**8, bytes_accessed=count * 10**6, transcendentals=count * 3 * 10**5
            ),
            name="near_%d" % first,
        )(idx, window_param, q_wide, keys, values, own_feat, query_map, key_map, *after)

    pieces = [pieces[0]] + [xor(pieces[m], m) for m in range(1, PART)]
    held = near(0, SPLIT[0], [])
    total = pl.pallas_call(
        total_kernel, in_specs=[vmem] * PART + [anywhere], out_specs=vmem, out_shape=piece_shape, compiler_params=params, name="totals"
    )(*pieces, held[1])
    held = list(held)
    if zs <= 4:
        earlier = [shift(total, PART * k) for k in range(1, zs)]
    else:
        columns = [[z * PART + k for z in range(zs)] for k in range(PART)]
        gathered = lax.all_gather(total, "seq", axis_index_groups=columns)
        below = jnp.arange(zs) < position // PART
        summed = jnp.sum(jnp.where(below[:, None, None, None], gathered.astype(F32), 0.0), axis=0)
        high = summed.astype(BF)
        earlier = [high, (summed - high.astype(F32)).astype(BF)]
    held += near(SPLIT[0], SPLIT[1] - SPLIT[0], [total])
    prefixes = pl.pallas_call(
        functools.partial(prefix_kernel, len(earlier)),
        in_specs=[smem] + [vmem] * (PART + len(earlier)) + [anywhere],
        out_specs=[vmem] * PART,
        out_shape=[piece_shape] * PART,
        compiler_params=params,
        name="prefixes",
    )(idx, *pieces, *earlier, held[4])
    prior = [prefixes[0]] + [xor(prefixes[m], m) for m in range(1, PART)]
    held += near(SPLIT[1], heads - SPLIT[1], [prefixes[0]])

    half = rows // 2
    theirs = pl.pallas_call(
        functools.partial(final_sent_kernel, per_part, half),
        in_specs=[smem, smem] + [vmem] * (9 + PART),
        out_specs=vmem,
        out_shape=jax.ShapeDtypeStruct((heads, half, width), BF),
        compiler_params=params,
        name="final_sent",
    )(idx, window_param, *held, *prior)
    got = lax.ppermute(theirs, "head", [(0, 1), (1, 0)])
    out = pl.pallas_call(
        functools.partial(final_kept_kernel, per_part, half),
        in_specs=[smem, smem] + [vmem] * (9 + PART) + [anywhere],
        out_specs=pl.BlockSpec(memory_space=pltpu.HBM),
        out_shape=jax.ShapeDtypeStruct((2 * heads, half, width), BF),
        scratch_shapes=[pltpu.VMEM((heads, half, width), BF), pltpu.SemaphoreType.DMA((heads,))],
        compiler_params=params,
        cost_estimate=pl.CostEstimate(flops=10**9, bytes_accessed=5 * 10**6, transcendentals=0),
        name="final_kept",
    )(idx, window_param, *held, *prior, theirs)
    return pl.pallas_call(
        place_kernel,
        in_specs=[smem, vmem, pl.BlockSpec(memory_space=pltpu.HBM)],
        out_specs=pl.BlockSpec(memory_space=pltpu.HBM),
        out_shape=jax.ShapeDtypeStruct(out.shape, BF),
        scratch_shapes=[pltpu.SemaphoreType.DMA((heads,))],
        input_output_aliases={2: 0},
        compiler_params=params,
        name="place",
    )(idx, got, out)


def solution(mesh):
    in_specs = (
        P("seq", "head", None),
        P("seq", "head", None),
        P("seq", "head", None),
        P("head", None, None),
        P("head", None, None),
        P("head"),
    )
    out_specs = P(None, ("seq", "head"), None)
    return jax.shard_map(
        per_device, mesh=mesh, in_specs=in_specs, out_specs=out_specs, check_vma=False
    )
```

time: 84.6 us -> 55.9 us (0.66)
  Pallas kernels: 52.5 us -> 26.6 us
  other arithmetic: 3.21 us -> 0.08 us
  local copies, waits for them, and re-layouts: 5.28 us -> 6.4 us
  starting transfers between devices: 22.4 us -> 21.3 us
  waiting for transfers between devices: 0.03 us -> 0.97 us
    pallas_call x6 -> x9, Pallas kernels: 48.3 us -> 25.6 us  [the longest x3 15.7 us: near(): pl.pallas_call(functools.partial(near_kernel, group_size, first, STEP), g...]
    unnamed x0 -> x18, local copies, waits for them, and re-layouts: none -> 6.4 us
    dynamic_update_slice x1 -> x0, local copies, waits for them, and re-layouts: 2.3 us -> none  [per_device(): return lax.dynamic_update_slice(out, got, (heads * (1 - core), 0, 0))]
    another operation x1 -> x0, other arithmetic: 1.99 us -> none  [per_device(): jnp.stack([prefixes[0]] + [xor(prefixes[m], m) for m in range(1, PART)])]
    pallas_call x1, Pallas kernels: 1.86 us -> 0.09 us  [per_device(): pl.pallas_call(total_kernel, in_specs=[vmem] * PART + [anywhere], out_spe...]
    slice x2 -> x0, local copies, waits for them, and re-layouts: 1.57 us -> none  [the longest x1 0.79 us: per_device(): value_vectors[rows - WINDOW:]]
    pallas_call x1, Pallas kernels: 2.4 us -> 0.9 us  [per_device(): pl.pallas_call(functools.partial(prefix_kernel, len(earlier)), in_specs=[...]
    squeeze x1 -> x0, local copies, waits for them, and re-layouts: 1.4 us -> none  [near(): halo[1]]
  transfers between devices with their start and end apart: 11 -> 11, of which waited for: 0 -> 2; matrix products, arithmetic and copies ran while one was open for 2% -> 0% of each run, Pallas kernels for 51% -> 40%
where the time goes in v1:
time: 55.9 us; the launch traced here: 55.5 us
  Pallas kernels  26.6 us (48%)
  starting transfers between devices  21.3 us (38%)
  local copies, waits for them, and re-layouts  6.4 us (11%)
  waiting for transfers between devices  0.97 us (2%)
    pallas_call x3, Pallas kernels, near(): pl.pallas_call(functools.partial(near_kernel, group_size, first, STEP), g...  15.7 us
    ppermute x4, starting transfers between devices, shift(): return lax.ppermute(x, 'seq', [(i, i + by) for i in range(devices - by)])  14.1 us
    ppermute x6, starting transfers between devices, xor(): return lax.ppermute(x, 'seq', [(i, i ^ m) for i in range(devices)])  7.1 us
    unnamed x18, local copies, waits for them, and re-layouts  6.4 us
    pallas_call x1, Pallas kernels, per_device(): pl.pallas_call(functools.partial(state_kernel, per_part, group_size), in_...  4.14 us
    pallas_call x1, Pallas kernels, per_device(): pl.pallas_call(functools.partial(final_kept_kernel, per_part, half), in_s...  2.19 us
    pallas_call x1, Pallas kernels, per_device(): pl.pallas_call(place_kernel, in_specs=[smem, vmem, pl.BlockSpec(memory_sp...  1.63 us
    pallas_call x1, Pallas kernels, per_device(): pl.pallas_call(functools.partial(final_sent_kernel, per_part, half), in_s...  1.41 us
  transfers between devices with their start and end apart: 11, of which 2 were waited for; matrix products, arithmetic and copies ran while one was open for 0% of the time, Pallas kernels for 40%

profile of v1, /device:TPU:0, one launch (start us, length us, event | category | flops | bytes accessed | tf_op | source)
XLA Modules:
  0.0 55.5 jit_solution(16915273774909210038)
XLA Ops:
  0.0 0.0 copy-start.1
  0.0 0.0 copy-start.4
  0.0 1.0 %copy-done.4 = bf16[512,2,128]{2,1,0:T(2,128)(2,1)S(1)} copy-done((bf16[512,2,128]{2,1,0:T(2,128)(2,1)S(1)}, bf16[512,2,128]{2,1,0:T(2,128)(2,1)}, u32[]{:S(2)}) %copy-start.4) | copy-done | bytes 262168
  1.0 0.0 copy-start.6
  1.0 0.9 %copy-done.6 = bf16[512,2,128]{2,1,0:T(2,128)(2,1)S(1)} copy-done((bf16[512,2,128]{2,1,0:T(2,128)(2,1)S(1)}, bf16[512,2,128]{2,1,0:T(2,128)(2,1)}, u32[]{:S(2)}) %copy-start.6) | copy-done | bytes 262168
  1.9 0.0 copy-start.3
  1.9 0.0 copy-start.8
  2.0 0.1 tails.1
  2.0 4.8 %collective-permute-start = (bf16[2,64,2,128]{3,2,1,0:T(2,128)(2,1)S(1)}, bf16[2,64,2,128]{3,2,1,0:T(2,128)(2,1)S(1)}, u32[]{:S(2)}, u32[]{:S(2)}) collective-permute-start(bf16[2,64,2,128]{3,2,1,0:T(2,128)(2,1)S(1)} %tails.1), channel_id=1, source_target_pairs={{0,2},{2,4},{4,6},{6,8},{8,10},{10,12},{12,14},{14,16},{16,18},{18... | collective-permute-start | bytes 196616 | tf_op jit(solution)/shard_map/ppermute | solution.py:277
  6.9 0.1 pad_add_fusion.idx_ref
  7.0 0.0 copy-start
  7.0 0.9 %copy-done = bf16[16,128,64]{1,2,0:T(8,128)(2,1)S(1)} copy-done((bf16[16,128,64]{1,2,0:T(8,128)(2,1)S(1)}, bf16[16,128,64]{1,2,0:T(8,128)(2,1)}, u32[]{:S(2)}) %copy-start) | copy-done | bytes 262168
  7.9 0.0 copy-start.5
  7.9 0.9 %copy-done.5 = bf16[512,2,128]{2,1,0:T(2,128)(2,1)S(1)} copy-done((bf16[512,2,128]{2,1,0:T(2,128)(2,1)S(1)}, bf16[512,2,128]{2,1,0:T(2,128)(2,1)}, u32[]{:S(2)}) %copy-start.5) | copy-done | bytes 262168
  8.9 0.0 copy-start.7
  8.9 0.9 %copy-done.7 = bf16[512,2,128]{2,1,0:T(2,128)(2,1)S(1)} copy-done((bf16[512,2,128]{2,1,0:T(2,128)(2,1)S(1)}, bf16[512,2,128]{2,1,0:T(2,128)(2,1)}, u32[]{:S(2)}) %copy-start.7) | copy-done | bytes 262168
  9.8 4.1 %states.1 = (bf16[16,512,128]{2,1,0:T(8,128)(2,1)S(1)}, bf16[2,512,128]{2,1,0:T(8,128)(2,1)S(1)}, bf16[2,512,128]{2,1,0:T(8,128)(2,1)S(1)}, bf16[4,136,128]{2,1,...) custom-call(s32[4]{0:T(128)S(1)} %pad_add_fusion.idx_ref, ...), custom_call_target="tpu_custom_call" | custom-call | tf_op jit(solution)/shard_map/states/pallas_call | solution.py:292
  14.0 1.6 %collective-permute-start.1 = (bf16[4,136,128]{2,1,0:T(8,128)(2,1)S(1)}, bf16[4,136,128]{2,1,0:T(8,128)(2,1)S(1)}, u32[]{:S(2)}, u32[]{:S(2)}) collective-permute-start(bf16[4,136,128]{2,1,0:T(8,128)(2,1)S(1)} %get-tuple-element.38), channel_id=1, source_target_pairs={{0,2},{2,0},{4,6},{6,4},{8,10},{10,8},{12,14},{14,12},{16,18},{18,... | collective-permute-start | bytes 417800 | tf_op jit(solution)/shard_map/ppermute | solution.py:274
  15.5 1.5 %collective-permute-start.2 = (bf16[4,136,128]{2,1,0:T(8,128)(2,1)S(1)}, bf16[4,136,128]{2,1,0:T(8,128)(2,1)S(1)}, u32[]{:S(2)}, u32[]{:S(2)}) collective-permute-start(bf16[4,136,128]{2,1,0:T(8,128)(2,1)S(1)} %get-tuple-element.39), channel_id=1, source_target_pairs={{0,4},{2,6},{4,0},{6,2},{8,12},{10,14},{12,8},{14,10},{16,20},{18,... | collective-permute-start | bytes 417800 | tf_op jit(solution)/shard_map/ppermute | solution.py:274
  17.1 0.5 collective-permute-start.3
  17.5 0.0 collective-permute-done.halo_ref
  17.5 0.0 copy-start.2
  17.5 1.6 %copy-done.2 = bf16[512,16,128]{2,1,0:T(8,128)(2,1)S(1)} copy-done((bf16[512,16,128]{2,1,0:T(8,128)(2,1)S(1)}, bf16[512,16,128]{2,1,0:T(8,128)(2,1)}, u32[]{:S(2)}) %copy-start.2) | copy-done | bytes 2097176
  19.1 0.4 prepare.1
  19.6 0.0 copy-done.1
  19.6 0.0 copy-done.3
  19.6 0.0 copy-done.8
  19.6 4.1 %near_0.1 = (f32[4,128,512]{2,1,0:T(8,128)S(1)}, f32[4,1,512]{2,1,0:T(1,128)S(1)}, bf16[4,128,512]{2,1,0:T(8,128)(2,1)S(1)}) custom-call(s32[4]{0:T(128)S(1)} %pad_add_fusion.idx_ref, f32[16]{0:T(128)S(1)} %copy-done.8, f32[2,4096,128]{2,1,0:T(8,128)S(1)} %get-tuple-element.30.q_wide, bf16[2,576,128]{2,1,0:T(8,128)(2,1)S(1)} %get-tuple-element.31.kx_ref, ...), custom_call_target="tpu_custom_call" | custom-call | flops 1600000000 | bytes 4000000 | tf_op jit(solution)/shard_map/near_0/pallas_call | solution.py:315
  23.7 0.0 collective-permute-done.1.b.refs_1_
  23.7 0.0 collective-permute-done.2.c.refs_2_
  23.7 0.0 collective-permute-done.3.d.refs_3_
  23.7 0.1 totals.1.refs_0_
  23.8 3.5 %collective-permute-start.4 = (bf16[4,136,128]{2,1,0:T(8,128)(2,1)S(1)}, bf16[4,136,128]{2,1,0:T(8,128)(2,1)S(1)}, u32[]{:S(2)}, u32[]{:S(2)}) collective-permute-start(bf16[4,136,128]{2,1,0:T(8,128)(2,1)S(1)} %totals.1.refs_0_), channel_id=1, source_target_pairs={{0,8},{2,10},{4,12},{6,14},{8,16},{10,18},{12,20},{14,22},{16,24},... | collective-permute-start | bytes 417800 | tf_op jit(solution)/shard_map/ppermute | solution.py:277
  27.3 4.5 %collective-permute-start.5 = (bf16[4,136,128]{2,1,0:T(8,128)(2,1)S(1)}, bf16[4,136,128]{2,1,0:T(8,128)(2,1)S(1)}, u32[]{:S(2)}, u32[]{:S(2)}) collective-permute-start(bf16[4,136,128]{2,1,0:T(8,128)(2,1)S(1)} %totals.1.refs_0_), channel_id=1, source_target_pairs={{0,16},{2,18},{4,20},{6,22},{8,24},{10,26},{12,28},{14,30},{1,17},... | collective-permute-start | bytes 417800 | tf_op jit(solution)/shard_map/ppermute | solution.py:277
  31.8 1.3 %collective-permute-start.6 = (bf16[4,136,128]{2,1,0:T(8,128)(2,1)S(1)}, bf16[4,136,128]{2,1,0:T(8,128)(2,1)S(1)}, u32[]{:S(2)}, u32[]{:S(2)}) collective-permute-start(bf16[4,136,128]{2,1,0:T(8,128)(2,1)S(1)} %totals.1.refs_0_), channel_id=1, source_target_pairs={{0,24},{2,26},{4,28},{6,30},{1,25},{3,27},{5,29},{7,31}} | collective-permute-start | bytes 417800 | tf_op jit(solution)/shard_map/ppermute | solution.py:277
  33.1 7.6 %near_4.1 = (f32[8,128,512]{2,1,0:T(8,128)S(1)}, f32[8,1,512]{2,1,0:T(1,128)S(1)}, bf16[8,128,512]{2,1,0:T(8,128)(2,1)S(1)}) custom-call(s32[4]{0:T(128)S(1)} %pad_add_fusion.idx_ref, f32[16]{0:T(128)S(1)} %copy-done.8, f32[2,4096,128]{2,1,0:T(8,128)S(1)} %get-tuple-element.30.q_wide, bf16[2,576,128]{2,1,0:T(8,128)(2,1)S(1)} %get-tuple-element.31.kx_ref, ...), custom_call_target="tpu_custom_call" | custom-call | flops 3200000000 | bytes 8000000 | tf_op jit(solution)/shard_map/near_4/pallas_call | solution.py:315
  40.7 0.0 collective-permute-done.4.refs_4_
  40.7 0.0 collective-permute-done.5.refs_5_
  40.7 0.0 collective-permute-done.6.refs_6_
  40.7 0.9 %prefixes.1 = (bf16[4,136,128]{2,1,0:T(8,128)(2,1)S(1)}, bf16[4,136,128]{2,1,0:T(8,128)(2,1)S(1)}, bf16[4,136,128]{2,1,0:T(8,128)(2,1)S(1)}, bf16[4,136,128]{2,1,0:T(8,128)(2,1)S(1)}) custom-call(s32[4]{0:T(128)S(1)} %pad_add_fusion.idx_ref, bf16[4,136,128]{2,1,0:T(8,128)(2,1)S(1)} %get-tuple-element.37.a.refs_0_, ...), custom_call_target="tpu_custom_call" | custom-call | tf_op jit(solution)/shard_map/prefixes/pallas_call | solution.py:349
  41.6 1.6 %collective-permute-start.7 = (bf16[4,136,128]{2,1,0:T(8,128)(2,1)S(1)}, bf16[4,136,128]{2,1,0:T(8,128)(2,1)S(1)}, u32[]{:S(2)}, u32[]{:S(2)}) collective-permute-start(bf16[4,136,128]{2,1,0:T(8,128)(2,1)S(1)} %get-tuple-element.48), channel_id=1, source_target_pairs={{0,2},{2,0},{4,6},{6,4},{8,10},{10,8},{12,14},{14,12},{16,18},{18,... | collective-permute-start | bytes 417800 | tf_op jit(solution)/shard_map/ppermute | solution.py:274
  43.2 0.2 collective-permute-start.8
  43.4 1.8 %collective-permute-start.9 = (bf16[4,136,128]{2,1,0:T(8,128)(2,1)S(1)}, bf16[4,136,128]{2,1,0:T(8,128)(2,1)S(1)}, u32[]{:S(2)}, u32[]{:S(2)}) collective-permute-start(bf16[4,136,128]{2,1,0:T(8,128)(2,1)S(1)} %get-tuple-element.50), channel_id=1, source_target_pairs={{0,6},{2,4},{4,2},{6,0},{8,14},{10,12},{12,10},{14,8},{16,22},{18,... | collective-permute-start | bytes 417800 | tf_op jit(solution)/shard_map/ppermute | solution.py:274
  45.2 4.0 %near_12.1 = (f32[4,128,512]{2,1,0:T(8,128)S(1)}, f32[4,1,512]{2,1,0:T(1,128)S(1)}, bf16[4,128,512]{2,1,0:T(8,128)(2,1)S(1)}) custom-call(s32[4]{0:T(128)S(1)} %pad_add_fusion.idx_ref, f32[16]{0:T(128)S(1)} %copy-done.8, f32[2,4096,128]{2,1,0:T(8,128)S(1)} %get-tuple-element.30.q_wide, bf16[2,576,128]{2,1,0:T(8,128)(2,1)S(1)} %get-tuple-element.31.kx_ref, ...), custom_call_target="tpu_custom_call" | custom-call | flops 1600000000 | bytes 4000000 | tf_op jit(solution)/shard_map/near_12/pallas_call | solution.py:315
  49.2 0.0 collective-permute-done.7.refs_10_
  49.3 0.5 collective-permute-done.8.refs_11_
  49.7 0.0 collective-permute-done.9.refs_12_
  49.7 1.4 %final_sent.1.refs_13_ = bf16[16,256,128]{2,1,0:T(8,128)(2,1)S(1)} custom-call(s32[4]{0:T(128)S(1)} %pad_add_fusion.idx_ref, f32[16]{0:T(128)S(1)} %copy-done.8, f32[4,128,512]{2,1,0:T(8,128)S(1)} %get-tuple-element.34.refs_0_, f32[4,1,512]{2,1,0:T(1,128)S(1)} %get-tuple-element.35._.refs_1_, bf16[4,128,512]{2,1,0:T(8,128)(2,1)S(1)} %get-tuple-element.36.refs_2_, ...), custom_call_target="tpu_custom_call" | custom-call | tf_op jit(solution)/shard_map/final_sent/pallas_call | solution.py:361
  51.2 0.1 collective-permute-start.10
  51.2 2.2 %final_kept.1._ = bf16[32,256,128]{2,1,0:T(8,128)(2,1)} custom-call(s32[4]{0:T(128)S(1)} %pad_add_fusion.idx_ref, f32[16]{0:T(128)S(1)} %copy-done.8, f32[4,128,512]{2,1,0:T(8,128)S(1)} %get-tuple-element.34.refs_0_, f32[4,1,512]{2,1,0:T(1,128)S(1)} %get-tuple-element.35._.refs_1_, bf16[4,128,512]{2,1,0:T(8,128)(2,1)S(1)} %get-tuple-element.36.refs_2_, ...), custom_call_target="tpu_custom_call" | custom-call | flops 1000000000 | bytes 5000000 | tf_op jit(solution)/shard_map/final_kept/pallas_call | solution.py:370
  53.4 0.5 collective-permute-done.10.got_ref
  53.9 1.6 %place.1 = bf16[32,256,128]{2,1,0:T(8,128)(2,1)} custom-call(s32[4]{0:T(128)S(1)} %pad_add_fusion.idx_ref, bf16[16,256,128]{2,1,0:T(8,128)(2,1)S(1)} %collective-permute-done.10.got_ref, bf16[32,256,128]{2,1,0:T(8,128)(2,1)} %final_kept.1._), custom_call_target="tpu_custom_call", output_to_operand_aliasing={{}: (2, {})} | custom-call | tf_op jit(solution)/shard_map/place/pallas_call | solution.py:380
Async XLA Ops:
  0.0 19.6 %copy-start.1 = (bf16[16,128,64]{1,2,0:T(8,128)(2,1)S(1)}, bf16[16,128,64]{1,2,0:T(8,128)(2,1)}, u32[]{:S(2)}) copy-start(bf16[16,128,64]{1,2,0:T(8,128)(2,1)} %param.10) | copy-start | bytes 786436
  0.0 1.0 %copy-start.4 = (bf16[512,2,128]{2,1,0:T(2,128)(2,1)S(1)}, bf16[512,2,128]{2,1,0:T(2,128)(2,1)}, u32[]{:S(2)}) copy-start(bf16[512,2,128]{2,1,0:T(2,128)(2,1)} %k_ref.3) | copy-start | bytes 786436
  1.0 0.9 %copy-start.6 = (bf16[512,2,128]{2,1,0:T(2,128)(2,1)S(1)}, bf16[512,2,128]{2,1,0:T(2,128)(2,1)}, u32[]{:S(2)}) copy-start(bf16[512,2,128]{2,1,0:T(2,128)(2,1)} %v_ref.3) | copy-start | bytes 786436
  1.9 17.7 %copy-start.3 = (bf16[16,128,64]{1,2,0:T(8,128)(2,1)S(1)}, bf16[16,128,64]{1,2,0:T(8,128)(2,1)}, u32[]{:S(2)}) copy-start(bf16[16,128,64]{1,2,0:T(8,128)(2,1)} %param.9) | copy-start | bytes 786436
  1.9 17.7 %copy-start.8 = (f32[16]{0:T(128)S(1)}, f32[16]{0:T(128)}, u32[]{:S(2)}) copy-start(f32[16]{0:T(128)} %share_ref.9) | copy-start | bytes 196
  2.0 15.5 %collective-permute-start = (bf16[2,64,2,128]{3,2,1,0:T(2,128)(2,1)S(1)}, bf16[2,64,2,128]{3,2,1,0:T(2,128)(2,1)S(1)}, u32[]{:S(2)}, u32[]{:S(2)}) collective-permute-start(bf16[2,64,2,128]{3,2,1,0:T(2,128)(2,1)S(1)} %tails.1), channel_id=1, source_target_pairs={{0,2},{2,4},{4,6},{6,8},{8,10},{10,12},{12,14},{14,16},{16,18},{18... | collective-permute-start | bytes 196616 | tf_op jit(solution)/shard_map/ppermute | solution.py:277
  7.0 1.0 %copy-start = (bf16[16,128,64]{1,2,0:T(8,128)(2,1)S(1)}, bf16[16,128,64]{1,2,0:T(8,128)(2,1)}, u32[]{:S(2)}) copy-start(bf16[16,128,64]{1,2,0:T(8,128)(2,1)} %param.10) | copy-start | bytes 786436
  7.9 0.9 %copy-start.5 = (bf16[512,2,128]{2,1,0:T(2,128)(2,1)S(1)}, bf16[512,2,128]{2,1,0:T(2,128)(2,1)}, u32[]{:S(2)}) copy-start(bf16[512,2,128]{2,1,0:T(2,128)(2,1)} %k_ref.3) | copy-start | bytes 786436
  8.9 0.9 %copy-start.7 = (bf16[512,2,128]{2,1,0:T(2,128)(2,1)S(1)}, bf16[512,2,128]{2,1,0:T(2,128)(2,1)}, u32[]{:S(2)}) copy-start(bf16[512,2,128]{2,1,0:T(2,128)(2,1)} %v_ref.3) | copy-start | bytes 786436
  14.0 9.7 %collective-permute-start.1 = (bf16[4,136,128]{2,1,0:T(8,128)(2,1)S(1)}, bf16[4,136,128]{2,1,0:T(8,128)(2,1)S(1)}, u32[]{:S(2)}, u32[]{:S(2)}) collective-permute-start(bf16[4,136,128]{2,1,0:T(8,128)(2,1)S(1)} %get-tuple-element.38), channel_id=1, source_target_pairs={{0,2},{2,0},{4,6},{6,4},{8,10},{10,8},{12,14},{14,12},{16,18},{18,... | collective-permute-start | bytes 417800 | tf_op jit(solution)/shard_map/ppermute | solution.py:274
  15.5 8.2 %collective-permute-start.2 = (bf16[4,136,128]{2,1,0:T(8,128)(2,1)S(1)}, bf16[4,136,128]{2,1,0:T(8,128)(2,1)S(1)}, u32[]{:S(2)}, u32[]{:S(2)}) collective-permute-start(bf16[4,136,128]{2,1,0:T(8,128)(2,1)S(1)} %get-tuple-element.39), channel_id=1, source_target_pairs={{0,4},{2,6},{4,0},{6,2},{8,12},{10,14},{12,8},{14,10},{16,20},{18,... | collective-permute-start | bytes 417800 | tf_op jit(solution)/shard_map/ppermute | solution.py:274
  17.1 6.6 %collective-permute-start.3 = (bf16[4,136,128]{2,1,0:T(8,128)(2,1)S(1)}, bf16[4,136,128]{2,1,0:T(8,128)(2,1)S(1)}, u32[]{:S(2)}, u32[]{:S(2)}) collective-permute-start(bf16[4,136,128]{2,1,0:T(8,128)(2,1)S(1)} %get-tuple-element.40), channel_id=1, source_target_pairs={{0,6},{2,4},{4,2},{6,0},{8,14},{10,12},{12,10},{14,8},{16,22},{18,... | collective-permute-start | bytes 417800 | tf_op jit(solution)/shard_map/ppermute | solution.py:274
  17.5 1.6 %copy-start.2 = (bf16[512,16,128]{2,1,0:T(8,128)(2,1)S(1)}, bf16[512,16,128]{2,1,0:T(8,128)(2,1)}, u32[]{:S(2)}) copy-start(bf16[512,16,128]{2,1,0:T(8,128)(2,1)} %q_ref.1) | copy-start | bytes 6291460
  23.8 16.9 %collective-permute-start.4 = (bf16[4,136,128]{2,1,0:T(8,128)(2,1)S(1)}, bf16[4,136,128]{2,1,0:T(8,128)(2,1)S(1)}, u32[]{:S(2)}, u32[]{:S(2)}) collective-permute-start(bf16[4,136,128]{2,1,0:T(8,128)(2,1)S(1)} %totals.1.refs_0_), channel_id=1, source_target_pairs={{0,8},{2,10},{4,12},{6,14},{8,16},{10,18},{12,20},{14,22},{16,24},... | collective-permute-start | bytes 417800 | tf_op jit(solution)/shard_map/ppermute | solution.py:277
  27.3 13.4 %collective-permute-start.5 = (bf16[4,136,128]{2,1,0:T(8,128)(2,1)S(1)}, bf16[4,136,128]{2,1,0:T(8,128)(2,1)S(1)}, u32[]{:S(2)}, u32[]{:S(2)}) collective-permute-start(bf16[4,136,128]{2,1,0:T(8,128)(2,1)S(1)} %totals.1.refs_0_), channel_id=1, source_target_pairs={{0,16},{2,18},{4,20},{6,22},{8,24},{10,26},{12,28},{14,30},{1,17},... | collective-permute-start | bytes 417800 | tf_op jit(solution)/shard_map/ppermute | solution.py:277
  31.8 8.9 %collective-permute-start.6 = (bf16[4,136,128]{2,1,0:T(8,128)(2,1)S(1)}, bf16[4,136,128]{2,1,0:T(8,128)(2,1)S(1)}, u32[]{:S(2)}, u32[]{:S(2)}) collective-permute-start(bf16[4,136,128]{2,1,0:T(8,128)(2,1)S(1)} %totals.1.refs_0_), channel_id=1, source_target_pairs={{0,24},{2,26},{4,28},{6,30},{1,25},{3,27},{5,29},{7,31}} | collective-permute-start | bytes 417800 | tf_op jit(solution)/shard_map/ppermute | solution.py:277
  41.6 7.6 %collective-permute-start.7 = (bf16[4,136,128]{2,1,0:T(8,128)(2,1)S(1)}, bf16[4,136,128]{2,1,0:T(8,128)(2,1)S(1)}, u32[]{:S(2)}, u32[]{:S(2)}) collective-permute-start(bf16[4,136,128]{2,1,0:T(8,128)(2,1)S(1)} %get-tuple-element.48), channel_id=1, source_target_pairs={{0,2},{2,0},{4,6},{6,4},{8,10},{10,8},{12,14},{14,12},{16,18},{18,... | collective-permute-start | bytes 417800 | tf_op jit(solution)/shard_map/ppermute | solution.py:274
  43.2 6.5 %collective-permute-start.8 = (bf16[4,136,128]{2,1,0:T(8,128)(2,1)S(1)}, bf16[4,136,128]{2,1,0:T(8,128)(2,1)S(1)}, u32[]{:S(2)}, u32[]{:S(2)}) collective-permute-start(bf16[4,136,128]{2,1,0:T(8,128)(2,1)S(1)} %get-tuple-element.49), channel_id=1, source_target_pairs={{0,4},{2,6},{4,0},{6,2},{8,12},{10,14},{12,8},{14,10},{16,20},{18,... | collective-permute-start | bytes 417800 | tf_op jit(solution)/shard_map/ppermute | solution.py:274
  43.4 6.3 %collective-permute-start.9 = (bf16[4,136,128]{2,1,0:T(8,128)(2,1)S(1)}, bf16[4,136,128]{2,1,0:T(8,128)(2,1)S(1)}, u32[]{:S(2)}, u32[]{:S(2)}) collective-permute-start(bf16[4,136,128]{2,1,0:T(8,128)(2,1)S(1)} %get-tuple-element.50), channel_id=1, source_target_pairs={{0,6},{2,4},{4,2},{6,0},{8,14},{10,12},{12,10},{14,8},{16,22},{18,... | collective-permute-start | bytes 417800 | tf_op jit(solution)/shard_map/ppermute | solution.py:274
  51.2 2.7 %collective-permute-start.10 = (bf16[16,256,128]{2,1,0:T(8,128)(2,1)S(1)}, bf16[16,256,128]{2,1,0:T(8,128)(2,1)S(1)}, u32[]{:S(2)}, u32[]{:S(2)}) collective-permute-start(bf16[16,256,128]{2,1,0:T(8,128)(2,1)S(1)} %final_sent.1.refs_13_), channel_id=1, source_target_pairs={{0,1},{1,0},{2,3},{3,2},{4,5},{5,4},{6,7},{7,6},{8,9},{9,8},{10,11... | collective-permute-start | bytes 3145736 | tf_op jit(solution)/shard_map/ppermute | solution.py:369

commit v2 on v1

--- a/solution.py
+++ b/solution.py
@@ -14,7 +14,7 @@
 F32 = jnp.float32
 LIMIT = 16 * 1024 * 1024
 STEP = 2
-SPLIT = (4, 12)
+SPLIT = 12
 
 
 def mm(a, b, ca=1, cb=0):
@@ -54,27 +54,49 @@
     return jnp.concatenate([values.T, jnp.where(row == 0, 1.0, 0.0).astype(BF)], axis=0)
 
 
-def state_kernel(per_part, group_size, idx_ref, k_ref, v_ref, w_ref, feat_ref, kg_ref, vg_ref, p0, p1, p2, p3, vt):
-    rows, groups, width = k_ref.shape
-    wide_k = k_ref[...].astype(F32)
-    wide_v = v_ref[...].astype(F32)
+def quarter_states(m, per_part, group_size, idx_ref, k_ref, vt_ref, w_ref, feat_ref, out):
+    head = lax.bitwise_xor(idx_ref[0], m) * per_part
+    g = head // group_size
+    logits = mm(w_ref[pl.ds(head, per_part)].reshape(-1, k_ref.shape[-1]), k_ref[g], 1, 1)
+    f = w_ref.shape[1]
+    for e in range(per_part):
+        feat = features_t(logits[e * f : (e + 1) * f]).T
+        feat_ref[head + e] = feat
+        out[e] = split_norm(mm(vt_ref[g], feat))
+
+
+def sent_states_kernel(
+    per_part, group_size, idx_ref, k_hbm, v_hbm, w_hbm, feat_ref, kg_ref, vg_ref, vt_ref, p1, p2, p3,
+    k_raw, v_raw, w_raw, sems,
+):
+    copies = [
+        pltpu.make_async_copy(source, target, sems.at[n])
+        for n, (source, target) in enumerate(((k_hbm, k_raw), (v_hbm, v_raw), (w_hbm, w_raw)))
+    ]
+    for copy in copies:
+        copy.start()
+    for copy in copies:
+        copy.wait()
+    rows, groups, _ = k_raw.shape
+    wide_k = k_raw[...].astype(F32)
+    wide_v = v_raw[...].astype(F32)
     for g in range(groups):
         kg_ref[g] = wide_k[:, g].astype(BF)
         values = wide_v[:, g].astype(BF)
         vg_ref[g] = values
-        vt[g] = values_with_one(values)
-    for m, out in enumerate((p0, p1, p2, p3)):
-        head = lax.bitwise_xor(idx_ref[0], m) * per_part
-        g = head // group_size
-        logits = mm(w_ref[pl.ds(head, per_part)].reshape(-1, width), kg_ref[g], 1, 1)
-        for e in range(per_part):
-            f = logits.shape[0] // per_part
-            feat = features_t(logits[e * f : (e + 1) * f]).T
-            feat_ref[head + e] = feat
-            out[e] = split_norm(mm(vt[g], feat))
-
-
-def total_kernel(a, b, c, d, _, out):
+        vt_ref[g] = values_with_one(values)
+    for m, out in enumerate((p1, p2, p3), 1):
+        quarter_states(m, per_part, group_size, idx_ref, kg_ref, vt_ref, w_raw, feat_ref, out)
+
+
+def own_states_kernel(per_part, group_size, idx_ref, k_ref, v_ref, vt_ref, w_ref, _, feat_ref, out, tail_ref):
+    rows = k_ref.shape[1]
+    tail_ref[0] = k_ref[:, rows - WINDOW :]
+    tail_ref[1] = v_ref[:, rows - WINDOW :]
+    quarter_states(0, per_part, group_size, idx_ref, k_ref, vt_ref, w_ref, feat_ref, out)
+
+
+def total_kernel(a, b, c, d, out):
     for e in range(out.shape[0]):
         out[e] = split_norm(join_norm(a[e]) + join_norm(b[e]) + join_norm(c[e]) + join_norm(d[e]))
 
@@ -95,15 +117,14 @@
             outs[m][e] = split_norm(total)
 
 
-def prepare_kernel(group_size, q_ref, k_ref, v_ref, halo_ref, q_wide, kx, vt):
+def prepare_kernel(group_size, q_ref, k_ref, v_ref, halo_ref, _, q_wide, kx, vt):
     rows, _, width = q_ref.shape
-    wide = halo_ref[...].astype(F32)
     for g in range(k_ref.shape[0]):
         q = q_ref[:, g * group_size : (g + 1) * group_size].astype(F32)
         q_wide[g] = q.reshape(rows * group_size, width)
-        kx[g, :WINDOW] = wide[0, :, g].astype(BF)
+        kx[g, :WINDOW] = halo_ref[0, g]
         kx[g, WINDOW:] = k_ref[g]
-        vt[g] = jnp.concatenate([wide[1, :, g].astype(BF), v_ref[g]], axis=0).T
+        vt[g] = jnp.concatenate([halo_ref[1, g], v_ref[g]], axis=0).T
 
 
 def near_kernel(group_size, first, count, idx_ref, share_ref, q_wide, kx_ref, vt_ref, feat_ref, wq_ref, wk_ref, *refs):
@@ -204,8 +225,8 @@
 
 
 def split_refs(refs):
-    held = [refs[3 * k : 3 * k + 3] for k in range(3)]
-    return held, refs[9 : 9 + PART]
+    held = [refs[3 * k : 3 * k + 3] for k in range(2)]
+    return held, refs[6 : 6 + PART]
 
 
 def final_sent_kernel(per_part, half, idx_ref, share_ref, *refs):
@@ -222,18 +243,6 @@
         kept[head] = rows
         copies.append(pltpu.make_async_copy(kept.at[head], out_ref.at[heads * idx_ref[2] + head], sems.at[head]))
         copies[-1].start()
-    for copy in copies:
-        copy.wait()
-
-
-def tails_kernel(k_ref, v_ref, out_ref, sems):
-    rows = k_ref.shape[0]
-    copies = [
-        pltpu.make_async_copy(ref.at[pl.ds(rows - WINDOW, WINDOW)], out_ref.at[n], sems.at[n])
-        for n, ref in enumerate((k_ref, v_ref))
-    ]
-    for copy in copies:
-        copy.start()
     for copy in copies:
         copy.wait()
 
@@ -276,31 +285,58 @@
     def shift(x, by):
         return lax.ppermute(x, "seq", [(i, i + by) for i in range(devices - by)])
 
-    tails = pl.pallas_call(
-        tails_kernel,
-        in_specs=[anywhere] * 2,
-        out_specs=pl.BlockSpec(memory_space=pltpu.VMEM),
-        out_shape=jax.ShapeDtypeStruct((2, WINDOW, groups, width), BF),
-        scratch_shapes=[pltpu.SemaphoreType.DMA((2,))],
-        compiler_params=params,
-        name="tails",
-    )(key_vectors, value_vectors)
-    halo = shift(tails, 1)
-
     piece_shape = jax.ShapeDtypeStruct((per_part, tall, width), BF)
     grouped = jax.ShapeDtypeStruct((groups, rows, width), BF)
-    own_feat, keys, values, *pieces = pl.pallas_call(
-        functools.partial(state_kernel, per_part, group_size),
-        in_specs=[smem] + [vmem] * 3,
-        out_specs=[vmem] * (3 + PART),
-        out_shape=[jax.ShapeDtypeStruct((heads, rows, width), BF), grouped, grouped] + [piece_shape] * PART,
-        scratch_shapes=[pltpu.VMEM((groups, tall, rows), BF)],
-        compiler_params=params,
-        name="states",
-    )(idx, key_vectors, value_vectors, key_map)
+    feat_shape = jax.ShapeDtypeStruct((heads, rows, width), BF)
+    hbm = pl.BlockSpec(memory_space=pltpu.HBM)
+    own_feat, keys, values, values_t, *pieces = pl.pallas_call(
+        functools.partial(sent_states_kernel, per_part, group_size),
+        in_specs=[smem] + [hbm] * 3,
+        out_specs=[vmem] * (4 + PART - 1),
+        out_shape=[
+            feat_shape,
+            grouped,
+            grouped,
+            jax.ShapeDtypeStruct((groups, tall, rows), BF),
+        ]
+        + [piece_shape] * (PART - 1),
+        scratch_shapes=[
+            pltpu.VMEM((rows, groups, width), BF),
+            pltpu.VMEM((rows, groups, width), BF),
+            pltpu.VMEM(key_map.shape, BF),
+            pltpu.SemaphoreType.DMA((3,)),
+        ],
+        compiler_params=params,
+        name="sent_states",
+    )(idx, *(pltpu.with_memory_space_constraint(x, pltpu.HBM) for x in (key_vectors, value_vectors, key_map)))
+    pieces = [xor(pieces[m - 1], m) for m in range(1, PART)]
+    own_feat, own_piece, tails = pl.pallas_call(
+        functools.partial(own_states_kernel, per_part, group_size),
+        in_specs=[smem] + [vmem] * 5,
+        out_specs=[vmem] * 3,
+        out_shape=[feat_shape, piece_shape, jax.ShapeDtypeStruct((2, groups, WINDOW, width), BF)],
+        input_output_aliases={5: 0},
+        compiler_params=params,
+        cost_estimate=pl.CostEstimate(flops=10**9, bytes_accessed=2 * 10**6, transcendentals=10**6),
+        name="own_states",
+    )(idx, keys, values, values_t, key_map, own_feat)
+    halo = shift(tails, 1)
+    pieces = [own_piece] + pieces
+    total = pl.pallas_call(
+        total_kernel, in_specs=[vmem] * PART, out_specs=vmem, out_shape=piece_shape, compiler_params=params, name="totals"
+    )(*pieces)
+    if zs <= 4:
+        earlier = [shift(total, PART * k) for k in range(1, zs)]
+    else:
+        columns = [[z * PART + k for z in range(zs)] for k in range(PART)]
+        gathered = lax.all_gather(total, "seq", axis_index_groups=columns)
+        below = jnp.arange(zs) < position // PART
+        summed = jnp.sum(jnp.where(below[:, None, None, None], gathered.astype(F32), 0.0), axis=0)
+        high = summed.astype(BF)
+        earlier = [high, (summed - high.astype(F32)).astype(BF)]
     q_wide, keys, values = pl.pallas_call(
         functools.partial(prepare_kernel, group_size),
-        in_specs=[vmem] * 4,
+        in_specs=[vmem] * 4 + [anywhere],
         out_specs=[vmem] * 3,
         out_shape=[
             jax.ShapeDtypeStruct((groups, rows * group_size, width), F32),
@@ -309,7 +345,7 @@
         ],
         compiler_params=params,
         name="prepare",
-    )(queries, keys, values, halo)
+    )(queries, keys, values, halo, total)
 
     def near(first, count, after):
         return pl.pallas_call(
@@ -330,22 +366,7 @@
             name="near_%d" % first,
         )(idx, window_param, q_wide, keys, values, own_feat, query_map, key_map, *after)
 
-    pieces = [pieces[0]] + [xor(pieces[m], m) for m in range(1, PART)]
-    held = near(0, SPLIT[0], [])
-    total = pl.pallas_call(
-        total_kernel, in_specs=[vmem] * PART + [anywhere], out_specs=vmem, out_shape=piece_shape, compiler_params=params, name="totals"
-    )(*pieces, held[1])
-    held = list(held)
-    if zs <= 4:
-        earlier = [shift(total, PART * k) for k in range(1, zs)]
-    else:
-        columns = [[z * PART + k for z in range(zs)] for k in range(PART)]
-        gathered = lax.all_gather(total, "seq", axis_index_groups=columns)
-        below = jnp.arange(zs) < position // PART
-        summed = jnp.sum(jnp.where(below[:, None, None, None], gathered.astype(F32), 0.0), axis=0)
-        high = summed.astype(BF)
-        earlier = [high, (summed - high.astype(F32)).astype(BF)]
-    held += near(SPLIT[0], SPLIT[1] - SPLIT[0], [total])
+    held = list(near(0, SPLIT, []))
     prefixes = pl.pallas_call(
         functools.partial(prefix_kernel, len(earlier)),
         in_specs=[smem] + [vmem] * (PART + len(earlier)) + [anywhere],
@@ -353,14 +374,14 @@
         out_shape=[piece_shape] * PART,
         compiler_params=params,
         name="prefixes",
-    )(idx, *pieces, *earlier, held[4])
+    )(idx, *pieces, *earlier, held[1])
     prior = [prefixes[0]] + [xor(prefixes[m], m) for m in range(1, PART)]
-    held += near(SPLIT[1], heads - SPLIT[1], [prefixes[0]])
+    held += near(SPLIT, heads - SPLIT, [prefixes[0]])
 
     half = rows // 2
     theirs = pl.pallas_call(
         functools.partial(final_sent_kernel, per_part, half),
-        in_specs=[smem, smem] + [vmem] * (9 + PART),
+        in_specs=[smem, smem] + [vmem] * (6 + PART),
         out_specs=vmem,
         out_shape=jax.ShapeDtypeStruct((heads, half, width), BF),
         compiler_params=params,
@@ -369,7 +390,7 @@
     got = lax.ppermute(theirs, "head", [(0, 1), (1, 0)])
     out = pl.pallas_call(
         functools.partial(final_kept_kernel, per_part, half),
-        in_specs=[smem, smem] + [vmem] * (9 + PART) + [anywhere],
+        in_specs=[smem, smem] + [vmem] * (6 + PART) + [anywhere],
         out_specs=pl.BlockSpec(memory_space=pltpu.HBM),
         out_shape=jax.ShapeDtypeStruct((2 * heads, half, width), BF),
         scratch_shapes=[pltpu.VMEM((heads, half, width), BF), pltpu.SemaphoreType.DMA((heads,))],

time: 55.9 us -> 51.6 us (0.923)
  local copies, waits for them, and re-layouts: 6.4 us -> 0.97 us
  Pallas kernels: 26.6 us -> 27.4 us
    unnamed x18 -> x8, local copies, waits for them, and re-layouts: 6.4 us -> 0.97 us
    pallas_call x3, Pallas kernels: 4.32 us -> 5.84 us  [the longest x1 4.44 us: per_device(): pl.pallas_call(functools.partial(sent_states_kernel, per_part, group_size...]
    ppermute x6, starting transfers between devices: 7.1 us -> 8.1 us  [xor(): return lax.ppermute(x, 'seq', [(i, i ^ m) for i in range(devices)])]
    ppermute x4, starting transfers between devices: 14.1 us -> 13.3 us  [shift(): return lax.ppermute(x, 'seq', [(i, i + by) for i in range(devices - by)])]
    pallas_call x3 -> x2, Pallas kernels: 15.7 us -> 15.1 us  [near(): pl.pallas_call(functools.partial(near_kernel, group_size, first, STEP), g...]
  transfers between devices with their start and end apart: 11 -> 11, of which waited for: 2 -> 3; matrix products, arithmetic and copies ran while one was open for 0% -> 0% of each run, Pallas kernels for 40% -> 37%
where the time goes in v2:
time: 51.6 us; the launch traced here: 51.3 us
  Pallas kernels  27.4 us (53%)
  starting transfers between devices  21.4 us (41%)
  waiting for transfers between devices  1.25 us (2%)
  local copies, waits for them, and re-layouts  0.97 us (2%)
    pallas_call x2, Pallas kernels, near(): pl.pallas_call(functools.partial(near_kernel, group_size, first, STEP), g...  15.1 us
    ppermute x4, starting transfers between devices, shift(): return lax.ppermute(x, 'seq', [(i, i + by) for i in range(devices - by)])  13.3 us
    ppermute x6, starting transfers between devices, xor(): return lax.ppermute(x, 'seq', [(i, i ^ m) for i in range(devices)])  8.1 us
    pallas_call x1, Pallas kernels, per_device(): pl.pallas_call(functools.partial(sent_states_kernel, per_part, group_size...  4.44 us
    pallas_call x1, Pallas kernels, per_device(): pl.pallas_call(functools.partial(final_kept_kernel, per_part, half), in_s...  2.15 us
    pallas_call x1, Pallas kernels, per_device(): pl.pallas_call(place_kernel, in_specs=[smem, vmem, pl.BlockSpec(memory_sp...  1.63 us
    pallas_call x1, Pallas kernels, per_device(): pl.pallas_call(functools.partial(final_sent_kernel, per_part, half), in_s...  1.42 us
    pallas_call x1, Pallas kernels, per_device(): pl.pallas_call(functools.partial(own_states_kernel, per_part, group_size)...  1.3 us
  transfers between devices with their start and end apart: 11, of which 3 were waited for; matrix products, arithmetic and copies ran while one was open for 0% of the time, Pallas kernels for 37%

profile of v2, /device:TPU:0, one launch (start us, length us, event | category | flops | bytes accessed | tf_op | source)
XLA Modules:
  0.0 51.3 jit_solution(13411731136298764678)
XLA Ops:
  0.0 0.1 pad_add_fusion.idx_ref
  0.1 4.4 %sent_states.1 = (bf16[16,512,128]{2,1,0:T(8,128)(2,1)S(1)}, bf16[2,512,128]{2,1,0:T(8,128)(2,1)S(1)}, bf16[2,512,128]{2,1,0:T(8,128)(2,1)S(1)}, bf16[2,136,512]...) custom-call(s32[4]{0:T(128)S(1)} %pad_add_fusion.idx_ref, ...), custom_call_target="tpu_custom_call" | custom-call | tf_op jit(solution)/shard_map/sent_states/pallas_call | solution.py:292
  4.5 3.0 %collective-permute-start.1 = (bf16[4,136,128]{2,1,0:T(8,128)(2,1)S(1)}, bf16[4,136,128]{2,1,0:T(8,128)(2,1)S(1)}, u32[]{:S(2)}, u32[]{:S(2)}) collective-permute-start(bf16[4,136,128]{2,1,0:T(8,128)(2,1)S(1)} %get-tuple-element.34), channel_id=1, source_target_pairs={{0,2},{2,0},{4,6},{6,4},{8,10},{10,8},{12,14},{14,12},{16,18},{18,... | collective-permute-start | bytes 417800 | tf_op jit(solution)/shard_map/ppermute | solution.py:283
  7.5 1.5 %collective-permute-start.2 = (bf16[4,136,128]{2,1,0:T(8,128)(2,1)S(1)}, bf16[4,136,128]{2,1,0:T(8,128)(2,1)S(1)}, u32[]{:S(2)}, u32[]{:S(2)}) collective-permute-start(bf16[4,136,128]{2,1,0:T(8,128)(2,1)S(1)} %get-tuple-element.35), channel_id=1, source_target_pairs={{0,4},{2,6},{4,0},{6,2},{8,12},{10,14},{12,8},{14,10},{16,20},{18,... | collective-permute-start | bytes 417800 | tf_op jit(solution)/shard_map/ppermute | solution.py:283
  9.0 0.0 collective-permute-start.3
  9.1 0.0 copy-start.1
  9.1 0.9 %copy-done.1 = bf16[16,128,64]{1,2,0:T(8,128)(2,1)S(1)} copy-done((bf16[16,128,64]{1,2,0:T(8,128)(2,1)S(1)}, bf16[16,128,64]{1,2,0:T(8,128)(2,1)}, u32[]{:S(2)}) %copy-start.1) | copy-done | bytes 262168
  10.0 0.0 copy-start
  10.0 1.3 %own_states.1 = (bf16[16,512,128]{2,1,0:T(8,128)(2,1)S(1)}, bf16[4,136,128]{2,1,0:T(8,128)(2,1)S(1)}, bf16[2,2,64,128]{3,2,1,0:T(8,128)(2,1)S(1)}) custom-call(s32[4]{0:T(128)S(1)} %pad_add_fusion.idx_ref, bf16[2,512,128]{2,1,0:T(8,128)(2,1)S(1)} %get-tuple-element.28.k_ref, ...), custom_call_target="tpu_custom_call", output_to_operand_aliasing={{0}: (5, {})} | custom-call | flops 1000000000 | bytes 2000000 | tf_op jit(solution)/shard_map/own_states/pallas_call | solution.py:313
  11.3 0.0 copy-start.2
  11.3 0.0 copy-start.3
  11.4 4.0 %collective-permute-start = (bf16[2,2,64,128]{3,2,1,0:T(8,128)(2,1)S(1)}, bf16[2,2,64,128]{3,2,1,0:T(8,128)(2,1)S(1)}, u32[]{:S(2)}, u32[]{:S(2)}) collective-permute-start(bf16[2,2,64,128]{3,2,1,0:T(8,128)(2,1)S(1)} %get-tuple-element.32), channel_id=1, source_target_pairs={{0,2},{2,4},{4,6},{6,8},{8,10},{10,12},{12,14},{14,16},{16,18},{18... | collective-permute-start | bytes 196616 | tf_op jit(solution)/shard_map/ppermute | solution.py:286
  15.4 0.0 collective-permute-done.1.b.refs_1_
  15.4 0.3 collective-permute-done.2.c.refs_2_
  15.7 0.0 collective-permute-done.3.d.refs_3_
  15.7 0.1 totals.1._
  15.7 3.5 %collective-permute-start.4 = (bf16[4,136,128]{2,1,0:T(8,128)(2,1)S(1)}, bf16[4,136,128]{2,1,0:T(8,128)(2,1)S(1)}, u32[]{:S(2)}, u32[]{:S(2)}) collective-permute-start(bf16[4,136,128]{2,1,0:T(8,128)(2,1)S(1)} %totals.1._), channel_id=1, source_target_pairs={{0,8},{2,10},{4,12},{6,14},{8,16},{10,18},{12,20},{14,22},{16,24},... | collective-permute-start | bytes 417800 | tf_op jit(solution)/shard_map/ppermute | solution.py:286
  19.2 4.5 %collective-permute-start.5 = (bf16[4,136,128]{2,1,0:T(8,128)(2,1)S(1)}, bf16[4,136,128]{2,1,0:T(8,128)(2,1)S(1)}, u32[]{:S(2)}, u32[]{:S(2)}) collective-permute-start(bf16[4,136,128]{2,1,0:T(8,128)(2,1)S(1)} %totals.1._), channel_id=1, source_target_pairs={{0,16},{2,18},{4,20},{6,22},{8,24},{10,26},{12,28},{14,30},{1,17},... | collective-permute-start | bytes 417800 | tf_op jit(solution)/shard_map/ppermute | solution.py:286
  23.7 1.3 %collective-permute-start.6 = (bf16[4,136,128]{2,1,0:T(8,128)(2,1)S(1)}, bf16[4,136,128]{2,1,0:T(8,128)(2,1)S(1)}, u32[]{:S(2)}, u32[]{:S(2)}) collective-permute-start(bf16[4,136,128]{2,1,0:T(8,128)(2,1)S(1)} %totals.1._), channel_id=1, source_target_pairs={{0,24},{2,26},{4,28},{6,30},{1,25},{3,27},{5,29},{7,31}} | collective-permute-start | bytes 417800 | tf_op jit(solution)/shard_map/ppermute | solution.py:286
  25.1 0.0 collective-permute-done.halo_ref
  25.1 0.0 copy-done
  25.1 0.4 prepare.1
  25.5 0.0 copy-done.2
  25.5 0.0 copy-done.3
  25.5 11.1 %near_0.1 = (f32[12,128,512]{2,1,0:T(8,128)S(1)}, f32[12,1,512]{2,1,0:T(1,128)S(1)}, bf16[12,128,512]{2,1,0:T(8,128)(2,1)S(1)}) custom-call(s32[4]{0:T(128)S(1)} %pad_add_fusion.idx_ref, f32[16]{0:T(128)S(1)} %copy-done.3, f32[2,4096,128]{2,1,0:T(8,128)S(1)} %get-tuple-element.37.q_wide, bf16[2,576,128]{2,1,0:T(8,128)(2,1)S(1)} %get-tuple-element.38.kx_ref, ...), custom_call_target="tpu_custom_call" | custom-call | flops 4800000000 | bytes 12000000 | tf_op jit(solution)/shard_map/near_0/pallas_call | solution.py:351
  36.5 0.0 collective-permute-done.4.refs_4_
  36.6 0.0 collective-permute-done.5.refs_5_
  36.6 0.0 collective-permute-done.6.refs_6_
  36.6 0.9 %prefixes.1 = (bf16[4,136,128]{2,1,0:T(8,128)(2,1)S(1)}, bf16[4,136,128]{2,1,0:T(8,128)(2,1)S(1)}, bf16[4,136,128]{2,1,0:T(8,128)(2,1)S(1)}, bf16[4,136,128]{2,1,0:T(8,128)(2,1)S(1)}) custom-call(s32[4]{0:T(128)S(1)} %pad_add_fusion.idx_ref, bf16[4,136,128]{2,1,0:T(8,128)(2,1)S(1)} %get-tuple-element.33.a.refs_0_, ...), custom_call_target="tpu_custom_call" | custom-call | tf_op jit(solution)/shard_map/prefixes/pallas_call | solution.py:370
  37.5 1.3 %collective-permute-start.7 = (bf16[4,136,128]{2,1,0:T(8,128)(2,1)S(1)}, bf16[4,136,128]{2,1,0:T(8,128)(2,1)S(1)}, u32[]{:S(2)}, u32[]{:S(2)}) collective-permute-start(bf16[4,136,128]{2,1,0:T(8,128)(2,1)S(1)} %get-tuple-element.48), channel_id=1, source_target_pairs={{0,2},{2,0},{4,6},{6,4},{8,10},{10,8},{12,14},{14,12},{16,18},{18,... | collective-permute-start | bytes 417800 | tf_op jit(solution)/shard_map/ppermute | solution.py:283
  38.8 0.8 %collective-permute-start.8 = (bf16[4,136,128]{2,1,0:T(8,128)(2,1)S(1)}, bf16[4,136,128]{2,1,0:T(8,128)(2,1)S(1)}, u32[]{:S(2)}, u32[]{:S(2)}) collective-permute-start(bf16[4,136,128]{2,1,0:T(8,128)(2,1)S(1)} %get-tuple-element.49), channel_id=1, source_target_pairs={{0,4},{2,6},{4,0},{6,2},{8,12},{10,14},{12,8},{14,10},{16,20},{18,... | collective-permute-start | bytes 417800 | tf_op jit(solution)/shard_map/ppermute | solution.py:283
  39.6 1.4 %collective-permute-start.9 = (bf16[4,136,128]{2,1,0:T(8,128)(2,1)S(1)}, bf16[4,136,128]{2,1,0:T(8,128)(2,1)S(1)}, u32[]{:S(2)}, u32[]{:S(2)}) collective-permute-start(bf16[4,136,128]{2,1,0:T(8,128)(2,1)S(1)} %get-tuple-element.50), channel_id=1, source_target_pairs={{0,6},{2,4},{4,2},{6,0},{8,14},{10,12},{12,10},{14,8},{16,22},{18,... | collective-permute-start | bytes 417800 | tf_op jit(solution)/shard_map/ppermute | solution.py:283
  41.0 4.0 %near_12.1 = (f32[4,128,512]{2,1,0:T(8,128)S(1)}, f32[4,1,512]{2,1,0:T(1,128)S(1)}, bf16[4,128,512]{2,1,0:T(8,128)(2,1)S(1)}) custom-call(s32[4]{0:T(128)S(1)} %pad_add_fusion.idx_ref, f32[16]{0:T(128)S(1)} %copy-done.3, f32[2,4096,128]{2,1,0:T(8,128)S(1)} %get-tuple-element.37.q_wide, bf16[2,576,128]{2,1,0:T(8,128)(2,1)S(1)} %get-tuple-element.38.kx_ref, ...), custom_call_target="tpu_custom_call" | custom-call | flops 1600000000 | bytes 4000000 | tf_op jit(solution)/shard_map/near_12/pallas_call | solution.py:351
  45.1 0.0 collective-permute-done.7.refs_7_
  45.1 0.0 collective-permute-done.8.refs_8_
  45.1 0.5 collective-permute-done.9.refs_9_
  45.6 1.4 %final_sent.1.refs_10_ = bf16[16,256,128]{2,1,0:T(8,128)(2,1)S(1)} custom-call(s32[4]{0:T(128)S(1)} %pad_add_fusion.idx_ref, f32[16]{0:T(128)S(1)} %copy-done.3, f32[12,128,512]{2,1,0:T(8,128)S(1)} %get-tuple-element.41.refs_0_, f32[12,1,512]{2,1,0:T(1,128)S(1)} %get-tuple-element.42.refs_7_.refs_1_, bf16[12,128,512]{2,1,0:T(8,128)(2,1)S(1)} %get-tuple-element.43.refs_2_, ...), custom_call_target="tpu_custom_call" | custom-call | tf_op jit(solution)/shard_map/final_sent/pallas_call | solution.py:382
  47.0 0.1 collective-permute-start.10
  47.1 2.1 %final_kept.1._ = bf16[32,256,128]{2,1,0:T(8,128)(2,1)} custom-call(s32[4]{0:T(128)S(1)} %pad_add_fusion.idx_ref, f32[16]{0:T(128)S(1)} %copy-done.3, f32[12,128,512]{2,1,0:T(8,128)S(1)} %get-tuple-element.41.refs_0_, f32[12,1,512]{2,1,0:T(1,128)S(1)} %get-tuple-element.42.refs_7_.refs_1_, bf16[12,128,512]{2,1,0:T(8,128)(2,1)S(1)} %get-tuple-element.43.refs_2_, ...), custom_call_target="tpu_custom_call" | custom-call | flops 1000000000 | bytes 5000000 | tf_op jit(solution)/shard_map/final_kept/pallas_call | solution.py:391
  49.2 0.5 collective-permute-done.10.got_ref
  49.7 1.6 %place.1 = bf16[32,256,128]{2,1,0:T(8,128)(2,1)} custom-call(s32[4]{0:T(128)S(1)} %pad_add_fusion.idx_ref, bf16[16,256,128]{2,1,0:T(8,128)(2,1)S(1)} %collective-permute-done.10.got_ref, bf16[32,256,128]{2,1,0:T(8,128)(2,1)} %final_kept.1._), custom_call_target="tpu_custom_call", output_to_operand_aliasing={{}: (2, {})} | custom-call | tf_op jit(solution)/shard_map/place/pallas_call | solution.py:401
Async XLA Ops:
  4.5 10.8 %collective-permute-start.1 = (bf16[4,136,128]{2,1,0:T(8,128)(2,1)S(1)}, bf16[4,136,128]{2,1,0:T(8,128)(2,1)S(1)}, u32[]{:S(2)}, u32[]{:S(2)}) collective-permute-start(bf16[4,136,128]{2,1,0:T(8,128)(2,1)S(1)} %get-tuple-element.34), channel_id=1, source_target_pairs={{0,2},{2,0},{4,6},{6,4},{8,10},{10,8},{12,14},{14,12},{16,18},{18,... | collective-permute-start | bytes 417800 | tf_op jit(solution)/shard_map/ppermute | solution.py:283
  7.5 8.1 %collective-permute-start.2 = (bf16[4,136,128]{2,1,0:T(8,128)(2,1)S(1)}, bf16[4,136,128]{2,1,0:T(8,128)(2,1)S(1)}, u32[]{:S(2)}, u32[]{:S(2)}) collective-permute-start(bf16[4,136,128]{2,1,0:T(8,128)(2,1)S(1)} %get-tuple-element.35), channel_id=1, source_target_pairs={{0,4},{2,6},{4,0},{6,2},{8,12},{10,14},{12,8},{14,10},{16,20},{18,... | collective-permute-start | bytes 417800 | tf_op jit(solution)/shard_map/ppermute | solution.py:283
  9.0 6.6 %collective-permute-start.3 = (bf16[4,136,128]{2,1,0:T(8,128)(2,1)S(1)}, bf16[4,136,128]{2,1,0:T(8,128)(2,1)S(1)}, u32[]{:S(2)}, u32[]{:S(2)}) collective-permute-start(bf16[4,136,128]{2,1,0:T(8,128)(2,1)S(1)} %get-tuple-element.36), channel_id=1, source_target_pairs={{0,6},{2,4},{4,2},{6,0},{8,14},{10,12},{12,10},{14,8},{16,22},{18,... | collective-permute-start | bytes 417800 | tf_op jit(solution)/shard_map/ppermute | solution.py:283
  9.1 0.9 %copy-start.1 = (bf16[16,128,64]{1,2,0:T(8,128)(2,1)S(1)}, bf16[16,128,64]{1,2,0:T(8,128)(2,1)}, u32[]{:S(2)}) copy-start(bf16[16,128,64]{1,2,0:T(8,128)(2,1)} %param.10) | copy-start | bytes 786436
  10.0 15.0 %copy-start = (bf16[512,16,128]{2,1,0:T(8,128)(2,1)S(1)}, bf16[512,16,128]{2,1,0:T(8,128)(2,1)}, u32[]{:S(2)}) copy-start(bf16[512,16,128]{2,1,0:T(8,128)(2,1)} %q_ref.1) | copy-start | bytes 6291460
  11.3 14.1 %copy-start.2 = (bf16[16,128,64]{1,2,0:T(8,128)(2,1)S(1)}, bf16[16,128,64]{1,2,0:T(8,128)(2,1)}, u32[]{:S(2)}) copy-start(bf16[16,128,64]{1,2,0:T(8,128)(2,1)} %param.9) | copy-start | bytes 786436
  11.3 14.1 %copy-start.3 = (f32[16]{0:T(128)S(1)}, f32[16]{0:T(128)}, u32[]{:S(2)}) copy-start(f32[16]{0:T(128)} %share_ref.7) | copy-start | bytes 196
  11.4 13.7 %collective-permute-start = (bf16[2,2,64,128]{3,2,1,0:T(8,128)(2,1)S(1)}, bf16[2,2,64,128]{3,2,1,0:T(8,128)(2,1)S(1)}, u32[]{:S(2)}, u32[]{:S(2)}) collective-permute-start(bf16[2,2,64,128]{3,2,1,0:T(8,128)(2,1)S(1)} %get-tuple-element.32), channel_id=1, source_target_pairs={{0,2},{2,4},{4,6},{6,8},{8,10},{10,12},{12,14},{14,16},{16,18},{18... | collective-permute-start | bytes 196616 | tf_op jit(solution)/shard_map/ppermute | solution.py:286
  15.7 20.8 %collective-permute-start.4 = (bf16[4,136,128]{2,1,0:T(8,128)(2,1)S(1)}, bf16[4,136,128]{2,1,0:T(8,128)(2,1)S(1)}, u32[]{:S(2)}, u32[]{:S(2)}) collective-permute-start(bf16[4,136,128]{2,1,0:T(8,128)(2,1)S(1)} %totals.1._), channel_id=1, source_target_pairs={{0,8},{2,10},{4,12},{6,14},{8,16},{10,18},{12,20},{14,22},{16,24},... | collective-permute-start | bytes 417800 | tf_op jit(solution)/shard_map/ppermute | solution.py:286
  19.2 17.3 %collective-permute-start.5 = (bf16[4,136,128]{2,1,0:T(8,128)(2,1)S(1)}, bf16[4,136,128]{2,1,0:T(8,128)(2,1)S(1)}, u32[]{:S(2)}, u32[]{:S(2)}) collective-permute-start(bf16[4,136,128]{2,1,0:T(8,128)(2,1)S(1)} %totals.1._), channel_id=1, source_target_pairs={{0,16},{2,18},{4,20},{6,22},{8,24},{10,26},{12,28},{14,30},{1,17},... | collective-permute-start | bytes 417800 | tf_op jit(solution)/shard_map/ppermute | solution.py:286
  23.7 12.8 %collective-permute-start.6 = (bf16[4,136,128]{2,1,0:T(8,128)(2,1)S(1)}, bf16[4,136,128]{2,1,0:T(8,128)(2,1)S(1)}, u32[]{:S(2)}, u32[]{:S(2)}) collective-permute-start(bf16[4,136,128]{2,1,0:T(8,128)(2,1)S(1)} %totals.1._), channel_id=1, source_target_pairs={{0,24},{2,26},{4,28},{6,30},{1,25},{3,27},{5,29},{7,31}} | collective-permute-start | bytes 417800 | tf_op jit(solution)/shard_map/ppermute | solution.py:286
  37.5 7.6 %collective-permute-start.7 = (bf16[4,136,128]{2,1,0:T(8,128)(2,1)S(1)}, bf16[4,136,128]{2,1,0:T(8,128)(2,1)S(1)}, u32[]{:S(2)}, u32[]{:S(2)}) collective-permute-start(bf16[4,136,128]{2,1,0:T(8,128)(2,1)S(1)} %get-tuple-element.48), channel_id=1, source_target_pairs={{0,2},{2,0},{4,6},{6,4},{8,10},{10,8},{12,14},{14,12},{16,18},{18,... | collective-permute-start | bytes 417800 | tf_op jit(solution)/shard_map/ppermute | solution.py:283
  38.8 6.3 %collective-permute-start.8 = (bf16[4,136,128]{2,1,0:T(8,128)(2,1)S(1)}, bf16[4,136,128]{2,1,0:T(8,128)(2,1)S(1)}, u32[]{:S(2)}, u32[]{:S(2)}) collective-permute-start(bf16[4,136,128]{2,1,0:T(8,128)(2,1)S(1)} %get-tuple-element.49), channel_id=1, source_target_pairs={{0,4},{2,6},{4,0},{6,2},{8,12},{10,14},{12,8},{14,10},{16,20},{18,... | collective-permute-start | bytes 417800 | tf_op jit(solution)/shard_map/ppermute | solution.py:283
  39.6 6.0 %collective-permute-start.9 = (bf16[4,136,128]{2,1,0:T(8,128)(2,1)S(1)}, bf16[4,136,128]{2,1,0:T(8,128)(2,1)S(1)}, u32[]{:S(2)}, u32[]{:S(2)}) collective-permute-start(bf16[4,136,128]{2,1,0:T(8,128)(2,1)S(1)} %get-tuple-element.50), channel_id=1, source_target_pairs={{0,6},{2,4},{4,2},{6,0},{8,14},{10,12},{12,10},{14,8},{16,22},{18,... | collective-permute-start | bytes 417800 | tf_op jit(solution)/shard_map/ppermute | solution.py:283
  47.0 2.7 %collective-permute-start.10 = (bf16[16,256,128]{2,1,0:T(8,128)(2,1)S(1)}, bf16[16,256,128]{2,1,0:T(8,128)(2,1)S(1)}, u32[]{:S(2)}, u32[]{:S(2)}) collective-permute-start(bf16[16,256,128]{2,1,0:T(8,128)(2,1)S(1)} %final_sent.1.refs_10_), channel_id=1, source_target_pairs={{0,1},{1,0},{2,3},{3,2},{4,5},{5,4},{6,7},{7,6},{8,9},{9,8},{10,11... | collective-permute-start | bytes 3145736 | tf_op jit(solution)/shard_map/ppermute | solution.py:390

commit v3 on v2

--- a/solution.py
+++ b/solution.py
@@ -13,7 +13,7 @@
 BF = jnp.bfloat16
 F32 = jnp.float32
 LIMIT = 16 * 1024 * 1024
-STEP = 2
+STEP = 4
 SPLIT = 12
 
 
@@ -147,15 +147,28 @@
     feat = halo_logits.shape[0] // count
     for pair in range(0, count, 2):
         qs, mixes, rests, lnums, lsums = [], [], [], [], []
+        products, logits = [], [[], []]
+        for r in range(rows // block):
+            at = r * block
+            both = jnp.concatenate(
+                [
+                    q_wide[g, pl.ds(at * group_size + head % group_size + e, block, stride=group_size), :].astype(BF)
+                    for e in (pair, pair + 1)
+                ],
+                axis=0,
+            )
+            maps = [wq_ref[head + pair], wq_ref[head + pair + 1], kx[at : at + span]]
+            x = mm(jnp.concatenate(maps, axis=0), both, 1, 1)
+            logits[0].append(x[:feat, :block])
+            logits[1].append(x[feat : 2 * feat, block:])
+            products.append(x[2 * feat :])
         for e in (pair, pair + 1):
             halo_feat = features_t(halo_logits[e * feat : (e + 1) * feat]).T[:WINDOW]
             fx[e, :WINDOW] = jnp.where(present, halo_feat.astype(F32), 0.0).astype(BF)
             fx[e, WINDOW:] = feat_ref[head + e]
             mixes.append(jax.nn.sigmoid(jnp.full((1, block), share_ref[head + e], F32)))
             rests.append(1.0 - mixes[-1])
-            q = q_wide[g, pl.ds(head % group_size + e, rows, stride=group_size), :].astype(BF)
-            qs.append(q)
-            qf = features_t(mm(wq_ref[head + e], q, 1, 1))
+            qf = features_t(jnp.concatenate(logits[e - pair], axis=1))
             qf_ref[out + e] = qf
             for r in range(rows // wide):
                 at = r * wide
@@ -188,9 +201,7 @@
         for r in range(rows // block):
             at = r * block
             mask = (band & ((key >= WINDOW) | present)) if r == 0 else band
-            both = jnp.concatenate([q[at : at + block] for q in qs], axis=0)
-            s = mm(kx[at : at + span], both, 1, 1)
-            s = jnp.where(mask, s, -1e30)
+            s = jnp.where(mask, products[r], -1e30)
             p = jnp.exp2((s - jnp.max(s, axis=0, keepdims=True)) * scale)
             wsum = jnp.sum(p, axis=0, keepdims=True)
             wnum = mm(vt[:, at : at + span], p.astype(BF))

time: 51.6 us -> 48.2 us (0.934)
  Pallas kernels: 27.4 us -> 22.8 us
  waiting for transfers between devices: 1.25 us -> 2.43 us
    pallas_call x2, Pallas kernels: 15.1 us -> 10.5 us  [near(): pl.pallas_call(functools.partial(near_kernel, group_size, first, STEP), g...]
    ppermute x6, waiting for transfers between devices: 0.75 us -> 1.93 us  [xor(): return lax.ppermute(x, 'seq', [(i, i ^ m) for i in range(devices)])]
  transfers between devices with their start and end apart: 11 -> 11, of which waited for: 3 -> 3; matrix products, arithmetic and copies ran while one was open for 0% -> 0% of each run, Pallas kernels for 37% -> 30%
where the time goes in v3:
time: 48.2 us; the launch traced here: 47.9 us
  Pallas kernels  22.8 us (47%)
  starting transfers between devices  21.4 us (44%)
  waiting for transfers between devices  2.43 us (5%)
  local copies, waits for them, and re-layouts  0.97 us (2%)
    ppermute x4, starting transfers between devices, shift(): return lax.ppermute(x, 'seq', [(i, i + by) for i in range(devices - by)])  13.3 us
    pallas_call x2, Pallas kernels, near(): pl.pallas_call(functools.partial(near_kernel, group_size, first, STEP), g...  10.5 us
    ppermute x6, starting transfers between devices, xor(): return lax.ppermute(x, 'seq', [(i, i ^ m) for i in range(devices)])  8.1 us
    pallas_call x1, Pallas kernels, per_device(): pl.pallas_call(functools.partial(sent_states_kernel, per_part, group_size...  4.44 us
    pallas_call x1, Pallas kernels, per_device(): pl.pallas_call(functools.partial(final_kept_kernel, per_part, half), in_s...  2.15 us
    ppermute x6, waiting for transfers between devices, xor(): return lax.ppermute(x, 'seq', [(i, i ^ m) for i in range(devices)])  1.93 us
    pallas_call x1, Pallas kernels, per_device(): pl.pallas_call(place_kernel, in_specs=[smem, vmem, pl.BlockSpec(memory_sp...  1.63 us
    pallas_call x1, Pallas kernels, per_device(): pl.pallas_call(functools.partial(final_sent_kernel, per_part, half), in_s...  1.43 us
  transfers between devices with their start and end apart: 11, of which 3 were waited for; matrix products, arithmetic and copies ran while one was open for 0% of the time, Pallas kernels for 30%

profile of v3, /device:TPU:0, one launch (start us, length us, event | category | flops | bytes accessed | tf_op | source)
XLA Modules:
  0.0 47.9 jit_solution(2964423521111713454)
XLA Ops:
  0.0 0.1 pad_add_fusion.idx_ref
  0.1 4.4 %sent_states.1 = (bf16[16,512,128]{2,1,0:T(8,128)(2,1)S(1)}, bf16[2,512,128]{2,1,0:T(8,128)(2,1)S(1)}, bf16[2,512,128]{2,1,0:T(8,128)(2,1)S(1)}, bf16[2,136,512]...) custom-call(s32[4]{0:T(128)S(1)} %pad_add_fusion.idx_ref, ...), custom_call_target="tpu_custom_call" | custom-call | tf_op jit(solution)/shard_map/sent_states/pallas_call | solution.py:303
  4.5 3.0 %collective-permute-start.1 = (bf16[4,136,128]{2,1,0:T(8,128)(2,1)S(1)}, bf16[4,136,128]{2,1,0:T(8,128)(2,1)S(1)}, u32[]{:S(2)}, u32[]{:S(2)}) collective-permute-start(bf16[4,136,128]{2,1,0:T(8,128)(2,1)S(1)} %get-tuple-element.34), channel_id=1, source_target_pairs={{0,2},{2,0},{4,6},{6,4},{8,10},{10,8},{12,14},{14,12},{16,18},{18,... | collective-permute-start | bytes 417800 | tf_op jit(solution)/shard_map/ppermute | solution.py:294
  7.5 1.5 %collective-permute-start.2 = (bf16[4,136,128]{2,1,0:T(8,128)(2,1)S(1)}, bf16[4,136,128]{2,1,0:T(8,128)(2,1)S(1)}, u32[]{:S(2)}, u32[]{:S(2)}) collective-permute-start(bf16[4,136,128]{2,1,0:T(8,128)(2,1)S(1)} %get-tuple-element.35), channel_id=1, source_target_pairs={{0,4},{2,6},{4,0},{6,2},{8,12},{10,14},{12,8},{14,10},{16,20},{18,... | collective-permute-start | bytes 417800 | tf_op jit(solution)/shard_map/ppermute | solution.py:294
  9.0 0.0 collective-permute-start.3
  9.1 0.0 copy-start.1
  9.1 0.9 %copy-done.1 = bf16[16,128,64]{1,2,0:T(8,128)(2,1)S(1)} copy-done((bf16[16,128,64]{1,2,0:T(8,128)(2,1)S(1)}, bf16[16,128,64]{1,2,0:T(8,128)(2,1)}, u32[]{:S(2)}) %copy-start.1) | copy-done | bytes 262168
  10.0 0.0 copy-start
  10.0 1.3 %own_states.1 = (bf16[16,512,128]{2,1,0:T(8,128)(2,1)S(1)}, bf16[4,136,128]{2,1,0:T(8,128)(2,1)S(1)}, bf16[2,2,64,128]{3,2,1,0:T(8,128)(2,1)S(1)}) custom-call(s32[4]{0:T(128)S(1)} %pad_add_fusion.idx_ref, bf16[2,512,128]{2,1,0:T(8,128)(2,1)S(1)} %get-tuple-element.28.k_ref, ...), custom_call_target="tpu_custom_call", output_to_operand_aliasing={{0}: (5, {})} | custom-call | flops 1000000000 | bytes 2000000 | tf_op jit(solution)/shard_map/own_states/pallas_call | solution.py:324
  11.3 0.0 copy-start.2
  11.3 0.0 copy-start.3
  11.4 4.0 %collective-permute-start = (bf16[2,2,64,128]{3,2,1,0:T(8,128)(2,1)S(1)}, bf16[2,2,64,128]{3,2,1,0:T(8,128)(2,1)S(1)}, u32[]{:S(2)}, u32[]{:S(2)}) collective-permute-start(bf16[2,2,64,128]{3,2,1,0:T(8,128)(2,1)S(1)} %get-tuple-element.32), channel_id=1, source_target_pairs={{0,2},{2,4},{4,6},{6,8},{8,10},{10,12},{12,14},{14,16},{16,18},{18... | collective-permute-start | bytes 196616 | tf_op jit(solution)/shard_map/ppermute | solution.py:297
  15.4 0.0 collective-permute-done.1.b.refs_1_
  15.4 0.3 collective-permute-done.2.c.refs_2_
  15.7 0.0 collective-permute-done.3.d.refs_3_
  15.7 0.1 totals.1._
  15.7 3.5 %collective-permute-start.4 = (bf16[4,136,128]{2,1,0:T(8,128)(2,1)S(1)}, bf16[4,136,128]{2,1,0:T(8,128)(2,1)S(1)}, u32[]{:S(2)}, u32[]{:S(2)}) collective-permute-start(bf16[4,136,128]{2,1,0:T(8,128)(2,1)S(1)} %totals.1._), channel_id=1, source_target_pairs={{0,8},{2,10},{4,12},{6,14},{8,16},{10,18},{12,20},{14,22},{16,24},... | collective-permute-start | bytes 417800 | tf_op jit(solution)/shard_map/ppermute | solution.py:297
  19.2 4.5 %collective-permute-start.5 = (bf16[4,136,128]{2,1,0:T(8,128)(2,1)S(1)}, bf16[4,136,128]{2,1,0:T(8,128)(2,1)S(1)}, u32[]{:S(2)}, u32[]{:S(2)}) collective-permute-start(bf16[4,136,128]{2,1,0:T(8,128)(2,1)S(1)} %totals.1._), channel_id=1, source_target_pairs={{0,16},{2,18},{4,20},{6,22},{8,24},{10,26},{12,28},{14,30},{1,17},... | collective-permute-start | bytes 417800 | tf_op jit(solution)/shard_map/ppermute | solution.py:297
  23.7 1.3 %collective-permute-start.6 = (bf16[4,136,128]{2,1,0:T(8,128)(2,1)S(1)}, bf16[4,136,128]{2,1,0:T(8,128)(2,1)S(1)}, u32[]{:S(2)}, u32[]{:S(2)}) collective-permute-start(bf16[4,136,128]{2,1,0:T(8,128)(2,1)S(1)} %totals.1._), channel_id=1, source_target_pairs={{0,24},{2,26},{4,28},{6,30},{1,25},{3,27},{5,29},{7,31}} | collective-permute-start | bytes 417800 | tf_op jit(solution)/shard_map/ppermute | solution.py:297
  25.1 0.0 collective-permute-done.halo_ref
  25.1 0.0 copy-done
  25.1 0.4 prepare.1
  25.5 0.0 copy-done.2
  25.5 0.0 copy-done.3
  25.5 7.6 %near_0.1 = (f32[12,128,512]{2,1,0:T(8,128)S(1)}, f32[12,1,512]{2,1,0:T(1,128)S(1)}, bf16[12,128,512]{2,1,0:T(8,128)(2,1)S(1)}) custom-call(s32[4]{0:T(128)S(1)} %pad_add_fusion.idx_ref, f32[16]{0:T(128)S(1)} %copy-done.3, f32[2,4096,128]{2,1,0:T(8,128)S(1)} %get-tuple-element.37.q_wide, bf16[2,576,128]{2,1,0:T(8,128)(2,1)S(1)} %get-tuple-element.38.kx_ref, ...), custom_call_target="tpu_custom_call" | custom-call | flops 4800000000 | bytes 12000000 | tf_op jit(solution)/shard_map/near_0/pallas_call | solution.py:362
  33.1 0.0 collective-permute-done.4.refs_4_
  33.1 0.0 collective-permute-done.5.refs_5_
  33.1 0.0 collective-permute-done.6.refs_6_
  33.1 0.9 %prefixes.1 = (bf16[4,136,128]{2,1,0:T(8,128)(2,1)S(1)}, bf16[4,136,128]{2,1,0:T(8,128)(2,1)S(1)}, bf16[4,136,128]{2,1,0:T(8,128)(2,1)S(1)}, bf16[4,136,128]{2,1,0:T(8,128)(2,1)S(1)}) custom-call(s32[4]{0:T(128)S(1)} %pad_add_fusion.idx_ref, bf16[4,136,128]{2,1,0:T(8,128)(2,1)S(1)} %get-tuple-element.33.a.refs_0_, ...), custom_call_target="tpu_custom_call" | custom-call | tf_op jit(solution)/shard_map/prefixes/pallas_call | solution.py:381
  34.1 1.3 %collective-permute-start.7 = (bf16[4,136,128]{2,1,0:T(8,128)(2,1)S(1)}, bf16[4,136,128]{2,1,0:T(8,128)(2,1)S(1)}, u32[]{:S(2)}, u32[]{:S(2)}) collective-permute-start(bf16[4,136,128]{2,1,0:T(8,128)(2,1)S(1)} %get-tuple-element.48), channel_id=1, source_target_pairs={{0,2},{2,0},{4,6},{6,4},{8,10},{10,8},{12,14},{14,12},{16,18},{18,... | collective-permute-start | bytes 417800 | tf_op jit(solution)/shard_map/ppermute | solution.py:294
  35.3 0.8 %collective-permute-start.8 = (bf16[4,136,128]{2,1,0:T(8,128)(2,1)S(1)}, bf16[4,136,128]{2,1,0:T(8,128)(2,1)S(1)}, u32[]{:S(2)}, u32[]{:S(2)}) collective-permute-start(bf16[4,136,128]{2,1,0:T(8,128)(2,1)S(1)} %get-tuple-element.49), channel_id=1, source_target_pairs={{0,4},{2,6},{4,0},{6,2},{8,12},{10,14},{12,8},{14,10},{16,20},{18,... | collective-permute-start | bytes 417800 | tf_op jit(solution)/shard_map/ppermute | solution.py:294
  36.2 1.4 %collective-permute-start.9 = (bf16[4,136,128]{2,1,0:T(8,128)(2,1)S(1)}, bf16[4,136,128]{2,1,0:T(8,128)(2,1)S(1)}, u32[]{:S(2)}, u32[]{:S(2)}) collective-permute-start(bf16[4,136,128]{2,1,0:T(8,128)(2,1)S(1)} %get-tuple-element.50), channel_id=1, source_target_pairs={{0,6},{2,4},{4,2},{6,0},{8,14},{10,12},{12,10},{14,8},{16,22},{18,... | collective-permute-start | bytes 417800 | tf_op jit(solution)/shard_map/ppermute | solution.py:294
  37.6 2.9 %near_12.1 = (f32[4,128,512]{2,1,0:T(8,128)S(1)}, f32[4,1,512]{2,1,0:T(1,128)S(1)}, bf16[4,128,512]{2,1,0:T(8,128)(2,1)S(1)}) custom-call(s32[4]{0:T(128)S(1)} %pad_add_fusion.idx_ref, f32[16]{0:T(128)S(1)} %copy-done.3, f32[2,4096,128]{2,1,0:T(8,128)S(1)} %get-tuple-element.37.q_wide, bf16[2,576,128]{2,1,0:T(8,128)(2,1)S(1)} %get-tuple-element.38.kx_ref, ...), custom_call_target="tpu_custom_call" | custom-call | flops 1600000000 | bytes 4000000 | tf_op jit(solution)/shard_map/near_12/pallas_call | solution.py:362
  40.5 0.0 collective-permute-done.7.refs_7_
  40.5 0.0 collective-permute-done.8.refs_8_
  40.5 1.6 %collective-permute-done.9.refs_9_ = bf16[4,136,128]{2,1,0:T(8,128)(2,1)S(1)} collective-permute-done((bf16[4,136,128]{2,1,0:T(8,128)(2,1)S(1)}, bf16[4,136,128]{2,1,0:T(8,128)(2,1)S(1)}, u32[]{:S(2)}, u32[]{:S(2)}) %collective-permute-start.9) | collective-permute-done | bytes 139296 | tf_op jit(solution)/shard_map/ppermute | solution.py:294
  42.1 1.4 %final_sent.1.refs_10_ = bf16[16,256,128]{2,1,0:T(8,128)(2,1)S(1)} custom-call(s32[4]{0:T(128)S(1)} %pad_add_fusion.idx_ref, f32[16]{0:T(128)S(1)} %copy-done.3, f32[12,128,512]{2,1,0:T(8,128)S(1)} %get-tuple-element.41.refs_0_, f32[12,1,512]{2,1,0:T(1,128)S(1)} %get-tuple-element.42.refs_7_.refs_1_, bf16[12,128,512]{2,1,0:T(8,128)(2,1)S(1)} %get-tuple-element.43.refs_2_, ...), custom_call_target="tpu_custom_call" | custom-call | tf_op jit(solution)/shard_map/final_sent/pallas_call | solution.py:393
  43.6 0.1 collective-permute-start.10
  43.6 2.1 %final_kept.1._ = bf16[32,256,128]{2,1,0:T(8,128)(2,1)} custom-call(s32[4]{0:T(128)S(1)} %pad_add_fusion.idx_ref, f32[16]{0:T(128)S(1)} %copy-done.3, f32[12,128,512]{2,1,0:T(8,128)S(1)} %get-tuple-element.41.refs_0_, f32[12,1,512]{2,1,0:T(1,128)S(1)} %get-tuple-element.42.refs_7_.refs_1_, bf16[12,128,512]{2,1,0:T(8,128)(2,1)S(1)} %get-tuple-element.43.refs_2_, ...), custom_call_target="tpu_custom_call" | custom-call | flops 1000000000 | bytes 5000000 | tf_op jit(solution)/shard_map/final_kept/pallas_call | solution.py:402
  45.8 0.5 %collective-permute-done.10.got_ref = bf16[16,256,128]{2,1,0:T(8,128)(2,1)S(1)} collective-permute-done((bf16[16,256,128]{2,1,0:T(8,128)(2,1)S(1)}, bf16[16,256,128]{2,1,0:T(8,128)(2,1)S(1)}, u32[]{:S(2)}, u32[]{:S(2)}) %collective-permute-start.10) | collective-permute-done | bytes 1048608 | tf_op jit(solution)/shard_map/ppermute | solution.py:401
  46.3 1.6 %place.1 = bf16[32,256,128]{2,1,0:T(8,128)(2,1)} custom-call(s32[4]{0:T(128)S(1)} %pad_add_fusion.idx_ref, bf16[16,256,128]{2,1,0:T(8,128)(2,1)S(1)} %collective-permute-done.10.got_ref, bf16[32,256,128]{2,1,0:T(8,128)(2,1)} %final_kept.1._), custom_call_target="tpu_custom_call", output_to_operand_aliasing={{}: (2, {})} | custom-call | tf_op jit(solution)/shard_map/place/pallas_call | solution.py:412
Async XLA Ops:
  4.5 10.8 %collective-permute-start.1 = (bf16[4,136,128]{2,1,0:T(8,128)(2,1)S(1)}, bf16[4,136,128]{2,1,0:T(8,128)(2,1)S(1)}, u32[]{:S(2)}, u32[]{:S(2)}) collective-permute-start(bf16[4,136,128]{2,1,0:T(8,128)(2,1)S(1)} %get-tuple-element.34), channel_id=1, source_target_pairs={{0,2},{2,0},{4,6},{6,4},{8,10},{10,8},{12,14},{14,12},{16,18},{18,... | collective-permute-start | bytes 417800 | tf_op jit(solution)/shard_map/ppermute | solution.py:294
  7.5 8.1 %collective-permute-start.2 = (bf16[4,136,128]{2,1,0:T(8,128)(2,1)S(1)}, bf16[4,136,128]{2,1,0:T(8,128)(2,1)S(1)}, u32[]{:S(2)}, u32[]{:S(2)}) collective-permute-start(bf16[4,136,128]{2,1,0:T(8,128)(2,1)S(1)} %get-tuple-element.35), channel_id=1, source_target_pairs={{0,4},{2,6},{4,0},{6,2},{8,12},{10,14},{12,8},{14,10},{16,20},{18,... | collective-permute-start | bytes 417800 | tf_op jit(solution)/shard_map/ppermute | solution.py:294
  9.0 6.6 %collective-permute-start.3 = (bf16[4,136,128]{2,1,0:T(8,128)(2,1)S(1)}, bf16[4,136,128]{2,1,0:T(8,128)(2,1)S(1)}, u32[]{:S(2)}, u32[]{:S(2)}) collective-permute-start(bf16[4,136,128]{2,1,0:T(8,128)(2,1)S(1)} %get-tuple-element.36), channel_id=1, source_target_pairs={{0,6},{2,4},{4,2},{6,0},{8,14},{10,12},{12,10},{14,8},{16,22},{18,... | collective-permute-start | bytes 417800 | tf_op jit(solution)/shard_map/ppermute | solution.py:294
  9.1 0.9 %copy-start.1 = (bf16[16,128,64]{1,2,0:T(8,128)(2,1)S(1)}, bf16[16,128,64]{1,2,0:T(8,128)(2,1)}, u32[]{:S(2)}) copy-start(bf16[16,128,64]{1,2,0:T(8,128)(2,1)} %param.10) | copy-start | bytes 786436
  10.0 15.0 %copy-start = (bf16[512,16,128]{2,1,0:T(8,128)(2,1)S(1)}, bf16[512,16,128]{2,1,0:T(8,128)(2,1)}, u32[]{:S(2)}) copy-start(bf16[512,16,128]{2,1,0:T(8,128)(2,1)} %q_ref.1) | copy-start | bytes 6291460
  11.3 14.1 %copy-start.2 = (bf16[16,128,64]{1,2,0:T(8,128)(2,1)S(1)}, bf16[16,128,64]{1,2,0:T(8,128)(2,1)}, u32[]{:S(2)}) copy-start(bf16[16,128,64]{1,2,0:T(8,128)(2,1)} %param.9) | copy-start | bytes 786436
  11.3 14.1 %copy-start.3 = (f32[16]{0:T(128)S(1)}, f32[16]{0:T(128)}, u32[]{:S(2)}) copy-start(f32[16]{0:T(128)} %share_ref.7) | copy-start | bytes 196
  11.4 13.7 %collective-permute-start = (bf16[2,2,64,128]{3,2,1,0:T(8,128)(2,1)S(1)}, bf16[2,2,64,128]{3,2,1,0:T(8,128)(2,1)S(1)}, u32[]{:S(2)}, u32[]{:S(2)}) collective-permute-start(bf16[2,2,64,128]{3,2,1,0:T(8,128)(2,1)S(1)} %get-tuple-element.32), channel_id=1, source_target_pairs={{0,2},{2,4},{4,6},{6,8},{8,10},{10,12},{12,14},{14,16},{16,18},{18... | collective-permute-start | bytes 196616 | tf_op jit(solution)/shard_map/ppermute | solution.py:297
  15.7 17.4 %collective-permute-start.4 = (bf16[4,136,128]{2,1,0:T(8,128)(2,1)S(1)}, bf16[4,136,128]{2,1,0:T(8,128)(2,1)S(1)}, u32[]{:S(2)}, u32[]{:S(2)}) collective-permute-start(bf16[4,136,128]{2,1,0:T(8,128)(2,1)S(1)} %totals.1._), channel_id=1, source_target_pairs={{0,8},{2,10},{4,12},{6,14},{8,16},{10,18},{12,20},{14,22},{16,24},... | collective-permute-start | bytes 417800 | tf_op jit(solution)/shard_map/ppermute | solution.py:297
  19.2 13.9 %collective-permute-start.5 = (bf16[4,136,128]{2,1,0:T(8,128)(2,1)S(1)}, bf16[4,136,128]{2,1,0:T(8,128)(2,1)S(1)}, u32[]{:S(2)}, u32[]{:S(2)}) collective-permute-start(bf16[4,136,128]{2,1,0:T(8,128)(2,1)S(1)} %totals.1._), channel_id=1, source_target_pairs={{0,16},{2,18},{4,20},{6,22},{8,24},{10,26},{12,28},{14,30},{1,17},... | collective-permute-start | bytes 417800 | tf_op jit(solution)/shard_map/ppermute | solution.py:297
  23.7 9.4 %collective-permute-start.6 = (bf16[4,136,128]{2,1,0:T(8,128)(2,1)S(1)}, bf16[4,136,128]{2,1,0:T(8,128)(2,1)S(1)}, u32[]{:S(2)}, u32[]{:S(2)}) collective-permute-start(bf16[4,136,128]{2,1,0:T(8,128)(2,1)S(1)} %totals.1._), channel_id=1, source_target_pairs={{0,24},{2,26},{4,28},{6,30},{1,25},{3,27},{5,29},{7,31}} | collective-permute-start | bytes 417800 | tf_op jit(solution)/shard_map/ppermute | solution.py:297
  34.1 6.4 %collective-permute-start.7 = (bf16[4,136,128]{2,1,0:T(8,128)(2,1)S(1)}, bf16[4,136,128]{2,1,0:T(8,128)(2,1)S(1)}, u32[]{:S(2)}, u32[]{:S(2)}) collective-permute-start(bf16[4,136,128]{2,1,0:T(8,128)(2,1)S(1)} %get-tuple-element.48), channel_id=1, source_target_pairs={{0,2},{2,0},{4,6},{6,4},{8,10},{10,8},{12,14},{14,12},{16,18},{18,... | collective-permute-start | bytes 417800 | tf_op jit(solution)/shard_map/ppermute | solution.py:294
  35.3 5.2 %collective-permute-start.8 = (bf16[4,136,128]{2,1,0:T(8,128)(2,1)S(1)}, bf16[4,136,128]{2,1,0:T(8,128)(2,1)S(1)}, u32[]{:S(2)}, u32[]{:S(2)}) collective-permute-start(bf16[4,136,128]{2,1,0:T(8,128)(2,1)S(1)} %get-tuple-element.49), channel_id=1, source_target_pairs={{0,4},{2,6},{4,0},{6,2},{8,12},{10,14},{12,8},{14,10},{16,20},{18,... | collective-permute-start | bytes 417800 | tf_op jit(solution)/shard_map/ppermute | solution.py:294
  36.2 6.0 %collective-permute-start.9 = (bf16[4,136,128]{2,1,0:T(8,128)(2,1)S(1)}, bf16[4,136,128]{2,1,0:T(8,128)(2,1)S(1)}, u32[]{:S(2)}, u32[]{:S(2)}) collective-permute-start(bf16[4,136,128]{2,1,0:T(8,128)(2,1)S(1)} %get-tuple-element.50), channel_id=1, source_target_pairs={{0,6},{2,4},{4,2},{6,0},{8,14},{10,12},{12,10},{14,8},{16,22},{18,... | collective-permute-start | bytes 417800 | tf_op jit(solution)/shard_map/ppermute | solution.py:294
  43.6 2.7 %collective-permute-start.10 = (bf16[16,256,128]{2,1,0:T(8,128)(2,1)S(1)}, bf16[16,256,128]{2,1,0:T(8,128)(2,1)S(1)}, u32[]{:S(2)}, u32[]{:S(2)}) collective-permute-start(bf16[16,256,128]{2,1,0:T(8,128)(2,1)S(1)} %final_sent.1.refs_10_), channel_id=1, source_target_pairs={{0,1},{1,0},{2,3},{3,2},{4,5},{5,4},{6,7},{7,6},{8,9},{9,8},{10,11... | collective-permute-start | bytes 3145736 | tf_op jit(solution)/shard_map/ppermute | solution.py:401

commit v4 on v3

--- a/solution.py
+++ b/solution.py
@@ -31,22 +31,18 @@
     return jnp.concatenate([up, down], axis=0).astype(BF)
 
 
-def split_norm(state):
+def put_state(ref, e, state, norm):
     width = state.shape[-1]
-    norm = state[width : width + 1]
     high = norm.astype(BF).astype(F32)
-    low = norm - high
     row = lax.broadcasted_iota(jnp.int32, (8, width), 0)
-    tail = jnp.where(row == 0, high, jnp.where(row == 1, low, 0.0))
-    return jnp.concatenate([state[:width], tail], axis=0).astype(BF)
-
-
-def join_norm(piece):
-    wide = piece.astype(F32)
-    width = wide.shape[-1]
-    norm = wide[width : width + 1] + wide[width + 1 : width + 2]
-    row = lax.broadcasted_iota(jnp.int32, (8, width), 0)
-    return jnp.concatenate([wide[:width], jnp.where(row == 0, norm, 0.0)], axis=0)
+    ref[e, :width] = state.astype(BF)
+    ref[e, width:] = jnp.where(row == 0, high, jnp.where(row == 1, norm - high, 0.0)).astype(BF)
+
+
+def get_state(ref, e):
+    width = ref.shape[-1]
+    last = ref[e, width:].astype(F32)
+    return ref[e, :width].astype(F32), last[0:1] + last[1:2]
 
 
 def values_with_one(values):
@@ -62,7 +58,9 @@
     for e in range(per_part):
         feat = features_t(logits[e * f : (e + 1) * f]).T
         feat_ref[head + e] = feat
-        out[e] = split_norm(mm(vt_ref[g], feat))
+        state = mm(vt_ref[g], feat)
+        width = state.shape[-1]
+        put_state(out, e, state[:width], state[width : width + 1])
 
 
 def sent_states_kernel(
@@ -98,23 +96,29 @@
 
 def total_kernel(a, b, c, d, out):
     for e in range(out.shape[0]):
-        out[e] = split_norm(join_norm(a[e]) + join_norm(b[e]) + join_norm(c[e]) + join_norm(d[e]))
-
-
-def prefix_kernel(zs, idx_ref, *refs):
-    own, outs = refs[:PART], refs[PART + zs + 1 :]
+        states, norms = zip(*(get_state(ref, e) for ref in (a, b, c, d)))
+        put_state(out, e, sum(states[1:], states[0]), sum(norms[1:], norms[0]))
+
+
+def prefix_kernel(zs, exchanged, idx_ref, *refs):
+    layer = idx_ref[1] // PART
+    own, later, outs = refs[:PART], refs[PART : PART + zs], refs[PART + zs + 1 :]
     me = idx_ref[0]
     for e in range(outs[0].shape[0]):
-        base = jnp.zeros(own[0].shape[1:], F32)
-        for k in range(zs):
-            base = base + join_norm(refs[PART + k][e])
-        terms = [join_norm(r[e]) for r in own]
+        base = None
+        for k, ref in enumerate(later, 1):
+            term = get_state(ref, e)
+            if exchanged:
+                term = tuple(jnp.where(lax.bitwise_xor(layer, k) < layer, x, 0.0) for x in term)
+            base = term if base is None else (base[0] + term[0], base[1] + term[1])
+        terms = [get_state(ref, e) for ref in own]
         for m in range(PART):
             total = base
             for k in range(PART):
-                earlier = lax.bitwise_xor(me, k) < lax.bitwise_xor(me, m)
-                total = total + jnp.where(earlier, terms[k], 0.0)
-            outs[m][e] = split_norm(total)
+                if k != m:
+                    earlier = lax.bitwise_xor(me, k) < lax.bitwise_xor(me, m)
+                    total = tuple(t + jnp.where(earlier, x, 0.0) for t, x in zip(total, terms[k]))
+            put_state(outs[m], e, *total)
 
 
 def prepare_kernel(group_size, q_ref, k_ref, v_ref, halo_ref, _, q_wide, kx, vt):
@@ -127,10 +131,11 @@
         vt[g] = jnp.concatenate([halo_ref[1, g], v_ref[g]], axis=0).T
 
 
-def near_kernel(group_size, first, count, idx_ref, share_ref, q_wide, kx_ref, vt_ref, feat_ref, wq_ref, wk_ref, *refs):
+def near_kernel(group_size, per_part, first, count, idx_ref, share_ref, q_wide, kx_ref, vt_ref, feat_ref, wq_ref, wk_ref, *refs):
     num_ref, den_ref, qf_ref, fx = refs[-4:]
     out = pl.program_id(0) * count
-    head = first + out
+    slot = first + out
+    head = lax.bitwise_xor(idx_ref[0], slot // per_part) * per_part + slot % per_part
     g = head // group_size
     rows, width = feat_ref.shape[1:]
     scale = np.float32(np.log2(np.e) / np.sqrt(width))
@@ -217,52 +222,66 @@
                 )
 
 
-def finished(per_part, which, half, idx_ref, share_ref, held, pieces):
+def finished(per_part, which, half, first, idx_ref, share_ref, held, pieces):
     at = pl.ds(pl.multiple_of(idx_ref[which] * half, 128), half)
-    head = 0
+    slot = 0
     for num, den, qf in held:
         count, width, _ = num.shape
-        for e in range(count):
-            m = lax.bitwise_xor(idx_ref[0], head // per_part)
-            state = pieces[0][head % per_part]
-            for k in range(1, PART):
-                state = jnp.where(m == k, pieces[k][head % per_part], state)
+        for n in range(count):
+            m, e = divmod(slot, per_part)
+            slot += 1
+            if not first <= m < first + len(pieces):
+                continue
+            head = lax.bitwise_xor(idx_ref[0], m) * per_part + e
             rest = 1.0 - jax.nn.sigmoid(jnp.full((1, half), share_ref[head], F32))
-            both = mm(state, qf[e, :, at])
-            numer = num[e, :, at] + rest * both[:width]
-            denom = den[e, :, at] + rest * (both[width : width + 1] + both[width + 1 : width + 2])
-            yield head, (numer * (1.0 / denom)).astype(BF).T
-            head += 1
-
-
-def split_refs(refs):
-    held = [refs[3 * k : 3 * k + 3] for k in range(2)]
-    return held, refs[6 : 6 + PART]
+            both = mm(pieces[m - first][e], qf[n, :, at])
+            numer = num[n, :, at] + rest * both[:width]
+            denom = den[n, :, at] + rest * (both[width : width + 1] + both[width + 1 : width + 2])
+            yield m, e, (numer * (1.0 / denom)).astype(BF).T
+
+
+def quarter_at(core, m, per_part, idx_ref):
+    return pl.ds((idx_ref[core] * PART + lax.bitwise_xor(idx_ref[0], m)) * per_part, per_part)
+
+
+def final_own_kernel(per_part, half, idx_ref, share_ref, num, den, qf, piece, sent_ref, kept):
+    held, pieces = [(num, den, qf)], [piece]
+    for _, e, rows in finished(per_part, 3, half, 0, idx_ref, share_ref, held, pieces):
+        sent_ref[e] = rows
+    for _, e, rows in finished(per_part, 2, half, 0, idx_ref, share_ref, held, pieces):
+        kept[e] = rows
 
 
 def final_sent_kernel(per_part, half, idx_ref, share_ref, *refs):
-    out_ref = refs[-1]
-    for head, rows in finished(per_part, 3, half, idx_ref, share_ref, *split_refs(refs)):
-        out_ref[head] = rows
+    held, pieces, out_ref = (refs[:3], refs[3:6]), refs[6 : 5 + PART], refs[-1]
+    for m, e, rows in finished(per_part, 3, half, 1, idx_ref, share_ref, held, pieces):
+        out_ref[(m - 1) * per_part + e] = rows
 
 
 def final_kept_kernel(per_part, half, idx_ref, share_ref, *refs):
+    held, pieces = (refs[:3], refs[3:6]), refs[6 : 5 + PART]
     out_ref, kept, sems = refs[-3:]
-    heads = kept.shape[0]
-    copies = []
-    for head, rows in finished(per_part, 2, half, idx_ref, share_ref, *split_refs(refs)):
-        kept[head] = rows
-        copies.append(pltpu.make_async_copy(kept.at[head], out_ref.at[heads * idx_ref[2] + head], sems.at[head]))
-        copies[-1].start()
+    copies = [pltpu.make_async_copy(refs[5 + PART], out_ref.at[quarter_at(2, 0, per_part, idx_ref)], sems.at[0])]
+    copies[0].start()
+    for m, e, rows in finished(per_part, 2, half, 1, idx_ref, share_ref, held, pieces):
+        kept[m - 1, e] = rows
+        if e == per_part - 1:
+            copies.append(
+                pltpu.make_async_copy(kept.at[m - 1], out_ref.at[quarter_at(2, m, per_part, idx_ref)], sems.at[m])
+            )
+            copies[-1].start()
     for copy in copies:
         copy.wait()
 
 
-def place_kernel(idx_ref, got_ref, _, out_ref, sems):
-    heads = got_ref.shape[0]
+def place_kernel(per_part, idx_ref, own_ref, got_ref, _, out_ref, sems):
     copies = [
-        pltpu.make_async_copy(got_ref.at[head], out_ref.at[heads * idx_ref[3] + head], sems.at[head])
-        for head in range(heads)
+        pltpu.make_async_copy(
+            got_ref.at[pl.ds((m - 1) * per_part, per_part)] if m else own_ref,
+            out_ref.at[quarter_at(3, m, per_part, idx_ref)],
+            sems.at[m],
+        )
+        for m in range(PART)
     ]
     for copy in copies:
         copy.start()
@@ -336,8 +355,9 @@
     total = pl.pallas_call(
         total_kernel, in_specs=[vmem] * PART, out_specs=vmem, out_shape=piece_shape, compiler_params=params, name="totals"
     )(*pieces)
-    if zs <= 4:
-        earlier = [shift(total, PART * k) for k in range(1, zs)]
+    exchanged = zs in (1, 2, 4)
+    if exchanged:
+        earlier = [xor(total, PART * k) for k in range(1, zs)]
     else:
         columns = [[z * PART + k for z in range(zs)] for k in range(PART)]
         gathered = lax.all_gather(total, "seq", axis_index_groups=columns)
@@ -360,7 +380,7 @@
 
     def near(first, count, after):
         return pl.pallas_call(
-            functools.partial(near_kernel, group_size, first, STEP),
+            functools.partial(near_kernel, group_size, per_part, first, STEP),
             grid=(count // STEP,),
             in_specs=[smem, smem] + [vmem] * 6 + [anywhere] * len(after),
             out_specs=[vmem] * 3,
@@ -379,7 +399,7 @@
 
     held = list(near(0, SPLIT, []))
     prefixes = pl.pallas_call(
-        functools.partial(prefix_kernel, len(earlier)),
+        functools.partial(prefix_kernel, len(earlier), exchanged),
         in_specs=[smem] + [vmem] * (PART + len(earlier)) + [anywhere],
         out_specs=[vmem] * PART,
         out_shape=[piece_shape] * PART,
@@ -390,35 +410,50 @@
     held += near(SPLIT, heads - SPLIT, [prefixes[0]])
 
     half = rows // 2
-    theirs = pl.pallas_call(
+    out_shape = jax.ShapeDtypeStruct((2 * heads, half, width), BF)
+
+    def swapped(x):
+        return lax.ppermute(x, "head", [(0, 1), (1, 0)])
+
+    sent_own, kept_own = pl.pallas_call(
+        functools.partial(final_own_kernel, per_part, half),
+        in_specs=[smem, smem] + [vmem] * 4,
+        out_specs=[vmem] * 2,
+        out_shape=[jax.ShapeDtypeStruct((per_part, half, width), BF)] * 2,
+        compiler_params=params,
+        cost_estimate=pl.CostEstimate(flops=5 * 10**8, bytes_accessed=2 * 10**6, transcendentals=0),
+        name="final_own",
+    )(idx, window_param, *held[:3], prior[0])
+    got_own = swapped(sent_own)
+    sent = pl.pallas_call(
         functools.partial(final_sent_kernel, per_part, half),
-        in_specs=[smem, smem] + [vmem] * (6 + PART),
+        in_specs=[smem, smem] + [vmem] * (5 + PART) + [anywhere],
         out_specs=vmem,
-        out_shape=jax.ShapeDtypeStruct((heads, half, width), BF),
+        out_shape=jax.ShapeDtypeStruct((heads - per_part, half, width), BF),
         compiler_params=params,
         name="final_sent",
-    )(idx, window_param, *held, *prior)
-    got = lax.ppermute(theirs, "head", [(0, 1), (1, 0)])
+    )(idx, window_param, *held, *prior[1:], sent_own)
+    got = swapped(sent)
     out = pl.pallas_call(
         functools.partial(final_kept_kernel, per_part, half),
         in_specs=[smem, smem] + [vmem] * (6 + PART) + [anywhere],
-        out_specs=pl.BlockSpec(memory_space=pltpu.HBM),
-        out_shape=jax.ShapeDtypeStruct((2 * heads, half, width), BF),
-        scratch_shapes=[pltpu.VMEM((heads, half, width), BF), pltpu.SemaphoreType.DMA((heads,))],
+        out_specs=hbm,
+        out_shape=out_shape,
+        scratch_shapes=[pltpu.VMEM((PART - 1, per_part, half, width), BF), pltpu.SemaphoreType.DMA((PART,))],
         compiler_params=params,
         cost_estimate=pl.CostEstimate(flops=10**9, bytes_accessed=5 * 10**6, transcendentals=0),
         name="final_kept",
-    )(idx, window_param, *held, *prior, theirs)
+    )(idx, window_param, *held, *prior[1:], kept_own, sent)
     return pl.pallas_call(
-        place_kernel,
-        in_specs=[smem, vmem, pl.BlockSpec(memory_space=pltpu.HBM)],
-        out_specs=pl.BlockSpec(memory_space=pltpu.HBM),
-        out_shape=jax.ShapeDtypeStruct(out.shape, BF),
-        scratch_shapes=[pltpu.SemaphoreType.DMA((heads,))],
-        input_output_aliases={2: 0},
+        functools.partial(place_kernel, per_part),
+        in_specs=[smem, vmem, vmem, hbm],
+        out_specs=hbm,
+        out_shape=out_shape,
+        scratch_shapes=[pltpu.SemaphoreType.DMA((PART,))],
+        input_output_aliases={3: 0},
         compiler_params=params,
         name="place",
-    )(idx, got, out)
+    )(idx, got_own, got, out)
 
 
 def solution(mesh):

time: 48.2 us -> 46 us (0.954)
  starting transfers between devices: 21.4 us -> 17.1 us
  waiting for transfers between devices: 2.43 us -> 4.41 us
    ppermute x4 -> x1, starting transfers between devices: 13.3 us -> 3.98 us  [shift(): return lax.ppermute(x, 'seq', [(i, i + by) for i in range(devices - by)])]
    ppermute x6 -> x9, starting transfers between devices: 8.1 us -> 12.6 us  [xor(): return lax.ppermute(x, 'seq', [(i, i ^ m) for i in range(devices)])]
    ppermute x6 -> x9, waiting for transfers between devices: 1.93 us -> 4.1 us  [xor(): return lax.ppermute(x, 'seq', [(i, i ^ m) for i in range(devices)])]
    pallas_call x4 -> x5, Pallas kernels: 13 us -> 14 us  [the longest x2 10.5 us: near(): pl.pallas_call(functools.partial(near_kernel, group_size, per_part, first...]
    ppermute x1 -> x2, starting transfers between devices: 0.07 us -> 0.57 us  [swapped(): return lax.ppermute(x, 'head', [(0, 1), (1, 0)])]
    unnamed x8 -> x10, local copies, waits for them, and re-layouts: 0.97 us -> 0.97 us
  transfers between devices with their start and end apart: 11 -> 12, of which waited for: 3 -> 4; matrix products, arithmetic and copies ran while one was open for 0% -> 0% of each run, Pallas kernels for 30% -> 33%
where the time goes in v4:
time: 46 us; the launch traced here: 45.8 us
  Pallas kernels  23.1 us (50%)
  starting transfers between devices  17.1 us (37%)
  waiting for transfers between devices  4.41 us (10%)
  local copies, waits for them, and re-layouts  0.97 us (2%)
    ppermute x9, starting transfers between devices, xor(): return lax.ppermute(x, 'seq', [(i, i ^ m) for i in range(devices)])  12.6 us
    pallas_call x2, Pallas kernels, near(): pl.pallas_call(functools.partial(near_kernel, group_size, per_part, first...  10.5 us
    pallas_call x1, Pallas kernels, per_device(): pl.pallas_call(functools.partial(sent_states_kernel, per_part, group_size...  4.42 us
    ppermute x9, waiting for transfers between devices, xor(): return lax.ppermute(x, 'seq', [(i, i ^ m) for i in range(devices)])  4.1 us
    ppermute x1, starting transfers between devices, shift(): return lax.ppermute(x, 'seq', [(i, i + by) for i in range(devices - by)])  3.98 us
    pallas_call x1, Pallas kernels, per_device(): pl.pallas_call(functools.partial(final_kept_kernel, per_part, half), in_s...  1.83 us
    pallas_call x1, Pallas kernels, per_device(): pl.pallas_call(functools.partial(place_kernel, per_part), in_specs=[smem,...  1.54 us
    pallas_call x1, Pallas kernels, per_device(): pl.pallas_call(functools.partial(own_states_kernel, per_part, group_size)...  1.3 us
  transfers between devices with their start and end apart: 12, of which 4 were waited for; matrix products, arithmetic and copies ran while one was open for 0% of the time, Pallas kernels for 33%

profile of v4, /device:TPU:0, one launch (start us, length us, event | category | flops | bytes accessed | tf_op | source)
XLA Modules:
  0.0 45.8 jit_solution(16607680613532959441)
XLA Ops:
  0.0 0.1 pad_add_fusion.idx_ref
  0.1 4.4 %sent_states.1 = (bf16[16,512,128]{2,1,0:T(8,128)(2,1)S(1)}, bf16[2,512,128]{2,1,0:T(8,128)(2,1)S(1)}, bf16[2,512,128]{2,1,0:T(8,128)(2,1)S(1)}, bf16[2,136,512]...) custom-call(s32[4]{0:T(128)S(1)} %pad_add_fusion.idx_ref, ...), custom_call_target="tpu_custom_call" | custom-call | tf_op jit(solution)/shard_map/sent_states/pallas_call | solution.py:322
  4.5 3.0 %collective-permute-start.1 = (bf16[4,136,128]{2,1,0:T(8,128)(2,1)S(1)}, bf16[4,136,128]{2,1,0:T(8,128)(2,1)S(1)}, u32[]{:S(2)}, u32[]{:S(2)}) collective-permute-start(bf16[4,136,128]{2,1,0:T(8,128)(2,1)S(1)} %get-tuple-element.36), channel_id=1, source_target_pairs={{0,2},{2,0},{4,6},{6,4},{8,10},{10,8},{12,14},{14,12},{16,18},{18,... | collective-permute-start | bytes 417800 | tf_op jit(solution)/shard_map/ppermute | solution.py:313
  7.5 1.5 %collective-permute-start.2 = (bf16[4,136,128]{2,1,0:T(8,128)(2,1)S(1)}, bf16[4,136,128]{2,1,0:T(8,128)(2,1)S(1)}, u32[]{:S(2)}, u32[]{:S(2)}) collective-permute-start(bf16[4,136,128]{2,1,0:T(8,128)(2,1)S(1)} %get-tuple-element.37), channel_id=1, source_target_pairs={{0,4},{2,6},{4,0},{6,2},{8,12},{10,14},{12,8},{14,10},{16,20},{18,... | collective-permute-start | bytes 417800 | tf_op jit(solution)/shard_map/ppermute | solution.py:313
  9.0 0.0 collective-permute-start.3
  9.1 0.0 copy-start.1
  9.1 0.9 %copy-done.1 = bf16[16,128,64]{1,2,0:T(8,128)(2,1)S(1)} copy-done((bf16[16,128,64]{1,2,0:T(8,128)(2,1)S(1)}, bf16[16,128,64]{1,2,0:T(8,128)(2,1)}, u32[]{:S(2)}) %copy-start.1) | copy-done | bytes 262168
  10.0 0.0 copy-start
  10.0 1.3 %own_states.1 = (bf16[16,512,128]{2,1,0:T(8,128)(2,1)S(1)}, bf16[4,136,128]{2,1,0:T(8,128)(2,1)S(1)}, bf16[2,2,64,128]{3,2,1,0:T(8,128)(2,1)S(1)}) custom-call(s32[4]{0:T(128)S(1)} %pad_add_fusion.idx_ref, bf16[2,512,128]{2,1,0:T(8,128)(2,1)S(1)} %get-tuple-element.30.k_ref, ...), custom_call_target="tpu_custom_call", output_to_operand_aliasing={{0}: (5, {})} | custom-call | flops 1000000000 | bytes 2000000 | tf_op jit(solution)/shard_map/own_states/pallas_call | solution.py:343
  11.3 0.0 copy-start.2
  11.3 0.0 copy-start.3
  11.3 0.0 copy-start.4
  11.4 4.0 %collective-permute-start = (bf16[2,2,64,128]{3,2,1,0:T(8,128)(2,1)S(1)}, bf16[2,2,64,128]{3,2,1,0:T(8,128)(2,1)S(1)}, u32[]{:S(2)}, u32[]{:S(2)}) collective-permute-start(bf16[2,2,64,128]{3,2,1,0:T(8,128)(2,1)S(1)} %get-tuple-element.34), channel_id=1, source_target_pairs={{0,2},{2,4},{4,6},{6,8},{8,10},{10,12},{12,14},{14,16},{16,18},{18... | collective-permute-start | bytes 196616 | tf_op jit(solution)/shard_map/ppermute | solution.py:316
  15.3 0.0 collective-permute-done.1.b.refs_1_
  15.4 0.3 collective-permute-done.2.c.refs_2_
  15.6 0.0 collective-permute-done.3.d.refs_3_
  15.6 0.1 totals.1._
  15.7 3.7 %collective-permute-start.6 = (bf16[4,136,128]{2,1,0:T(8,128)(2,1)S(1)}, bf16[4,136,128]{2,1,0:T(8,128)(2,1)S(1)}, u32[]{:S(2)}, u32[]{:S(2)}) collective-permute-start(bf16[4,136,128]{2,1,0:T(8,128)(2,1)S(1)} %totals.1._), channel_id=1, source_target_pairs={{0,24},{2,26},{4,28},{6,30},{8,16},{10,18},{12,20},{14,22},{16,8},... | collective-permute-start | bytes 417800 | tf_op jit(solution)/shard_map/ppermute | solution.py:313
  19.4 0.0 collective-permute-start.5
  19.4 0.8 %collective-permute-start.4 = (bf16[4,136,128]{2,1,0:T(8,128)(2,1)S(1)}, bf16[4,136,128]{2,1,0:T(8,128)(2,1)S(1)}, u32[]{:S(2)}, u32[]{:S(2)}) collective-permute-start(bf16[4,136,128]{2,1,0:T(8,128)(2,1)S(1)} %totals.1._), channel_id=1, source_target_pairs={{0,8},{2,10},{4,12},{6,14},{8,0},{10,2},{12,4},{14,6},{16,24},{18,... | collective-permute-start | bytes 417800 | tf_op jit(solution)/shard_map/ppermute | solution.py:313
  20.2 0.0 collective-permute-done.halo_ref
  20.2 0.0 copy-done
  20.2 0.4 prepare.1
  20.6 0.0 copy-done.2
  20.6 0.0 copy-done.3
  20.6 0.0 copy-done.4
  20.6 7.7 %near_0.1 = (f32[12,128,512]{2,1,0:T(8,128)S(1)}, f32[12,1,512]{2,1,0:T(1,128)S(1)}, bf16[12,128,512]{2,1,0:T(8,128)(2,1)S(1)}) custom-call(s32[4]{0:T(128)S(1)} %pad_add_fusion.idx_ref, f32[16]{0:T(128)S(1)} %copy-done.4, f32[2,4096,128]{2,1,0:T(8,128)S(1)} %get-tuple-element.39.q_wide, bf16[2,576,128]{2,1,0:T(8,128)(2,1)S(1)} %get-tuple-element.40.kx_ref, ...), custom_call_target="tpu_custom_call" | custom-call | flops 4800000000 | bytes 12000000 | tf_op jit(solution)/shard_map/near_0/pallas_call | solution.py:382
  28.3 0.0 collective-permute-done.6.refs_6_
  28.3 1.8 %collective-permute-done.5.refs_5_ = bf16[4,136,128]{2,1,0:T(8,128)(2,1)S(1)} collective-permute-done((bf16[4,136,128]{2,1,0:T(8,128)(2,1)S(1)}, bf16[4,136,128]{2,1,0:T(8,128)(2,1)S(1)}, u32[]{:S(2)}, u32[]{:S(2)}) %collective-permute-start.5) | collective-permute-done | bytes 139296 | tf_op jit(solution)/shard_map/ppermute | solution.py:313
  30.0 0.0 collective-permute-done.4.refs_4_
  30.0 0.9 %prefixes.1 = (bf16[4,136,128]{2,1,0:T(8,128)(2,1)S(1)}, bf16[4,136,128]{2,1,0:T(8,128)(2,1)S(1)}, bf16[4,136,128]{2,1,0:T(8,128)(2,1)S(1)}, bf16[4,136,128]{2,1,0:T(8,128)(2,1)S(1)}) custom-call(s32[4]{0:T(128)S(1)} %pad_add_fusion.idx_ref, bf16[4,136,128]{2,1,0:T(8,128)(2,1)S(1)} %get-tuple-element.35.a.refs_0_, ...), custom_call_target="tpu_custom_call" | custom-call | tf_op jit(solution)/shard_map/prefixes/pallas_call | solution.py:401
  31.0 1.6 %collective-permute-start.8 = (bf16[4,136,128]{2,1,0:T(8,128)(2,1)S(1)}, bf16[4,136,128]{2,1,0:T(8,128)(2,1)S(1)}, u32[]{:S(2)}, u32[]{:S(2)}) collective-permute-start(bf16[4,136,128]{2,1,0:T(8,128)(2,1)S(1)} %get-tuple-element.51), channel_id=1, source_target_pairs={{0,2},{2,0},{4,6},{6,4},{8,10},{10,8},{12,14},{14,12},{16,18},{18,... | collective-permute-start | bytes 417800 | tf_op jit(solution)/shard_map/ppermute | solution.py:313
  32.5 1.3 %collective-permute-start.9 = (bf16[4,136,128]{2,1,0:T(8,128)(2,1)S(1)}, bf16[4,136,128]{2,1,0:T(8,128)(2,1)S(1)}, u32[]{:S(2)}, u32[]{:S(2)}) collective-permute-start(bf16[4,136,128]{2,1,0:T(8,128)(2,1)S(1)} %get-tuple-element.52), channel_id=1, source_target_pairs={{0,4},{2,6},{4,0},{6,2},{8,12},{10,14},{12,8},{14,10},{16,20},{18,... | collective-permute-start | bytes 417800 | tf_op jit(solution)/shard_map/ppermute | solution.py:313
  33.8 0.7 %collective-permute-start.10 = (bf16[4,136,128]{2,1,0:T(8,128)(2,1)S(1)}, bf16[4,136,128]{2,1,0:T(8,128)(2,1)S(1)}, u32[]{:S(2)}, u32[]{:S(2)}) collective-permute-start(bf16[4,136,128]{2,1,0:T(8,128)(2,1)S(1)} %get-tuple-element.53), channel_id=1, source_target_pairs={{0,6},{2,4},{4,2},{6,0},{8,14},{10,12},{12,10},{14,8},{16,22},{18,... | collective-permute-start | bytes 417800 | tf_op jit(solution)/shard_map/ppermute | solution.py:313
  34.5 1.0 %final_own.1 = (bf16[4,256,128]{2,1,0:T(8,128)(2,1)S(1)}, bf16[4,256,128]{2,1,0:T(8,128)(2,1)S(1)}) custom-call(s32[4]{0:T(128)S(1)} %pad_add_fusion.idx_ref, f32[16]{0:T(128)S(1)} %copy-done.4, f32[12,128,512]{2,1,0:T(8,128)S(1)} %get-tuple-element.43.num.refs_0_, f32[12,1,512]{2,1,0:T(1,128)S(1)} %get-tuple-element.44.refs_7_.den.refs_1_, ...), custom_call_target="tpu_custom_call" | custom-call | flops 500000000 | bytes 2000000 | tf_op jit(solution)/shard_map/final_own/pallas_call | solution.py:418
  35.5 2.9 %near_12.1 = (f32[4,128,512]{2,1,0:T(8,128)S(1)}, f32[4,1,512]{2,1,0:T(1,128)S(1)}, bf16[4,128,512]{2,1,0:T(8,128)(2,1)S(1)}) custom-call(s32[4]{0:T(128)S(1)} %pad_add_fusion.idx_ref, f32[16]{0:T(128)S(1)} %copy-done.4, f32[2,4096,128]{2,1,0:T(8,128)S(1)} %get-tuple-element.39.q_wide, bf16[2,576,128]{2,1,0:T(8,128)(2,1)S(1)} %get-tuple-element.40.kx_ref, ...), custom_call_target="tpu_custom_call" | custom-call | flops 1600000000 | bytes 4000000 | tf_op jit(solution)/shard_map/near_12/pallas_call | solution.py:382
  38.4 0.0 collective-permute-done.8.refs_6_
  38.4 2.0 %collective-permute-done.9.refs_7_ = bf16[4,136,128]{2,1,0:T(8,128)(2,1)S(1)} collective-permute-done((bf16[4,136,128]{2,1,0:T(8,128)(2,1)S(1)}, bf16[4,136,128]{2,1,0:T(8,128)(2,1)S(1)}, u32[]{:S(2)}, u32[]{:S(2)}) %collective-permute-start.9) | collective-permute-done | bytes 139296 | tf_op jit(solution)/shard_map/ppermute | solution.py:313
  40.4 0.0 collective-permute-done.10.refs_8_
  40.4 1.1 %final_sent.1.refs_10_ = bf16[12,256,128]{2,1,0:T(8,128)(2,1)S(1)} custom-call(s32[4]{0:T(128)S(1)} %pad_add_fusion.idx_ref, f32[16]{0:T(128)S(1)} %copy-done.4, f32[12,128,512]{2,1,0:T(8,128)S(1)} %get-tuple-element.43.num.refs_0_, f32[12,1,512]{2,1,0:T(1,128)S(1)} %get-tuple-element.44.refs_7_.den.refs_1_, ...), custom_call_target="tpu_custom_call" | custom-call | tf_op jit(solution)/shard_map/final_sent/pallas_call | solution.py:428
  41.5 0.1 collective-permute-start.11
  41.6 0.5 %collective-permute-start.7 = (bf16[4,256,128]{2,1,0:T(8,128)(2,1)S(1)}, bf16[4,256,128]{2,1,0:T(8,128)(2,1)S(1)}, u32[]{:S(2)}, u32[]{:S(2)}) collective-permute-start(bf16[4,256,128]{2,1,0:T(8,128)(2,1)S(1)} %get-tuple-element.47.refs_9_), channel_id=1, source_target_pairs={{0,1},{1,0},{2,3},{3,2},{4,5},{5,4},{6,7},{7,6},{8,9},{9,8},{10,11... | collective-permute-start | bytes 786440 | tf_op jit(solution)/shard_map/ppermute | solution.py:416
  42.1 1.8 %final_kept.1._ = bf16[32,256,128]{2,1,0:T(8,128)(2,1)} custom-call(s32[4]{0:T(128)S(1)} %pad_add_fusion.idx_ref, f32[16]{0:T(128)S(1)} %copy-done.4, f32[12,128,512]{2,1,0:T(8,128)S(1)} %get-tuple-element.43.num.refs_0_, f32[12,1,512]{2,1,0:T(1,128)S(1)} %get-tuple-element.44.refs_7_.den.refs_1_, bf16[12,128,512]{2,1,0:T(8,128)(2,1)S(1)} %get-tuple-element.45.qf.refs_2_, ...), custom_call_target="tpu_custom_call" | custom-call | flops 1000000000 | bytes 5000000 | tf_op jit(solution)/shard_map/final_kept/pallas_call | solution.py:437
  44.0 0.3 collective-permute-done.7.own_ref
  44.3 0.0 collective-permute-done.11.got_ref
  44.3 1.5 %place.1 = bf16[32,256,128]{2,1,0:T(8,128)(2,1)} custom-call(s32[4]{0:T(128)S(1)} %pad_add_fusion.idx_ref, bf16[4,256,128]{2,1,0:T(8,128)(2,1)S(1)} %collective-permute-done.7.own_ref, bf16[12,256,128]{2,1,0:T(8,128)(2,1)S(1)} %collective-permute-done.11.got_ref, bf16[32,256,128]{2,1,0:T(8,128)(2,1)} %final_kept.1._), custom_call_target="tpu_custom_call", output_to_operand_aliasing={{}: (3, {})} | custom-call | tf_op jit(solution)/shard_map/place/pallas_call | solution.py:447
Async XLA Ops:
  4.5 10.8 %collective-permute-start.1 = (bf16[4,136,128]{2,1,0:T(8,128)(2,1)S(1)}, bf16[4,136,128]{2,1,0:T(8,128)(2,1)S(1)}, u32[]{:S(2)}, u32[]{:S(2)}) collective-permute-start(bf16[4,136,128]{2,1,0:T(8,128)(2,1)S(1)} %get-tuple-element.36), channel_id=1, source_target_pairs={{0,2},{2,0},{4,6},{6,4},{8,10},{10,8},{12,14},{14,12},{16,18},{18,... | collective-permute-start | bytes 417800 | tf_op jit(solution)/shard_map/ppermute | solution.py:313
  7.5 8.1 %collective-permute-start.2 = (bf16[4,136,128]{2,1,0:T(8,128)(2,1)S(1)}, bf16[4,136,128]{2,1,0:T(8,128)(2,1)S(1)}, u32[]{:S(2)}, u32[]{:S(2)}) collective-permute-start(bf16[4,136,128]{2,1,0:T(8,128)(2,1)S(1)} %get-tuple-element.37), channel_id=1, source_target_pairs={{0,4},{2,6},{4,0},{6,2},{8,12},{10,14},{12,8},{14,10},{16,20},{18,... | collective-permute-start | bytes 417800 | tf_op jit(solution)/shard_map/ppermute | solution.py:313
  9.0 6.6 %collective-permute-start.3 = (bf16[4,136,128]{2,1,0:T(8,128)(2,1)S(1)}, bf16[4,136,128]{2,1,0:T(8,128)(2,1)S(1)}, u32[]{:S(2)}, u32[]{:S(2)}) collective-permute-start(bf16[4,136,128]{2,1,0:T(8,128)(2,1)S(1)} %get-tuple-element.38), channel_id=1, source_target_pairs={{0,6},{2,4},{4,2},{6,0},{8,14},{10,12},{12,10},{14,8},{16,22},{18,... | collective-permute-start | bytes 417800 | tf_op jit(solution)/shard_map/ppermute | solution.py:313
  9.1 0.9 %copy-start.1 = (bf16[16,128,64]{1,2,0:T(8,128)(2,1)S(1)}, bf16[16,128,64]{1,2,0:T(8,128)(2,1)}, u32[]{:S(2)}) copy-start(bf16[16,128,64]{1,2,0:T(8,128)(2,1)} %param.10) | copy-start | bytes 786436
  10.0 10.2 %copy-start = (bf16[512,16,128]{2,1,0:T(8,128)(2,1)S(1)}, bf16[512,16,128]{2,1,0:T(8,128)(2,1)}, u32[]{:S(2)}) copy-start(bf16[512,16,128]{2,1,0:T(8,128)(2,1)} %q_ref.1) | copy-start | bytes 6291460
  11.3 9.3 %copy-start.2 = (bf16[16,128,64]{1,2,0:T(8,128)(2,1)S(1)}, bf16[16,128,64]{1,2,0:T(8,128)(2,1)}, u32[]{:S(2)}) copy-start(bf16[16,128,64]{1,2,0:T(8,128)(2,1)} %param.10) | copy-start | bytes 786436
  11.3 9.2 %copy-start.3 = (bf16[16,128,64]{1,2,0:T(8,128)(2,1)S(1)}, bf16[16,128,64]{1,2,0:T(8,128)(2,1)}, u32[]{:S(2)}) copy-start(bf16[16,128,64]{1,2,0:T(8,128)(2,1)} %param.9) | copy-start | bytes 786436
  11.3 9.2 %copy-start.4 = (f32[16]{0:T(128)S(1)}, f32[16]{0:T(128)}, u32[]{:S(2)}) copy-start(f32[16]{0:T(128)} %share_ref.9) | copy-start | bytes 196
  11.4 8.8 %collective-permute-start = (bf16[2,2,64,128]{3,2,1,0:T(8,128)(2,1)S(1)}, bf16[2,2,64,128]{3,2,1,0:T(8,128)(2,1)S(1)}, u32[]{:S(2)}, u32[]{:S(2)}) collective-permute-start(bf16[2,2,64,128]{3,2,1,0:T(8,128)(2,1)S(1)} %get-tuple-element.34), channel_id=1, source_target_pairs={{0,2},{2,4},{4,6},{6,8},{8,10},{10,12},{12,14},{14,16},{16,18},{18... | collective-permute-start | bytes 196616 | tf_op jit(solution)/shard_map/ppermute | solution.py:316
  15.7 12.5 %collective-permute-start.6 = (bf16[4,136,128]{2,1,0:T(8,128)(2,1)S(1)}, bf16[4,136,128]{2,1,0:T(8,128)(2,1)S(1)}, u32[]{:S(2)}, u32[]{:S(2)}) collective-permute-start(bf16[4,136,128]{2,1,0:T(8,128)(2,1)S(1)} %totals.1._), channel_id=1, source_target_pairs={{0,24},{2,26},{4,28},{6,30},{8,16},{10,18},{12,20},{14,22},{16,8},... | collective-permute-start | bytes 417800 | tf_op jit(solution)/shard_map/ppermute | solution.py:313
  19.4 10.7 %collective-permute-start.5 = (bf16[4,136,128]{2,1,0:T(8,128)(2,1)S(1)}, bf16[4,136,128]{2,1,0:T(8,128)(2,1)S(1)}, u32[]{:S(2)}, u32[]{:S(2)}) collective-permute-start(bf16[4,136,128]{2,1,0:T(8,128)(2,1)S(1)} %totals.1._), channel_id=1, source_target_pairs={{0,16},{2,18},{4,20},{6,22},{8,24},{10,26},{12,28},{14,30},{16,0},... | collective-permute-start | bytes 417800 | tf_op jit(solution)/shard_map/ppermute | solution.py:313
  19.4 10.7 %collective-permute-start.4 = (bf16[4,136,128]{2,1,0:T(8,128)(2,1)S(1)}, bf16[4,136,128]{2,1,0:T(8,128)(2,1)S(1)}, u32[]{:S(2)}, u32[]{:S(2)}) collective-permute-start(bf16[4,136,128]{2,1,0:T(8,128)(2,1)S(1)} %totals.1._), channel_id=1, source_target_pairs={{0,8},{2,10},{4,12},{6,14},{8,0},{10,2},{12,4},{14,6},{16,24},{18,... | collective-permute-start | bytes 417800 | tf_op jit(solution)/shard_map/ppermute | solution.py:313
  31.0 7.4 %collective-permute-start.8 = (bf16[4,136,128]{2,1,0:T(8,128)(2,1)S(1)}, bf16[4,136,128]{2,1,0:T(8,128)(2,1)S(1)}, u32[]{:S(2)}, u32[]{:S(2)}) collective-permute-start(bf16[4,136,128]{2,1,0:T(8,128)(2,1)S(1)} %get-tuple-element.51), channel_id=1, source_target_pairs={{0,2},{2,0},{4,6},{6,4},{8,10},{10,8},{12,14},{14,12},{16,18},{18,... | collective-permute-start | bytes 417800 | tf_op jit(solution)/shard_map/ppermute | solution.py:313
  32.5 7.9 %collective-permute-start.9 = (bf16[4,136,128]{2,1,0:T(8,128)(2,1)S(1)}, bf16[4,136,128]{2,1,0:T(8,128)(2,1)S(1)}, u32[]{:S(2)}, u32[]{:S(2)}) collective-permute-start(bf16[4,136,128]{2,1,0:T(8,128)(2,1)S(1)} %get-tuple-element.52), channel_id=1, source_target_pairs={{0,4},{2,6},{4,0},{6,2},{8,12},{10,14},{12,8},{14,10},{16,20},{18,... | collective-permute-start | bytes 417800 | tf_op jit(solution)/shard_map/ppermute | solution.py:313
  33.8 6.6 %collective-permute-start.10 = (bf16[4,136,128]{2,1,0:T(8,128)(2,1)S(1)}, bf16[4,136,128]{2,1,0:T(8,128)(2,1)S(1)}, u32[]{:S(2)}, u32[]{:S(2)}) collective-permute-start(bf16[4,136,128]{2,1,0:T(8,128)(2,1)S(1)} %get-tuple-element.53), channel_id=1, source_target_pairs={{0,6},{2,4},{4,2},{6,0},{8,14},{10,12},{12,10},{14,8},{16,22},{18,... | collective-permute-start | bytes 417800 | tf_op jit(solution)/shard_map/ppermute | solution.py:313
  41.5 2.7 %collective-permute-start.11 = (bf16[12,256,128]{2,1,0:T(8,128)(2,1)S(1)}, bf16[12,256,128]{2,1,0:T(8,128)(2,1)S(1)}, u32[]{:S(2)}, u32[]{:S(2)}) collective-permute-start(bf16[12,256,128]{2,1,0:T(8,128)(2,1)S(1)} %final_sent.1.refs_10_), channel_id=1, source_target_pairs={{0,1},{1,0},{2,3},{3,2},{4,5},{5,4},{6,7},{7,6},{8,9},{9,8},{10,11... | collective-permute-start | bytes 2359304 | tf_op jit(solution)/shard_map/ppermute | solution.py:416
  41.6 2.6 %collective-permute-start.7 = (bf16[4,256,128]{2,1,0:T(8,128)(2,1)S(1)}, bf16[4,256,128]{2,1,0:T(8,128)(2,1)S(1)}, u32[]{:S(2)}, u32[]{:S(2)}) collective-permute-start(bf16[4,256,128]{2,1,0:T(8,128)(2,1)S(1)} %get-tuple-element.47.refs_9_), channel_id=1, source_target_pairs={{0,1},{1,0},{2,3},{3,2},{4,5},{5,4},{6,7},{7,6},{8,9},{9,8},{10,11... | collective-permute-start | bytes 786440 | tf_op jit(solution)/shard_map/ppermute | solution.py:416

commit v5 on v4

--- a/solution.py
+++ b/solution.py
@@ -64,23 +64,27 @@
 
 
 def sent_states_kernel(
-    per_part, group_size, idx_ref, k_hbm, v_hbm, w_hbm, feat_ref, kg_ref, vg_ref, vt_ref, p1, p2, p3,
-    k_raw, v_raw, w_raw, sems,
+    per_part, group_size, idx_ref, k_hbm, v_hbm, w_hbm, feat_ref, kg_ref, vg_ref, vt_ref, w_raw, p1, p2, p3,
+    k_raw, v_raw, sems,
 ):
-    copies = [
-        pltpu.make_async_copy(source, target, sems.at[n])
-        for n, (source, target) in enumerate(((k_hbm, k_raw), (v_hbm, v_raw), (w_hbm, w_raw)))
-    ]
-    for copy in copies:
-        copy.start()
-    for copy in copies:
+    rows, groups, _ = k_raw.shape
+    copies = []
+    for source, target in ((k_hbm, k_raw), (w_hbm, w_raw), (v_hbm, v_raw)):
+        part = source.shape[0] // 2
+        for n in range(2):
+            at = pl.ds(n * part, part)
+            copies.append(pltpu.make_async_copy(source.at[at], target.at[at], sems.at[len(copies)]))
+            copies[-1].start()
+    for copy in copies[:2]:
         copy.wait()
-    rows, groups, _ = k_raw.shape
-    wide_k = k_raw[...].astype(F32)
-    wide_v = v_raw[...].astype(F32)
+    wide = k_raw[...].astype(F32)
     for g in range(groups):
-        kg_ref[g] = wide_k[:, g].astype(BF)
-        values = wide_v[:, g].astype(BF)
+        kg_ref[g] = wide[:, g].astype(BF)
+    for copy in copies[2:]:
+        copy.wait()
+    wide = v_raw[...].astype(F32)
+    for g in range(groups):
+        values = wide[:, g].astype(BF)
         vg_ref[g] = values
         vt_ref[g] = values_with_one(values)
     for m, out in enumerate((p1, p2, p3), 1):
@@ -319,22 +323,22 @@
     grouped = jax.ShapeDtypeStruct((groups, rows, width), BF)
     feat_shape = jax.ShapeDtypeStruct((heads, rows, width), BF)
     hbm = pl.BlockSpec(memory_space=pltpu.HBM)
-    own_feat, keys, values, values_t, *pieces = pl.pallas_call(
+    own_feat, keys, values, values_t, key_map, *pieces = pl.pallas_call(
         functools.partial(sent_states_kernel, per_part, group_size),
         in_specs=[smem] + [hbm] * 3,
-        out_specs=[vmem] * (4 + PART - 1),
+        out_specs=[vmem] * (5 + PART - 1),
         out_shape=[
             feat_shape,
             grouped,
             grouped,
             jax.ShapeDtypeStruct((groups, tall, rows), BF),
+            jax.ShapeDtypeStruct(key_map.shape, BF),
         ]
         + [piece_shape] * (PART - 1),
         scratch_shapes=[
             pltpu.VMEM((rows, groups, width), BF),
             pltpu.VMEM((rows, groups, width), BF),
-            pltpu.VMEM(key_map.shape, BF),
-            pltpu.SemaphoreType.DMA((3,)),
+            pltpu.SemaphoreType.DMA((6,)),
         ],
         compiler_params=params,
         name="sent_states",

time: 46 us -> 45.4 us (0.987)
  local copies, waits for them, and re-layouts: 0.97 us -> 0.02 us
  waiting for transfers between devices: 4.41 us -> 4.99 us
    unnamed x10 -> x6, local copies, waits for them, and re-layouts: 0.97 us -> 0.02 us
    ppermute x9, waiting for transfers between devices: 4.1 us -> 4.67 us  [xor(): return lax.ppermute(x, 'seq', [(i, i ^ m) for i in range(devices)])]
where the time goes in v5:
time: 45.4 us; the launch traced here: 45.2 us
  Pallas kernels  22.9 us (50%)
  starting transfers between devices  17.1 us (38%)
  waiting for transfers between devices  4.99 us (11%)
    ppermute x9, starting transfers between devices, xor(): return lax.ppermute(x, 'seq', [(i, i ^ m) for i in range(devices)])  12.6 us
    pallas_call x2, Pallas kernels, near(): pl.pallas_call(functools.partial(near_kernel, group_size, per_part, first...  10.5 us
    ppermute x9, waiting for transfers between devices, xor(): return lax.ppermute(x, 'seq', [(i, i ^ m) for i in range(devices)])  4.67 us
    pallas_call x1, Pallas kernels, per_device(): pl.pallas_call(functools.partial(sent_states_kernel, per_part, group_size...  4.22 us
    ppermute x1, starting transfers between devices, shift(): return lax.ppermute(x, 'seq', [(i, i + by) for i in range(devices - by)])  3.99 us
    pallas_call x1, Pallas kernels, per_device(): pl.pallas_call(functools.partial(final_kept_kernel, per_part, half), in_s...  1.83 us
    pallas_call x1, Pallas kernels, per_device(): pl.pallas_call(functools.partial(place_kernel, per_part), in_specs=[smem,...  1.54 us
    pallas_call x1, Pallas kernels, per_device(): pl.pallas_call(functools.partial(own_states_kernel, per_part, group_size)...  1.3 us
  transfers between devices with their start and end apart: 12, of which 4 were waited for; matrix products, arithmetic and copies ran while one was open for 0% of the time, Pallas kernels for 33%

profile of v5, /device:TPU:0, one launch (start us, length us, event | category | flops | bytes accessed | tf_op | source)
XLA Modules:
  0.0 45.2 jit_solution(5097886177263619611)
XLA Ops:
  0.0 0.1 pad_add_fusion.idx_ref
  0.1 4.2 %sent_states.1 = (bf16[16,512,128]{2,1,0:T(8,128)(2,1)S(1)}, bf16[2,512,128]{2,1,0:T(8,128)(2,1)S(1)}, bf16[2,512,128]{2,1,0:T(8,128)(2,1)S(1)}, bf16[2,136,512]...) custom-call(s32[4]{0:T(128)S(1)} %pad_add_fusion.idx_ref, ...), custom_call_target="tpu_custom_call" | custom-call | tf_op jit(solution)/shard_map/sent_states/pallas_call | solution.py:326
  4.3 3.0 %collective-permute-start.1 = (bf16[4,136,128]{2,1,0:T(8,128)(2,1)S(1)}, bf16[4,136,128]{2,1,0:T(8,128)(2,1)S(1)}, u32[]{:S(2)}, u32[]{:S(2)}) collective-permute-start(bf16[4,136,128]{2,1,0:T(8,128)(2,1)S(1)} %get-tuple-element.38), channel_id=1, source_target_pairs={{0,2},{2,0},{4,6},{6,4},{8,10},{10,8},{12,14},{14,12},{16,18},{18,... | collective-permute-start | bytes 417800 | tf_op jit(solution)/shard_map/ppermute | solution.py:317
  7.3 1.5 %collective-permute-start.2 = (bf16[4,136,128]{2,1,0:T(8,128)(2,1)S(1)}, bf16[4,136,128]{2,1,0:T(8,128)(2,1)S(1)}, u32[]{:S(2)}, u32[]{:S(2)}) collective-permute-start(bf16[4,136,128]{2,1,0:T(8,128)(2,1)S(1)} %get-tuple-element.39), channel_id=1, source_target_pairs={{0,4},{2,6},{4,0},{6,2},{8,12},{10,14},{12,8},{14,10},{16,20},{18,... | collective-permute-start | bytes 417800 | tf_op jit(solution)/shard_map/ppermute | solution.py:317
  8.8 0.0 collective-permute-start.3
  8.9 0.0 copy-start
  8.9 1.3 %own_states.1 = (bf16[16,512,128]{2,1,0:T(8,128)(2,1)S(1)}, bf16[4,136,128]{2,1,0:T(8,128)(2,1)S(1)}, bf16[2,2,64,128]{3,2,1,0:T(8,128)(2,1)S(1)}) custom-call(s32[4]{0:T(128)S(1)} %pad_add_fusion.idx_ref, bf16[2,512,128]{2,1,0:T(8,128)(2,1)S(1)} %get-tuple-element.31.k_ref, ...), custom_call_target="tpu_custom_call", output_to_operand_aliasing={{0}: (5, {})} | custom-call | flops 1000000000 | bytes 2000000 | tf_op jit(solution)/shard_map/own_states/pallas_call | solution.py:347
  10.2 0.0 copy-start.1
  10.2 0.0 copy-start.2
  10.2 4.0 %collective-permute-start = (bf16[2,2,64,128]{3,2,1,0:T(8,128)(2,1)S(1)}, bf16[2,2,64,128]{3,2,1,0:T(8,128)(2,1)S(1)}, u32[]{:S(2)}, u32[]{:S(2)}) collective-permute-start(bf16[2,2,64,128]{3,2,1,0:T(8,128)(2,1)S(1)} %get-tuple-element.36), channel_id=1, source_target_pairs={{0,2},{2,4},{4,6},{6,8},{8,10},{10,12},{12,14},{14,16},{16,18},{18... | collective-permute-start | bytes 196616 | tf_op jit(solution)/shard_map/ppermute | solution.py:320
  14.2 0.0 collective-permute-done.1.b.refs_1_
  14.2 1.2 %collective-permute-done.2.c.refs_2_ = bf16[4,136,128]{2,1,0:T(8,128)(2,1)S(1)} collective-permute-done((bf16[4,136,128]{2,1,0:T(8,128)(2,1)S(1)}, bf16[4,136,128]{2,1,0:T(8,128)(2,1)S(1)}, u32[]{:S(2)}, u32[]{:S(2)}) %collective-permute-start.2) | collective-permute-done | bytes 139296 | tf_op jit(solution)/shard_map/ppermute | solution.py:317
  15.4 0.0 collective-permute-done.3.d.refs_3_
  15.4 0.1 totals.1._
  15.5 3.7 %collective-permute-start.6 = (bf16[4,136,128]{2,1,0:T(8,128)(2,1)S(1)}, bf16[4,136,128]{2,1,0:T(8,128)(2,1)S(1)}, u32[]{:S(2)}, u32[]{:S(2)}) collective-permute-start(bf16[4,136,128]{2,1,0:T(8,128)(2,1)S(1)} %totals.1._), channel_id=1, source_target_pairs={{0,24},{2,26},{4,28},{6,30},{8,16},{10,18},{12,20},{14,22},{16,8},... | collective-permute-start | bytes 417800 | tf_op jit(solution)/shard_map/ppermute | solution.py:317
  19.2 0.0 collective-permute-start.5
  19.2 0.8 %collective-permute-start.4 = (bf16[4,136,128]{2,1,0:T(8,128)(2,1)S(1)}, bf16[4,136,128]{2,1,0:T(8,128)(2,1)S(1)}, u32[]{:S(2)}, u32[]{:S(2)}) collective-permute-start(bf16[4,136,128]{2,1,0:T(8,128)(2,1)S(1)} %totals.1._), channel_id=1, source_target_pairs={{0,8},{2,10},{4,12},{6,14},{8,0},{10,2},{12,4},{14,6},{16,24},{18,... | collective-permute-start | bytes 417800 | tf_op jit(solution)/shard_map/ppermute | solution.py:317
  20.0 0.0 collective-permute-done.halo_ref
  20.0 0.0 copy-done
  20.0 0.4 prepare.1
  20.4 0.0 copy-done.1
  20.4 0.0 copy-done.2
  20.4 7.7 %near_0.1 = (f32[12,128,512]{2,1,0:T(8,128)S(1)}, f32[12,1,512]{2,1,0:T(1,128)S(1)}, bf16[12,128,512]{2,1,0:T(8,128)(2,1)S(1)}) custom-call(s32[4]{0:T(128)S(1)} %pad_add_fusion.idx_ref, f32[16]{0:T(128)S(1)} %copy-done.2, f32[2,4096,128]{2,1,0:T(8,128)S(1)} %get-tuple-element.41.q_wide, bf16[2,576,128]{2,1,0:T(8,128)(2,1)S(1)} %get-tuple-element.42.kx_ref, ...), custom_call_target="tpu_custom_call" | custom-call | flops 4800000000 | bytes 12000000 | tf_op jit(solution)/shard_map/near_0/pallas_call | solution.py:386
  28.0 0.0 collective-permute-done.6.refs_6_
  28.1 1.8 %collective-permute-done.5.refs_5_ = bf16[4,136,128]{2,1,0:T(8,128)(2,1)S(1)} collective-permute-done((bf16[4,136,128]{2,1,0:T(8,128)(2,1)S(1)}, bf16[4,136,128]{2,1,0:T(8,128)(2,1)S(1)}, u32[]{:S(2)}, u32[]{:S(2)}) %collective-permute-start.5) | collective-permute-done | bytes 139296 | tf_op jit(solution)/shard_map/ppermute | solution.py:317
  29.8 0.0 collective-permute-done.4.refs_4_
  29.9 0.9 %prefixes.1 = (bf16[4,136,128]{2,1,0:T(8,128)(2,1)S(1)}, bf16[4,136,128]{2,1,0:T(8,128)(2,1)S(1)}, bf16[4,136,128]{2,1,0:T(8,128)(2,1)S(1)}, bf16[4,136,128]{2,1,0:T(8,128)(2,1)S(1)}) custom-call(s32[4]{0:T(128)S(1)} %pad_add_fusion.idx_ref, bf16[4,136,128]{2,1,0:T(8,128)(2,1)S(1)} %get-tuple-element.37.a.refs_0_, ...), custom_call_target="tpu_custom_call" | custom-call | tf_op jit(solution)/shard_map/prefixes/pallas_call | solution.py:405
  30.8 1.5 %collective-permute-start.8 = (bf16[4,136,128]{2,1,0:T(8,128)(2,1)S(1)}, bf16[4,136,128]{2,1,0:T(8,128)(2,1)S(1)}, u32[]{:S(2)}, u32[]{:S(2)}) collective-permute-start(bf16[4,136,128]{2,1,0:T(8,128)(2,1)S(1)} %get-tuple-element.53), channel_id=1, source_target_pairs={{0,2},{2,0},{4,6},{6,4},{8,10},{10,8},{12,14},{14,12},{16,18},{18,... | collective-permute-start | bytes 417800 | tf_op jit(solution)/shard_map/ppermute | solution.py:317
  32.3 0.5 %collective-permute-start.9 = (bf16[4,136,128]{2,1,0:T(8,128)(2,1)S(1)}, bf16[4,136,128]{2,1,0:T(8,128)(2,1)S(1)}, u32[]{:S(2)}, u32[]{:S(2)}) collective-permute-start(bf16[4,136,128]{2,1,0:T(8,128)(2,1)S(1)} %get-tuple-element.54), channel_id=1, source_target_pairs={{0,4},{2,6},{4,0},{6,2},{8,12},{10,14},{12,8},{14,10},{16,20},{18,... | collective-permute-start | bytes 417800 | tf_op jit(solution)/shard_map/ppermute | solution.py:317
  32.8 1.5 %collective-permute-start.10 = (bf16[4,136,128]{2,1,0:T(8,128)(2,1)S(1)}, bf16[4,136,128]{2,1,0:T(8,128)(2,1)S(1)}, u32[]{:S(2)}, u32[]{:S(2)}) collective-permute-start(bf16[4,136,128]{2,1,0:T(8,128)(2,1)S(1)} %get-tuple-element.55), channel_id=1, source_target_pairs={{0,6},{2,4},{4,2},{6,0},{8,14},{10,12},{12,10},{14,8},{16,22},{18,... | collective-permute-start | bytes 417800 | tf_op jit(solution)/shard_map/ppermute | solution.py:317
  34.3 1.0 %final_own.1 = (bf16[4,256,128]{2,1,0:T(8,128)(2,1)S(1)}, bf16[4,256,128]{2,1,0:T(8,128)(2,1)S(1)}) custom-call(s32[4]{0:T(128)S(1)} %pad_add_fusion.idx_ref, f32[16]{0:T(128)S(1)} %copy-done.2, f32[12,128,512]{2,1,0:T(8,128)S(1)} %get-tuple-element.45.num.refs_0_, f32[12,1,512]{2,1,0:T(1,128)S(1)} %get-tuple-element.46.refs_7_.den.refs_1_, ...), custom_call_target="tpu_custom_call" | custom-call | flops 500000000 | bytes 2000000 | tf_op jit(solution)/shard_map/final_own/pallas_call | solution.py:422
  35.3 2.9 %near_12.1 = (f32[4,128,512]{2,1,0:T(8,128)S(1)}, f32[4,1,512]{2,1,0:T(1,128)S(1)}, bf16[4,128,512]{2,1,0:T(8,128)(2,1)S(1)}) custom-call(s32[4]{0:T(128)S(1)} %pad_add_fusion.idx_ref, f32[16]{0:T(128)S(1)} %copy-done.2, f32[2,4096,128]{2,1,0:T(8,128)S(1)} %get-tuple-element.41.q_wide, bf16[2,576,128]{2,1,0:T(8,128)(2,1)S(1)} %get-tuple-element.42.kx_ref, ...), custom_call_target="tpu_custom_call" | custom-call | flops 1600000000 | bytes 4000000 | tf_op jit(solution)/shard_map/near_12/pallas_call | solution.py:386
  38.2 0.0 collective-permute-done.8.refs_6_
  38.2 1.6 %collective-permute-done.9.refs_7_ = bf16[4,136,128]{2,1,0:T(8,128)(2,1)S(1)} collective-permute-done((bf16[4,136,128]{2,1,0:T(8,128)(2,1)S(1)}, bf16[4,136,128]{2,1,0:T(8,128)(2,1)S(1)}, u32[]{:S(2)}, u32[]{:S(2)}) %collective-permute-start.9) | collective-permute-done | bytes 139296 | tf_op jit(solution)/shard_map/ppermute | solution.py:317
  39.8 0.0 collective-permute-done.10.refs_8_
  39.9 1.1 %final_sent.1.refs_10_ = bf16[12,256,128]{2,1,0:T(8,128)(2,1)S(1)} custom-call(s32[4]{0:T(128)S(1)} %pad_add_fusion.idx_ref, f32[16]{0:T(128)S(1)} %copy-done.2, f32[12,128,512]{2,1,0:T(8,128)S(1)} %get-tuple-element.45.num.refs_0_, f32[12,1,512]{2,1,0:T(1,128)S(1)} %get-tuple-element.46.refs_7_.den.refs_1_, ...), custom_call_target="tpu_custom_call" | custom-call | tf_op jit(solution)/shard_map/final_sent/pallas_call | solution.py:432
  40.9 0.1 collective-permute-start.11
  41.0 0.5 %collective-permute-start.7 = (bf16[4,256,128]{2,1,0:T(8,128)(2,1)S(1)}, bf16[4,256,128]{2,1,0:T(8,128)(2,1)S(1)}, u32[]{:S(2)}, u32[]{:S(2)}) collective-permute-start(bf16[4,256,128]{2,1,0:T(8,128)(2,1)S(1)} %get-tuple-element.49.refs_9_), channel_id=1, source_target_pairs={{0,1},{1,0},{2,3},{3,2},{4,5},{5,4},{6,7},{7,6},{8,9},{9,8},{10,11... | collective-permute-start | bytes 786440 | tf_op jit(solution)/shard_map/ppermute | solution.py:420
  41.5 1.8 %final_kept.1._ = bf16[32,256,128]{2,1,0:T(8,128)(2,1)} custom-call(s32[4]{0:T(128)S(1)} %pad_add_fusion.idx_ref, f32[16]{0:T(128)S(1)} %copy-done.2, f32[12,128,512]{2,1,0:T(8,128)S(1)} %get-tuple-element.45.num.refs_0_, f32[12,1,512]{2,1,0:T(1,128)S(1)} %get-tuple-element.46.refs_7_.den.refs_1_, bf16[12,128,512]{2,1,0:T(8,128)(2,1)S(1)} %get-tuple-element.47.qf.refs_2_, ...), custom_call_target="tpu_custom_call" | custom-call | flops 1000000000 | bytes 5000000 | tf_op jit(solution)/shard_map/final_kept/pallas_call | solution.py:441
  43.4 0.3 collective-permute-done.7.own_ref
  43.7 0.0 collective-permute-done.11.got_ref
  43.7 1.5 %place.1 = bf16[32,256,128]{2,1,0:T(8,128)(2,1)} custom-call(s32[4]{0:T(128)S(1)} %pad_add_fusion.idx_ref, bf16[4,256,128]{2,1,0:T(8,128)(2,1)S(1)} %collective-permute-done.7.own_ref, bf16[12,256,128]{2,1,0:T(8,128)(2,1)S(1)} %collective-permute-done.11.got_ref, bf16[32,256,128]{2,1,0:T(8,128)(2,1)} %final_kept.1._), custom_call_target="tpu_custom_call", output_to_operand_aliasing={{}: (3, {})} | custom-call | tf_op jit(solution)/shard_map/place/pallas_call | solution.py:451
Async XLA Ops:
  4.3 9.9 %collective-permute-start.1 = (bf16[4,136,128]{2,1,0:T(8,128)(2,1)S(1)}, bf16[4,136,128]{2,1,0:T(8,128)(2,1)S(1)}, u32[]{:S(2)}, u32[]{:S(2)}) collective-permute-start(bf16[4,136,128]{2,1,0:T(8,128)(2,1)S(1)} %get-tuple-element.38), channel_id=1, source_target_pairs={{0,2},{2,0},{4,6},{6,4},{8,10},{10,8},{12,14},{14,12},{16,18},{18,... | collective-permute-start | bytes 417800 | tf_op jit(solution)/shard_map/ppermute | solution.py:317
  7.3 8.1 %collective-permute-start.2 = (bf16[4,136,128]{2,1,0:T(8,128)(2,1)S(1)}, bf16[4,136,128]{2,1,0:T(8,128)(2,1)S(1)}, u32[]{:S(2)}, u32[]{:S(2)}) collective-permute-start(bf16[4,136,128]{2,1,0:T(8,128)(2,1)S(1)} %get-tuple-element.39), channel_id=1, source_target_pairs={{0,4},{2,6},{4,0},{6,2},{8,12},{10,14},{12,8},{14,10},{16,20},{18,... | collective-permute-start | bytes 417800 | tf_op jit(solution)/shard_map/ppermute | solution.py:317
  8.8 6.6 %collective-permute-start.3 = (bf16[4,136,128]{2,1,0:T(8,128)(2,1)S(1)}, bf16[4,136,128]{2,1,0:T(8,128)(2,1)S(1)}, u32[]{:S(2)}, u32[]{:S(2)}) collective-permute-start(bf16[4,136,128]{2,1,0:T(8,128)(2,1)S(1)} %get-tuple-element.40), channel_id=1, source_target_pairs={{0,6},{2,4},{4,2},{6,0},{8,14},{10,12},{12,10},{14,8},{16,22},{18,... | collective-permute-start | bytes 417800 | tf_op jit(solution)/shard_map/ppermute | solution.py:317
  8.9 11.1 %copy-start = (bf16[512,16,128]{2,1,0:T(8,128)(2,1)S(1)}, bf16[512,16,128]{2,1,0:T(8,128)(2,1)}, u32[]{:S(2)}) copy-start(bf16[512,16,128]{2,1,0:T(8,128)(2,1)} %q_ref.1) | copy-start | bytes 6291460
  10.2 10.2 %copy-start.1 = (bf16[16,128,64]{1,2,0:T(8,128)(2,1)S(1)}, bf16[16,128,64]{1,2,0:T(8,128)(2,1)}, u32[]{:S(2)}) copy-start(bf16[16,128,64]{1,2,0:T(8,128)(2,1)} %param.9) | copy-start | bytes 786436
  10.2 10.2 %copy-start.2 = (f32[16]{0:T(128)S(1)}, f32[16]{0:T(128)}, u32[]{:S(2)}) copy-start(f32[16]{0:T(128)} %share_ref.9) | copy-start | bytes 196
  10.2 9.8 %collective-permute-start = (bf16[2,2,64,128]{3,2,1,0:T(8,128)(2,1)S(1)}, bf16[2,2,64,128]{3,2,1,0:T(8,128)(2,1)S(1)}, u32[]{:S(2)}, u32[]{:S(2)}) collective-permute-start(bf16[2,2,64,128]{3,2,1,0:T(8,128)(2,1)S(1)} %get-tuple-element.36), channel_id=1, source_target_pairs={{0,2},{2,4},{4,6},{6,8},{8,10},{10,12},{12,14},{14,16},{16,18},{18... | collective-permute-start | bytes 196616 | tf_op jit(solution)/shard_map/ppermute | solution.py:320
  15.5 12.5 %collective-permute-start.6 = (bf16[4,136,128]{2,1,0:T(8,128)(2,1)S(1)}, bf16[4,136,128]{2,1,0:T(8,128)(2,1)S(1)}, u32[]{:S(2)}, u32[]{:S(2)}) collective-permute-start(bf16[4,136,128]{2,1,0:T(8,128)(2,1)S(1)} %totals.1._), channel_id=1, source_target_pairs={{0,24},{2,26},{4,28},{6,30},{8,16},{10,18},{12,20},{14,22},{16,8},... | collective-permute-start | bytes 417800 | tf_op jit(solution)/shard_map/ppermute | solution.py:317
  19.2 10.7 %collective-permute-start.5 = (bf16[4,136,128]{2,1,0:T(8,128)(2,1)S(1)}, bf16[4,136,128]{2,1,0:T(8,128)(2,1)S(1)}, u32[]{:S(2)}, u32[]{:S(2)}) collective-permute-start(bf16[4,136,128]{2,1,0:T(8,128)(2,1)S(1)} %totals.1._), channel_id=1, source_target_pairs={{0,16},{2,18},{4,20},{6,22},{8,24},{10,26},{12,28},{14,30},{16,0},... | collective-permute-start | bytes 417800 | tf_op jit(solution)/shard_map/ppermute | solution.py:317
  19.2 10.7 %collective-permute-start.4 = (bf16[4,136,128]{2,1,0:T(8,128)(2,1)S(1)}, bf16[4,136,128]{2,1,0:T(8,128)(2,1)S(1)}, u32[]{:S(2)}, u32[]{:S(2)}) collective-permute-start(bf16[4,136,128]{2,1,0:T(8,128)(2,1)S(1)} %totals.1._), channel_id=1, source_target_pairs={{0,8},{2,10},{4,12},{6,14},{8,0},{10,2},{12,4},{14,6},{16,24},{18,... | collective-permute-start | bytes 417800 | tf_op jit(solution)/shard_map/ppermute | solution.py:317
  30.8 7.4 %collective-permute-start.8 = (bf16[4,136,128]{2,1,0:T(8,128)(2,1)S(1)}, bf16[4,136,128]{2,1,0:T(8,128)(2,1)S(1)}, u32[]{:S(2)}, u32[]{:S(2)}) collective-permute-start(bf16[4,136,128]{2,1,0:T(8,128)(2,1)S(1)} %get-tuple-element.53), channel_id=1, source_target_pairs={{0,2},{2,0},{4,6},{6,4},{8,10},{10,8},{12,14},{14,12},{16,18},{18,... | collective-permute-start | bytes 417800 | tf_op jit(solution)/shard_map/ppermute | solution.py:317
  32.3 7.5 %collective-permute-start.9 = (bf16[4,136,128]{2,1,0:T(8,128)(2,1)S(1)}, bf16[4,136,128]{2,1,0:T(8,128)(2,1)S(1)}, u32[]{:S(2)}, u32[]{:S(2)}) collective-permute-start(bf16[4,136,128]{2,1,0:T(8,128)(2,1)S(1)} %get-tuple-element.54), channel_id=1, source_target_pairs={{0,4},{2,6},{4,0},{6,2},{8,12},{10,14},{12,8},{14,10},{16,20},{18,... | collective-permute-start | bytes 417800 | tf_op jit(solution)/shard_map/ppermute | solution.py:317
  32.8 7.0 %collective-permute-start.10 = (bf16[4,136,128]{2,1,0:T(8,128)(2,1)S(1)}, bf16[4,136,128]{2,1,0:T(8,128)(2,1)S(1)}, u32[]{:S(2)}, u32[]{:S(2)}) collective-permute-start(bf16[4,136,128]{2,1,0:T(8,128)(2,1)S(1)} %get-tuple-element.55), channel_id=1, source_target_pairs={{0,6},{2,4},{4,2},{6,0},{8,14},{10,12},{12,10},{14,8},{16,22},{18,... | collective-permute-start | bytes 417800 | tf_op jit(solution)/shard_map/ppermute | solution.py:317
  40.9 2.7 %collective-permute-start.11 = (bf16[12,256,128]{2,1,0:T(8,128)(2,1)S(1)}, bf16[12,256,128]{2,1,0:T(8,128)(2,1)S(1)}, u32[]{:S(2)}, u32[]{:S(2)}) collective-permute-start(bf16[12,256,128]{2,1,0:T(8,128)(2,1)S(1)} %final_sent.1.refs_10_), channel_id=1, source_target_pairs={{0,1},{1,0},{2,3},{3,2},{4,5},{5,4},{6,7},{7,6},{8,9},{9,8},{10,11... | collective-permute-start | bytes 2359304 | tf_op jit(solution)/shard_map/ppermute | solution.py:420
  41.0 2.6 %collective-permute-start.7 = (bf16[4,256,128]{2,1,0:T(8,128)(2,1)S(1)}, bf16[4,256,128]{2,1,0:T(8,128)(2,1)S(1)}, u32[]{:S(2)}, u32[]{:S(2)}) collective-permute-start(bf16[4,256,128]{2,1,0:T(8,128)(2,1)S(1)} %get-tuple-element.49.refs_9_), channel_id=1, source_target_pairs={{0,1},{1,0},{2,3},{3,2},{4,5},{5,4},{6,7},{7,6},{8,9},{9,8},{10,11... | collective-permute-start | bytes 786440 | tf_op jit(solution)/shard_map/ppermute | solution.py:420

commit v6 on v5

--- a/solution.py
+++ b/solution.py
@@ -14,7 +14,7 @@
 F32 = jnp.float32
 LIMIT = 16 * 1024 * 1024
 STEP = 4
-SPLIT = 12
+SPLIT = (4, 12)
 
 
 def mm(a, b, ca=1, cb=0):
@@ -102,6 +102,12 @@
     for e in range(out.shape[0]):
         states, norms = zip(*(get_state(ref, e) for ref in (a, b, c, d)))
         put_state(out, e, sum(states[1:], states[0]), sum(norms[1:], norms[0]))
+
+
+def sum_kernel(a, b, _, out):
+    for e in range(out.shape[0]):
+        state, norm = zip(get_state(a, e), get_state(b, e))
+        put_state(out, e, state[0] + state[1], norm[0] + norm[1])
 
 
 def prefix_kernel(zs, exchanged, idx_ref, *refs):
@@ -257,15 +263,15 @@
 
 
 def final_sent_kernel(per_part, half, idx_ref, share_ref, *refs):
-    held, pieces, out_ref = (refs[:3], refs[3:6]), refs[6 : 5 + PART], refs[-1]
+    held, pieces, out_ref = [refs[k : k + 3] for k in range(0, 9, 3)], refs[9 : 8 + PART], refs[-1]
     for m, e, rows in finished(per_part, 3, half, 1, idx_ref, share_ref, held, pieces):
         out_ref[(m - 1) * per_part + e] = rows
 
 
 def final_kept_kernel(per_part, half, idx_ref, share_ref, *refs):
-    held, pieces = (refs[:3], refs[3:6]), refs[6 : 5 + PART]
+    held, pieces, kept_own = [refs[k : k + 3] for k in range(0, 9, 3)], refs[9 : 8 + PART], refs[8 + PART]
     out_ref, kept, sems = refs[-3:]
-    copies = [pltpu.make_async_copy(refs[5 + PART], out_ref.at[quarter_at(2, 0, per_part, idx_ref)], sems.at[0])]
+    copies = [pltpu.make_async_copy(kept_own, out_ref.at[quarter_at(2, 0, per_part, idx_ref)], sems.at[0])]
     copies[0].start()
     for m, e, rows in finished(per_part, 2, half, 1, idx_ref, share_ref, held, pieces):
         kept[m - 1, e] = rows
@@ -361,7 +367,7 @@
     )(*pieces)
     exchanged = zs in (1, 2, 4)
     if exchanged:
-        earlier = [xor(total, PART * k) for k in range(1, zs)]
+        earlier = [xor(total, PART * k) for k in range(1, min(zs, 2))]
     else:
         columns = [[z * PART + k for z in range(zs)] for k in range(PART)]
         gathered = lax.all_gather(total, "seq", axis_index_groups=columns)
@@ -401,7 +407,20 @@
             name="near_%d" % first,
         )(idx, window_param, q_wide, keys, values, own_feat, query_map, key_map, *after)
 
-    held = list(near(0, SPLIT, []))
+    held = list(near(0, SPLIT[0], []))
+    if zs == 4:
+        pair = pl.pallas_call(
+            sum_kernel,
+            in_specs=[vmem] * 2 + [anywhere],
+            out_specs=vmem,
+            out_shape=piece_shape,
+            compiler_params=params,
+            name="layer_sum",
+        )(total, earlier[0], held[1])
+        earlier.append(xor(pair, 2 * PART))
+        held += near(SPLIT[0], SPLIT[1] - SPLIT[0], [pair])
+    else:
+        held += near(SPLIT[0], SPLIT[1] - SPLIT[0], [])
     prefixes = pl.pallas_call(
         functools.partial(prefix_kernel, len(earlier), exchanged),
         in_specs=[smem] + [vmem] * (PART + len(earlier)) + [anywhere],
@@ -409,9 +428,9 @@
         out_shape=[piece_shape] * PART,
         compiler_params=params,
         name="prefixes",
-    )(idx, *pieces, *earlier, held[1])
+    )(idx, *pieces, *earlier, held[4])
     prior = [prefixes[0]] + [xor(prefixes[m], m) for m in range(1, PART)]
-    held += near(SPLIT, heads - SPLIT, [prefixes[0]])
+    held += near(SPLIT[1], heads - SPLIT[1], [prefixes[0]])
 
     half = rows // 2
     out_shape = jax.ShapeDtypeStruct((2 * heads, half, width), BF)
@@ -431,7 +450,7 @@
     got_own = swapped(sent_own)
     sent = pl.pallas_call(
         functools.partial(final_sent_kernel, per_part, half),
-        in_specs=[smem, smem] + [vmem] * (5 + PART) + [anywhere],
+        in_specs=[smem, smem] + [vmem] * (8 + PART) + [anywhere],
         out_specs=vmem,
         out_shape=jax.ShapeDtypeStruct((heads - per_part, half, width), BF),
         compiler_params=params,
@@ -440,7 +459,7 @@
     got = swapped(sent)
     out = pl.pallas_call(
         functools.partial(final_kept_kernel, per_part, half),
-        in_specs=[smem, smem] + [vmem] * (6 + PART) + [anywhere],
+        in_specs=[smem, smem] + [vmem] * (9 + PART) + [anywhere],
         out_specs=hbm,
         out_shape=out_shape,
         scratch_shapes=[pltpu.VMEM((PART - 1, per_part, half, width), BF), pltpu.SemaphoreType.DMA((PART,))],

time: 45.4 us -> 44.1 us (0.971)
  waiting for transfers between devices: 4.99 us -> 1.55 us
  starting transfers between devices: 17.1 us -> 18.5 us
  Pallas kernels: 22.9 us -> 23.5 us
    ppermute x9 -> x8, waiting for transfers between devices: 4.67 us -> 1.24 us  [xor(): return lax.ppermute(x, 'seq', [(i, i ^ m) for i in range(devices)])]
    ppermute x9 -> x8, starting transfers between devices: 12.6 us -> 13.8 us  [xor(): return lax.ppermute(x, 'seq', [(i, i ^ m) for i in range(devices)])]
    pallas_call x2 -> x3, Pallas kernels: 10.5 us -> 11.1 us  [near(): pl.pallas_call(functools.partial(near_kernel, group_size, per_part, first...]
  transfers between devices with their start and end apart: 12 -> 11, of which waited for: 4 -> 3; matrix products, arithmetic and copies ran while one was open for 0% -> 0% of each run, Pallas kernels for 33% -> 36%
where the time goes in v6:
time: 44.1 us; the launch traced here: 44 us
  Pallas kernels  23.5 us (53%)
  starting transfers between devices  18.5 us (42%)
  waiting for transfers between devices  1.55 us (4%)
    ppermute x8, starting transfers between devices, xor(): return lax.ppermute(x, 'seq', [(i, i ^ m) for i in range(devices)])  13.8 us
    pallas_call x3, Pallas kernels, near(): pl.pallas_call(functools.partial(near_kernel, group_size, per_part, first...  11.1 us
    pallas_call x1, Pallas kernels, per_device(): pl.pallas_call(functools.partial(sent_states_kernel, per_part, group_size...  4.22 us
    ppermute x1, starting transfers between devices, shift(): return lax.ppermute(x, 'seq', [(i, i + by) for i in range(devices - by)])  4.17 us
    pallas_call x1, Pallas kernels, per_device(): pl.pallas_call(functools.partial(final_kept_kernel, per_part, half), in_s...  1.84 us
    pallas_call x1, Pallas kernels, per_device(): pl.pallas_call(functools.partial(place_kernel, per_part), in_specs=[smem,...  1.54 us
    pallas_call x1, Pallas kernels, per_device(): pl.pallas_call(functools.partial(own_states_kernel, per_part, group_size)...  1.3 us
    ppermute x8, waiting for transfers between devices, xor(): return lax.ppermute(x, 'seq', [(i, i ^ m) for i in range(devices)])  1.24 us
  transfers between devices with their start and end apart: 11, of which 3 were waited for; matrix products, arithmetic and copies ran while one was open for 0% of the time, Pallas kernels for 36%

profile of v6, /device:TPU:0, one launch (start us, length us, event | category | flops | bytes accessed | tf_op | source)
XLA Modules:
  0.0 44.0 jit_solution(17053968068537164534)
XLA Ops:
  0.0 0.1 pad_add_fusion.idx_ref
  0.1 4.2 %sent_states.1 = (bf16[16,512,128]{2,1,0:T(8,128)(2,1)S(1)}, bf16[2,512,128]{2,1,0:T(8,128)(2,1)S(1)}, bf16[2,512,128]{2,1,0:T(8,128)(2,1)S(1)}, bf16[2,136,512]...) custom-call(s32[4]{0:T(128)S(1)} %pad_add_fusion.idx_ref, ...), custom_call_target="tpu_custom_call" | custom-call | tf_op jit(solution)/shard_map/sent_states/pallas_call | solution.py:332
  4.3 3.0 %collective-permute-start.1 = (bf16[4,136,128]{2,1,0:T(8,128)(2,1)S(1)}, bf16[4,136,128]{2,1,0:T(8,128)(2,1)S(1)}, u32[]{:S(2)}, u32[]{:S(2)}) collective-permute-start(bf16[4,136,128]{2,1,0:T(8,128)(2,1)S(1)} %get-tuple-element.41), channel_id=1, source_target_pairs={{0,2},{2,0},{4,6},{6,4},{8,10},{10,8},{12,14},{14,12},{16,18},{18,... | collective-permute-start | bytes 417800 | tf_op jit(solution)/shard_map/ppermute | solution.py:323
  7.3 1.5 %collective-permute-start.2 = (bf16[4,136,128]{2,1,0:T(8,128)(2,1)S(1)}, bf16[4,136,128]{2,1,0:T(8,128)(2,1)S(1)}, u32[]{:S(2)}, u32[]{:S(2)}) collective-permute-start(bf16[4,136,128]{2,1,0:T(8,128)(2,1)S(1)} %get-tuple-element.42), channel_id=1, source_target_pairs={{0,4},{2,6},{4,0},{6,2},{8,12},{10,14},{12,8},{14,10},{16,20},{18,... | collective-permute-start | bytes 417800 | tf_op jit(solution)/shard_map/ppermute | solution.py:323
  8.8 0.0 collective-permute-start.3
  8.8 0.0 copy-start
  8.9 1.3 %own_states.1 = (bf16[16,512,128]{2,1,0:T(8,128)(2,1)S(1)}, bf16[4,136,128]{2,1,0:T(8,128)(2,1)S(1)}, bf16[2,2,64,128]{3,2,1,0:T(8,128)(2,1)S(1)}) custom-call(s32[4]{0:T(128)S(1)} %pad_add_fusion.idx_ref, bf16[2,512,128]{2,1,0:T(8,128)(2,1)S(1)} %get-tuple-element.34.k_ref, ...), custom_call_target="tpu_custom_call", output_to_operand_aliasing={{0}: (5, {})} | custom-call | flops 1000000000 | bytes 2000000 | tf_op jit(solution)/shard_map/own_states/pallas_call | solution.py:353
  10.2 0.0 copy-start.1
  10.2 0.0 copy-start.2
  10.2 4.2 %collective-permute-start = (bf16[2,2,64,128]{3,2,1,0:T(8,128)(2,1)S(1)}, bf16[2,2,64,128]{3,2,1,0:T(8,128)(2,1)S(1)}, u32[]{:S(2)}, u32[]{:S(2)}) collective-permute-start(bf16[2,2,64,128]{3,2,1,0:T(8,128)(2,1)S(1)} %get-tuple-element.39), channel_id=1, source_target_pairs={{0,2},{2,4},{4,6},{6,8},{8,10},{10,12},{12,14},{14,16},{16,18},{18... | collective-permute-start | bytes 196616 | tf_op jit(solution)/shard_map/ppermute | solution.py:326
  14.4 0.0 collective-permute-done.1.b.refs_1_
  14.4 1.1 %collective-permute-done.2.c.refs_2_ = bf16[4,136,128]{2,1,0:T(8,128)(2,1)S(1)} collective-permute-done((bf16[4,136,128]{2,1,0:T(8,128)(2,1)S(1)}, bf16[4,136,128]{2,1,0:T(8,128)(2,1)S(1)}, u32[]{:S(2)}, u32[]{:S(2)}) %collective-permute-start.2) | collective-permute-done | bytes 139296 | tf_op jit(solution)/shard_map/ppermute | solution.py:323
  15.4 0.0 collective-permute-done.3.d.refs_3_
  15.4 0.1 totals.1._.a
  15.5 1.6 %collective-permute-start.4 = (bf16[4,136,128]{2,1,0:T(8,128)(2,1)S(1)}, bf16[4,136,128]{2,1,0:T(8,128)(2,1)S(1)}, u32[]{:S(2)}, u32[]{:S(2)}) collective-permute-start(bf16[4,136,128]{2,1,0:T(8,128)(2,1)S(1)} %totals.1._.a), channel_id=1, source_target_pairs={{0,8},{2,10},{4,12},{6,14},{8,0},{10,2},{12,4},{14,6},{16,24},{18,... | collective-permute-start | bytes 417800 | tf_op jit(solution)/shard_map/ppermute | solution.py:323
  17.2 0.0 collective-permute-done.halo_ref
  17.2 0.0 copy-done
  17.2 0.4 prepare.1
  17.5 0.0 copy-done.1
  17.6 0.0 copy-done.2
  17.6 2.9 %near_0.1 = (f32[4,128,512]{2,1,0:T(8,128)S(1)}, f32[4,1,512]{2,1,0:T(1,128)S(1)}, bf16[4,128,512]{2,1,0:T(8,128)(2,1)S(1)}) custom-call(s32[4]{0:T(128)S(1)} %pad_add_fusion.idx_ref, f32[16]{0:T(128)S(1)} %copy-done.2, f32[2,4096,128]{2,1,0:T(8,128)S(1)} %get-tuple-element.44.q_wide, bf16[2,576,128]{2,1,0:T(8,128)(2,1)S(1)} %get-tuple-element.45.kx_ref, ...), custom_call_target="tpu_custom_call" | custom-call | flops 1600000000 | bytes 4000000 | tf_op jit(solution)/shard_map/near_0/pallas_call | solution.py:392
  20.5 0.2 collective-permute-done.4.b.refs_4_
  20.7 4.1 %collective-permute-start.5 = (bf16[4,136,128]{2,1,0:T(8,128)(2,1)S(1)}, bf16[4,136,128]{2,1,0:T(8,128)(2,1)S(1)}, u32[]{:S(2)}, u32[]{:S(2)}) collective-permute-start(bf16[4,136,128]{2,1,0:T(8,128)(2,1)S(1)} %layer_sum.1.refs_0_), channel_id=1, source_target_pairs={{0,16},{2,18},{4,20},{6,22},{8,24},{10,26},{12,28},{14,30},{16,0},... | collective-permute-start | bytes 417800 | tf_op jit(solution)/shard_map/ppermute | solution.py:323
  24.7 5.3 %near_4.1 = (f32[8,128,512]{2,1,0:T(8,128)S(1)}, f32[8,1,512]{2,1,0:T(1,128)S(1)}, bf16[8,128,512]{2,1,0:T(8,128)(2,1)S(1)}) custom-call(s32[4]{0:T(128)S(1)} %pad_add_fusion.idx_ref, f32[16]{0:T(128)S(1)} %copy-done.2, f32[2,4096,128]{2,1,0:T(8,128)S(1)} %get-tuple-element.44.q_wide, bf16[2,576,128]{2,1,0:T(8,128)(2,1)S(1)} %get-tuple-element.45.kx_ref, ...), custom_call_target="tpu_custom_call" | custom-call | flops 3200000000 | bytes 8000000 | tf_op jit(solution)/shard_map/near_4/pallas_call | solution.py:392
  30.0 0.0 collective-permute-done.5.refs_5_
  30.1 0.9 %prefixes.1 = (bf16[4,136,128]{2,1,0:T(8,128)(2,1)S(1)}, bf16[4,136,128]{2,1,0:T(8,128)(2,1)S(1)}, bf16[4,136,128]{2,1,0:T(8,128)(2,1)S(1)}, bf16[4,136,128]{2,1,0:T(8,128)(2,1)S(1)}) custom-call(s32[4]{0:T(128)S(1)} %pad_add_fusion.idx_ref, bf16[4,136,128]{2,1,0:T(8,128)(2,1)S(1)} %get-tuple-element.40.a.refs_0_, ...), custom_call_target="tpu_custom_call" | custom-call | tf_op jit(solution)/shard_map/prefixes/pallas_call | solution.py:424
  31.0 0.1 collective-permute-start.7
  31.0 1.2 %collective-permute-start.8 = (bf16[4,136,128]{2,1,0:T(8,128)(2,1)S(1)}, bf16[4,136,128]{2,1,0:T(8,128)(2,1)S(1)}, u32[]{:S(2)}, u32[]{:S(2)}) collective-permute-start(bf16[4,136,128]{2,1,0:T(8,128)(2,1)S(1)} %get-tuple-element.60), channel_id=1, source_target_pairs={{0,4},{2,6},{4,0},{6,2},{8,12},{10,14},{12,8},{14,10},{16,20},{18,... | collective-permute-start | bytes 417800 | tf_op jit(solution)/shard_map/ppermute | solution.py:323
  32.3 2.3 %collective-permute-start.9 = (bf16[4,136,128]{2,1,0:T(8,128)(2,1)S(1)}, bf16[4,136,128]{2,1,0:T(8,128)(2,1)S(1)}, u32[]{:S(2)}, u32[]{:S(2)}) collective-permute-start(bf16[4,136,128]{2,1,0:T(8,128)(2,1)S(1)} %get-tuple-element.61), channel_id=1, source_target_pairs={{0,6},{2,4},{4,2},{6,0},{8,14},{10,12},{12,10},{14,8},{16,22},{18,... | collective-permute-start | bytes 417800 | tf_op jit(solution)/shard_map/ppermute | solution.py:323
  34.5 1.0 %final_own.1 = (bf16[4,256,128]{2,1,0:T(8,128)(2,1)S(1)}, bf16[4,256,128]{2,1,0:T(8,128)(2,1)S(1)}) custom-call(s32[4]{0:T(128)S(1)} %pad_add_fusion.idx_ref, f32[16]{0:T(128)S(1)} %copy-done.2, f32[4,128,512]{2,1,0:T(8,128)S(1)} %get-tuple-element.48.num.refs_0_, f32[4,1,512]{2,1,0:T(1,128)S(1)} %get-tuple-element.49._.den.refs_1_, ...), custom_call_target="tpu_custom_call" | custom-call | flops 500000000 | bytes 2000000 | tf_op jit(solution)/shard_map/final_own/pallas_call | solution.py:441
  35.5 2.9 %near_12.1 = (f32[4,128,512]{2,1,0:T(8,128)S(1)}, f32[4,1,512]{2,1,0:T(1,128)S(1)}, bf16[4,128,512]{2,1,0:T(8,128)(2,1)S(1)}) custom-call(s32[4]{0:T(128)S(1)} %pad_add_fusion.idx_ref, f32[16]{0:T(128)S(1)} %copy-done.2, f32[2,4096,128]{2,1,0:T(8,128)S(1)} %get-tuple-element.44.q_wide, bf16[2,576,128]{2,1,0:T(8,128)(2,1)S(1)} %get-tuple-element.45.kx_ref, ...), custom_call_target="tpu_custom_call" | custom-call | flops 1600000000 | bytes 4000000 | tf_op jit(solution)/shard_map/near_12/pallas_call | solution.py:392
  38.4 0.0 collective-permute-done.7.refs_9_
  38.4 0.0 collective-permute-done.8.refs_10_
  38.4 0.0 collective-permute-done.9.refs_11_
  38.4 1.1 %final_sent.1.refs_13_ = bf16[12,256,128]{2,1,0:T(8,128)(2,1)S(1)} custom-call(s32[4]{0:T(128)S(1)} %pad_add_fusion.idx_ref, f32[16]{0:T(128)S(1)} %copy-done.2, f32[4,128,512]{2,1,0:T(8,128)S(1)} %get-tuple-element.48.num.refs_0_, f32[4,1,512]{2,1,0:T(1,128)S(1)} %get-tuple-element.49._.den.refs_1_, bf16[4,128,512]{2,1,0:T(8,128)(2,1)S(1)} %get-tuple-element.50.qf.refs_2_, ...), custom_call_target="tpu_custom_call" | custom-call | tf_op jit(solution)/shard_map/final_sent/pallas_call | solution.py:451
  39.5 0.1 collective-permute-start.10
  39.6 0.5 %collective-permute-start.6 = (bf16[4,256,128]{2,1,0:T(8,128)(2,1)S(1)}, bf16[4,256,128]{2,1,0:T(8,128)(2,1)S(1)}, u32[]{:S(2)}, u32[]{:S(2)}) collective-permute-start(bf16[4,256,128]{2,1,0:T(8,128)(2,1)S(1)} %get-tuple-element.53.refs_12_), channel_id=1, source_target_pairs={{0,1},{1,0},{2,3},{3,2},{4,5},{5,4},{6,7},{7,6},{8,9},{9,8},{10,11... | collective-permute-start | bytes 786440 | tf_op jit(solution)/shard_map/ppermute | solution.py:439
  40.1 1.8 %final_kept.1._ = bf16[32,256,128]{2,1,0:T(8,128)(2,1)} custom-call(s32[4]{0:T(128)S(1)} %pad_add_fusion.idx_ref, f32[16]{0:T(128)S(1)} %copy-done.2, f32[4,128,512]{2,1,0:T(8,128)S(1)} %get-tuple-element.48.num.refs_0_, f32[4,1,512]{2,1,0:T(1,128)S(1)} %get-tuple-element.49._.den.refs_1_, bf16[4,128,512]{2,1,0:T(8,128)(2,1)S(1)} %get-tuple-element.50.qf.refs_2_, ...), custom_call_target="tpu_custom_call" | custom-call | flops 1000000000 | bytes 5000000 | tf_op jit(solution)/shard_map/final_kept/pallas_call | solution.py:460
  41.9 0.3 collective-permute-done.6.own_ref
  42.3 0.0 collective-permute-done.10.got_ref
  42.3 1.5 %place.1 = bf16[32,256,128]{2,1,0:T(8,128)(2,1)} custom-call(s32[4]{0:T(128)S(1)} %pad_add_fusion.idx_ref, bf16[4,256,128]{2,1,0:T(8,128)(2,1)S(1)} %collective-permute-done.6.own_ref, bf16[12,256,128]{2,1,0:T(8,128)(2,1)S(1)} %collective-permute-done.10.got_ref, bf16[32,256,128]{2,1,0:T(8,128)(2,1)} %final_kept.1._), custom_call_target="tpu_custom_call", output_to_operand_aliasing={{}: (3, {})} | custom-call | tf_op jit(solution)/shard_map/place/pallas_call | solution.py:470
  (1 shorter events, 0.0 us)
Async XLA Ops:
  4.3 10.1 %collective-permute-start.1 = (bf16[4,136,128]{2,1,0:T(8,128)(2,1)S(1)}, bf16[4,136,128]{2,1,0:T(8,128)(2,1)S(1)}, u32[]{:S(2)}, u32[]{:S(2)}) collective-permute-start(bf16[4,136,128]{2,1,0:T(8,128)(2,1)S(1)} %get-tuple-element.41), channel_id=1, source_target_pairs={{0,2},{2,0},{4,6},{6,4},{8,10},{10,8},{12,14},{14,12},{16,18},{18,... | collective-permute-start | bytes 417800 | tf_op jit(solution)/shard_map/ppermute | solution.py:323
  7.3 8.1 %collective-permute-start.2 = (bf16[4,136,128]{2,1,0:T(8,128)(2,1)S(1)}, bf16[4,136,128]{2,1,0:T(8,128)(2,1)S(1)}, u32[]{:S(2)}, u32[]{:S(2)}) collective-permute-start(bf16[4,136,128]{2,1,0:T(8,128)(2,1)S(1)} %get-tuple-element.42), channel_id=1, source_target_pairs={{0,4},{2,6},{4,0},{6,2},{8,12},{10,14},{12,8},{14,10},{16,20},{18,... | collective-permute-start | bytes 417800 | tf_op jit(solution)/shard_map/ppermute | solution.py:323
  8.8 6.6 %collective-permute-start.3 = (bf16[4,136,128]{2,1,0:T(8,128)(2,1)S(1)}, bf16[4,136,128]{2,1,0:T(8,128)(2,1)S(1)}, u32[]{:S(2)}, u32[]{:S(2)}) collective-permute-start(bf16[4,136,128]{2,1,0:T(8,128)(2,1)S(1)} %get-tuple-element.43), channel_id=1, source_target_pairs={{0,6},{2,4},{4,2},{6,0},{8,14},{10,12},{12,10},{14,8},{16,22},{18,... | collective-permute-start | bytes 417800 | tf_op jit(solution)/shard_map/ppermute | solution.py:323
  8.8 8.3 %copy-start = (bf16[512,16,128]{2,1,0:T(8,128)(2,1)S(1)}, bf16[512,16,128]{2,1,0:T(8,128)(2,1)}, u32[]{:S(2)}) copy-start(bf16[512,16,128]{2,1,0:T(8,128)(2,1)} %q_ref.1) | copy-start | bytes 6291460
  10.2 7.4 %copy-start.1 = (bf16[16,128,64]{1,2,0:T(8,128)(2,1)S(1)}, bf16[16,128,64]{1,2,0:T(8,128)(2,1)}, u32[]{:S(2)}) copy-start(bf16[16,128,64]{1,2,0:T(8,128)(2,1)} %param.9) | copy-start | bytes 786436
  10.2 7.4 %copy-start.2 = (f32[16]{0:T(128)S(1)}, f32[16]{0:T(128)}, u32[]{:S(2)}) copy-start(f32[16]{0:T(128)} %share_ref.11) | copy-start | bytes 196
  10.2 7.0 %collective-permute-start = (bf16[2,2,64,128]{3,2,1,0:T(8,128)(2,1)S(1)}, bf16[2,2,64,128]{3,2,1,0:T(8,128)(2,1)S(1)}, u32[]{:S(2)}, u32[]{:S(2)}) collective-permute-start(bf16[2,2,64,128]{3,2,1,0:T(8,128)(2,1)S(1)} %get-tuple-element.39), channel_id=1, source_target_pairs={{0,2},{2,4},{4,6},{6,8},{8,10},{10,12},{12,14},{14,16},{16,18},{18... | collective-permute-start | bytes 196616 | tf_op jit(solution)/shard_map/ppermute | solution.py:326
  15.5 5.1 %collective-permute-start.4 = (bf16[4,136,128]{2,1,0:T(8,128)(2,1)S(1)}, bf16[4,136,128]{2,1,0:T(8,128)(2,1)S(1)}, u32[]{:S(2)}, u32[]{:S(2)}) collective-permute-start(bf16[4,136,128]{2,1,0:T(8,128)(2,1)S(1)} %totals.1._.a), channel_id=1, source_target_pairs={{0,8},{2,10},{4,12},{6,14},{8,0},{10,2},{12,4},{14,6},{16,24},{18,... | collective-permute-start | bytes 417800 | tf_op jit(solution)/shard_map/ppermute | solution.py:323
  20.7 9.4 %collective-permute-start.5 = (bf16[4,136,128]{2,1,0:T(8,128)(2,1)S(1)}, bf16[4,136,128]{2,1,0:T(8,128)(2,1)S(1)}, u32[]{:S(2)}, u32[]{:S(2)}) collective-permute-start(bf16[4,136,128]{2,1,0:T(8,128)(2,1)S(1)} %layer_sum.1.refs_0_), channel_id=1, source_target_pairs={{0,16},{2,18},{4,20},{6,22},{8,24},{10,26},{12,28},{14,30},{16,0},... | collective-permute-start | bytes 417800 | tf_op jit(solution)/shard_map/ppermute | solution.py:323
  31.0 7.4 %collective-permute-start.7 = (bf16[4,136,128]{2,1,0:T(8,128)(2,1)S(1)}, bf16[4,136,128]{2,1,0:T(8,128)(2,1)S(1)}, u32[]{:S(2)}, u32[]{:S(2)}) collective-permute-start(bf16[4,136,128]{2,1,0:T(8,128)(2,1)S(1)} %get-tuple-element.59), channel_id=1, source_target_pairs={{0,2},{2,0},{4,6},{6,4},{8,10},{10,8},{12,14},{14,12},{16,18},{18,... | collective-permute-start | bytes 417800 | tf_op jit(solution)/shard_map/ppermute | solution.py:323
  31.0 7.4 %collective-permute-start.8 = (bf16[4,136,128]{2,1,0:T(8,128)(2,1)S(1)}, bf16[4,136,128]{2,1,0:T(8,128)(2,1)S(1)}, u32[]{:S(2)}, u32[]{:S(2)}) collective-permute-start(bf16[4,136,128]{2,1,0:T(8,128)(2,1)S(1)} %get-tuple-element.60), channel_id=1, source_target_pairs={{0,4},{2,6},{4,0},{6,2},{8,12},{10,14},{12,8},{14,10},{16,20},{18,... | collective-permute-start | bytes 417800 | tf_op jit(solution)/shard_map/ppermute | solution.py:323
  32.3 6.2 %collective-permute-start.9 = (bf16[4,136,128]{2,1,0:T(8,128)(2,1)S(1)}, bf16[4,136,128]{2,1,0:T(8,128)(2,1)S(1)}, u32[]{:S(2)}, u32[]{:S(2)}) collective-permute-start(bf16[4,136,128]{2,1,0:T(8,128)(2,1)S(1)} %get-tuple-element.61), channel_id=1, source_target_pairs={{0,6},{2,4},{4,2},{6,0},{8,14},{10,12},{12,10},{14,8},{16,22},{18,... | collective-permute-start | bytes 417800 | tf_op jit(solution)/shard_map/ppermute | solution.py:323
  39.5 2.7 %collective-permute-start.10 = (bf16[12,256,128]{2,1,0:T(8,128)(2,1)S(1)}, bf16[12,256,128]{2,1,0:T(8,128)(2,1)S(1)}, u32[]{:S(2)}, u32[]{:S(2)}) collective-permute-start(bf16[12,256,128]{2,1,0:T(8,128)(2,1)S(1)} %final_sent.1.refs_13_), channel_id=1, source_target_pairs={{0,1},{1,0},{2,3},{3,2},{4,5},{5,4},{6,7},{7,6},{8,9},{9,8},{10,11... | collective-permute-start | bytes 2359304 | tf_op jit(solution)/shard_map/ppermute | solution.py:439
  39.6 2.6 %collective-permute-start.6 = (bf16[4,256,128]{2,1,0:T(8,128)(2,1)S(1)}, bf16[4,256,128]{2,1,0:T(8,128)(2,1)S(1)}, u32[]{:S(2)}, u32[]{:S(2)}) collective-permute-start(bf16[4,256,128]{2,1,0:T(8,128)(2,1)S(1)} %get-tuple-element.53.refs_12_), channel_id=1, source_target_pairs={{0,1},{1,0},{2,3},{3,2},{4,5},{5,4},{6,7},{7,6},{8,9},{9,8},{10,11... | collective-permute-start | bytes 786440 | tf_op jit(solution)/shard_map/ppermute | solution.py:439
